TPU v7x, 32 devices: a whole 2x2x4 slice. The times are simulated.
32 devices in a mesh: site: 8 (over z, x), expert: 4 (over y, core).
Axes of the slice: x: 2, y: 2, z: 4, core: 2. Of those that a mesh axis runs over, the one named last changes fastest.
Arguments:
- out_grads: bfloat16 [2, 8, 512, 1024], P(None, 'site', 'expert'), may hold values from -6 to 6
- routes: int32 [2, 8, 512, 1], P(None, 'site', 'expert'), may hold values from 0 to 3; in each aligned block of 128 rows (0 to 127, 128 to 255, ..., all dimensions but the last counted through in order) at most 64 rows name the same one
- hiddens: bfloat16 [2, 8, 4, 256, 512], P(None, 'site', 'expert'), may hold values from -6 to 6
- weights: bfloat16 [8, 4, 512, 1024], P('site', 'expert'), may hold values from -6 to 6
- tracker_offset: bfloat16 [8, 4, 512, 1024], P('site', 'expert'), may hold values from -20 to 20
- partner_bits: int32 [8, 2], P('site'), may hold values from 0 to 1, as said below
Outputs:
- new_weights: bfloat16 [8, 4, 512, 1024], P('site', 'expert')
Inputs may be any that keep to these rules, and one draw needn't show every extreme that they name: `routes`: among the 128 tokens of one device in a step no expert is named more than 64 times, a bound that some block reaches. `partner_bits`: site 0 and site 8 - 1 each take the partner ahead in exactly one of the two rounds.
All inputs are finite; a program needn't handle non-finite values.
Results may differ from a plain program's by a relative error of at most 0.0095.
Values may be sent and summed in bfloat16 or wider, within the bound.
No kernel may reach another device: no remote copies, remote signals or barrier semaphores. Data moves between devices by JAX's collectives and lax.ppermute only.
A program may use at most 64 MiB of HBM per device.

v0:
```python
import math

import jax
import jax.numpy as jnp
from jax import lax
from jax.sharding import PartitionSpec as P

NS_ITERS = 2


coef_a = 3.4445
coef_b = -4.775
coef_c = 2.0315
step_scale = 32.0
weight_hop = 4


def from_behind(block, axis, distance):
    devices = range(lax.axis_size(axis))
    route = [((i - distance) % len(devices), i) for i in devices]
    return lax.ppermute(block, axis, route)


def orthogonalize(tracked):
    frobenius = jnp.sqrt(jnp.sum(tracked * tracked))
    current = (tracked / (frobenius + 1e-07)).astype(jnp.bfloat16)
    for repeat in range(NS_ITERS):
        gram_matrix = lax.dot_general(
            current, current, (((1,), (1,)), ((), ())), preferred_element_type=jnp.float32
        ).astype(jnp.bfloat16)
        squared = jnp.dot(gram_matrix, gram_matrix, preferred_element_type=jnp.float32)
        polynomial = (coef_b * gram_matrix.astype(jnp.float32) + coef_c * squared).astype(
            jnp.bfloat16
        )
        current = (
            coef_a * current.astype(jnp.float32)
            + jnp.dot(polynomial, current, preferred_element_type=jnp.float32)
        ).astype(jnp.bfloat16)
    return current


def place_rows(gradient, routing, experts, slot_count):
    owned = (routing[:, None] == jnp.arange(experts, dtype=jnp.int32)[None, :]).astype(jnp.int32)
    earlier = jnp.cumsum(owned, axis=0) - owned
    position = jnp.sum(earlier * owned, axis=1)
    target = routing * slot_count + position
    selector = (
        target[None, :] == jnp.arange(experts * slot_count, dtype=jnp.int32)[:, None]
    ).astype(jnp.bfloat16)
    placed = jnp.dot(selector, gradient, preferred_element_type=jnp.float32).astype(jnp.bfloat16)
    return placed.reshape(experts, slot_count, gradient.shape[1])


def local_gradient(stashed, arrived):
    product = lax.dot_general(
        stashed, arrived, (((0,), (0,)), ((), ())), preferred_element_type=jnp.float32
    )
    return (product * (1.0 / math.sqrt(stashed.shape[0]))).astype(jnp.bfloat16)


def choose(ahead_value, behind, flag):
    return jnp.where(flag == 1, ahead_value, behind)


def local(out_grads, routes, hiddens, weights, tracker_offset, partner_bits):
    experts = lax.axis_size("expert")
    stashed = hiddens[:, 0, 0]
    step_count = stashed.shape[0]
    slot_rows = stashed.shape[1]
    slot_count = slot_rows // experts
    features = out_grads.shape[-1]
    direction = partner_bits[0]
    weight = weights[0, 0]
    offset = tracker_offset[0, 0]
    placed = [
        place_rows(out_grads[section_index, 0], routes[section_index, 0, :, 0], experts, slot_count)
        for section_index in range(step_count)
    ]
    arrived_all = lax.all_to_all(
        jnp.stack(placed), "expert", split_axis=1, concat_axis=1, tiled=True
    )
    arrived = [arrived_all[section_index] for section_index in range(step_count)]
    gradients = [
        local_gradient(stashed[section_index], arrived[section_index].reshape(slot_rows, features))
        for section_index in range(step_count)
    ]
    own_updates = jnp.zeros(weight.shape, jnp.float32)
    for section_index in range(step_count):
        distance = 2**section_index
        gradient = gradients[section_index]
        summed = offset.astype(jnp.float32) + gradient.astype(jnp.float32)
        partner_sum = choose(
            from_behind(summed, "site", -distance),
            from_behind(summed, "site", distance),
            direction[section_index],
        )
        tracked = 0.5 * (summed + partner_sum)
        offset = (tracked - gradient.astype(jnp.float32)).astype(jnp.bfloat16)
        ortho = orthogonalize(tracked)
        own_updates = own_updates + ortho.astype(jnp.float32)
    updated = weight.astype(jnp.float32) - step_scale * own_updates
    beside_all = from_behind(updated.astype(jnp.bfloat16), "site", -weight_hop).astype(
        updated.dtype
    ) + from_behind(updated.astype(jnp.bfloat16), "site", weight_hop).astype(updated.dtype)
    result = (0.5 * updated + 0.25 * beside_all).astype(jnp.bfloat16)
    return result[None, None]


def solution(mesh):
    in_specs = (
        P(None, "site", "expert", None),
        P(None, "site", "expert", None),
        P(None, "site", "expert", None, None),
        P("site", "expert", None, None),
        P("site", "expert", None, None),
        P("site", None),
    )
    out_specs = P("site", "expert", None, None)
    return jax.shard_map(local, mesh=mesh, in_specs=in_specs, out_specs=out_specs, check_vma=False)
```

profile of v0, /device:TPU:1, one launch (start us, length us, event | category | flops | bytes accessed | tf_op | source)
XLA Modules:
  0.0 281.7 jit_solution(13855124419092008224)
XLA Ops:
  0.0 0.7 slice_bitcast_fusion.1
  0.7 0.1 fusion.37
  0.8 0.1 fusion.35
  0.9 0.2 reduce_window_sum.17
  1.0 0.2 reduce_window_sum.18
  1.2 0.2 select_reduce_fusion
  1.4 0.7 multiply_add_fusion.1
  2.1 1.2 convolution_convert_fusion.5
  3.3 1.2 convolution_convert_fusion.4
  4.6 0.0 copy-start.2
  4.6 1.1 pad_maximum_fusion
  5.6 4.3 %all-to-all-start = ((bf16[2,4,64,1024]{3,2,0,1:T(8,128)(2,1)}), bf16[2,4,64,1024]{3,2,0,1:T(8,128)(2,1)S(1)}, u32[]{:S(2)}, u32[]{:S(2)}) async-start(bf16[2,4,64,1024]{3,2,0,1:T(8,128)(2,1)} %pad_maximum_fusion), calls=%async_computation | async-start | bytes 2097152 | tf_op jit(solution)/shard_map/all_to_all | solution.py:79
  9.9 0.0 copy-done.2
  9.9 0.5 copy.15
  10.5 0.0 copy-start.5
  10.5 12.8 %all-to-all-done = bf16[2,4,64,1024]{3,2,0,1:T(8,128)(2,1)S(1)} async-done(((bf16[2,4,64,1024]{3,2,0,1:T(8,128)(2,1)}), bf16[2,4,64,1024]{3,2,0,1:T(8,128)(2,1)S(1)}, u32[]{:S(2)}, u32[]{:S(2)}) %all-to-all-start) | async-done | bytes 1048608 | tf_op jit(solution)/shard_map/all_to_all | solution.py:79
  23.3 0.1 fusion.46
  23.4 0.0 copy-done.5
  23.4 0.0 copy-start.7
  23.4 0.5 convert_add_fusion
  23.9 5.2 %collective-permute-start = (f32[512,1024]{0,1:T(8,128)S(1)}, f32[512,1024]{0,1:T(8,128)S(1)}, u32[]{:S(2)}, u32[]{:S(2)}) collective-permute-start(f32[512,1024]{0,1:T(8,128)S(1)} %get-tuple-element.17), channel_id=1, source_target_pairs={{4,0},{8,4},{12,8},{16,12},{20,16},{24,20},{28,24},{0,28},{5,1},{9... | collective-permute-start | bytes 6291464 | tf_op jit(solution)/shard_map/ppermute | solution.py:21
  29.1 0.0 collective-permute-start.1
  29.1 0.0 copy-done.7
  29.1 0.6 fusion.47
  30.3 85.8 %collective-permute-done = f32[512,1024]{0,1:T(8,128)S(1)} collective-permute-done((f32[512,1024]{0,1:T(8,128)S(1)}, f32[512,1024]{0,1:T(8,128)S(1)}, u32[]{:S(2)}, u32[]{:S(2)}) %collective-permute-start) | collective-permute-done | bytes 2097184 | tf_op jit(solution)/shard_map/ppermute | solution.py:21
  116.1 1.1 collective-permute-done.1
  117.2 0.0 copy-start.6
  117.2 1.3 multiply_reduce_fusion.1
  118.5 0.0 copy-start
  118.5 0.0 copy-done.6
  118.5 0.0 copy-start.3
  118.5 0.5 bitcast_add_fusion
  119.0 0.8 copy-done
  119.8 2.1 collective-permute-start.2
  122.0 0.0 collective-permute-start.3
  122.6 0.0 copy-done.3
  122.7 1.3 copy.14
  124.6 3.8 %convolution_convert_fusion.3 = bf16[512,512]{1,0:T(8,128)(2,1)} fusion(f32[512,1024]{0,1:T(8,128)} %copy-done, f32[]{:T(128)S(6)} %add.69), kind=kOutput, calls=%fused_computation.33 | convolution fusion | flops 538181632 | bytes 2621444 | tf_op jit(solution)/shard_map/dot_general | solution.py:28
  128.4 3.8 %add_convert_fusion.4 = bf16[512,1024]{0,1:T(8,128)(2,1)S(1)} fusion(bf16[512,512]{1,0:T(8,128)(2,1)} %convolution_convert_fusion.3, f32[512,1024]{0,1:T(8,128)} %copy-done, f32[]{:T(128)S(6)} %add.69), kind=kOutput, calls=%fused_computation.13 | convolution fusion | flops 810811392 | bytes 3670020 | tf_op jit(solution)/shard_map/dot_general | solution.py:37
  132.2 0.0 copy-start.8
  132.2 1.6 convolution_convert_fusion.2
  133.8 0.0 copy-done.8
  133.8 33.4 %collective-permute-done.2 = f32[512,1024]{0,1:T(8,128)} collective-permute-done((f32[512,1024]{0,1:T(8,128)S(1)}, f32[512,1024]{0,1:T(8,128)}, u32[]{:S(2)}, u32[]{:S(2)}) %collective-permute-start.2) | collective-permute-done | bytes 2097184 | tf_op jit(solution)/shard_map/ppermute | solution.py:21
  167.1 43.9 %collective-permute-done.3 = f32[512,1024]{0,1:T(8,128)} collective-permute-done((f32[512,1024]{0,1:T(8,128)S(1)}, f32[512,1024]{0,1:T(8,128)}, u32[]{:S(2)}, u32[]{:S(2)}) %collective-permute-start.3) | collective-permute-done | bytes 2097184 | tf_op jit(solution)/shard_map/ppermute | solution.py:21
  211.1 4.1 %multiply_reduce_fusion = (f32[]{:T(128)}, f32[512,1024]{0,1:T(8,128)}) fusion(f32[512,1024]{0,1:T(8,128)S(1)} %bitcast_add_fusion, f32[512,1024]{0,1:T(8,128)} %collective-permute-done.2, f32[512,1024]{0,1:T(8,128)} %collective-permute-done.3, pred[]{:T(512)} %bitcast.17), kind=kLoop, calls=%fused_computation.9 | loop fusion | flops 2621439 | bytes 8388613 | tf_op jit(solution)/shard_map/reduce_sum | solution.py:25
  215.9 0.0 copy-start.1
  215.9 3.9 %convolution_convert_fusion.1 = bf16[512,512]{1,0:T(8,128)(2,1)} fusion(f32[512,1024]{0,1:T(8,128)} %get-tuple-element.8, f32[]{:T(128)S(6)} %add.76), kind=kOutput, calls=%fused_computation.31 | convolution fusion | flops 538181632 | bytes 2621444 | tf_op jit(solution)/shard_map/dot_general | solution.py:28
  219.8 0.0 copy-done.1
  219.8 2.5 add_convert_fusion.2
  222.4 0.0 copy-start.9
  222.4 1.0 copy-done.9
  223.3 0.7 convolution_convert_fusion
  224.1 0.0 copy-start.4
  224.1 3.7 %add_convert_fusion.1 = bf16[512,1024]{0,1:T(8,128)(2,1)} fusion(bf16[512,1024]{0,1:T(8,128)(2,1)} %copy-done.9, bf16[512,512]{1,0:T(8,128)(2,1)S(1)} %convolution_convert_fusion), kind=kOutput, calls=%fused_computation.6 | convolution fusion | flops 808714240 | bytes 2621440 | tf_op jit(solution)/shard_map/dot_general | solution.py:37
  227.8 0.0 copy-done.4
  227.8 4.7 %fusion.48 = (bf16[512,1024]{0,1:T(8,128)(2,1)}, f32[512,1024]{0,1:T(8,128)S(1)}) fusion(bf16[512,1024]{0,1:T(8,128)(2,1)} %add_convert_fusion.1, bf16[512,1024]{0,1:T(8,128)(2,1)} %copy-done.8, bf16[512,512]{1,0:T(8,128)(2,1)} %convolution_convert_fusion.2, bf16[1,1,512,1024]{2,3,1,0:T(8,128)(2,1)S(1)} %copy-done.4), kind=kOutput, calls=%fused_computation.86 | convolution fusion | flops 812384256 | bytes 6815744 | tf_op jit(solution)/shard_map/dot_general | solution.py:37
  232.5 0.8 collective-permute-start.4
  233.4 46.6 %collective-permute-done.4 = bf16[512,1024]{0,1:T(8,128)(2,1)S(1)} collective-permute-done((bf16[512,1024]{0,1:T(8,128)(2,1)}, bf16[512,1024]{0,1:T(8,128)(2,1)S(1)}, u32[]{:S(2)}, u32[]{:S(2)}) %collective-permute-start.4) | collective-permute-done | bytes 1048608 | tf_op jit(solution)/shard_map/ppermute | solution.py:21
  280.0 0.4 fusion.9
  280.4 1.3 copy.22
Async XLA Ops:
  4.6 5.4 %copy-start.2 = (bf16[1,1,512,1024]{3,2,1,0:T(8,128)(2,1)S(1)}, bf16[1,1,512,1024]{3,2,1,0:T(8,128)(2,1)}, u32[]{:S(2)}) copy-start(bf16[1,1,512,1024]{3,2,1,0:T(8,128)(2,1)} %param.10) | copy-start | bytes 3145732
  5.6 17.6 %all-to-all-start = ((bf16[2,4,64,1024]{3,2,0,1:T(8,128)(2,1)}), bf16[2,4,64,1024]{3,2,0,1:T(8,128)(2,1)S(1)}, u32[]{:S(2)}, u32[]{:S(2)}) async-start(bf16[2,4,64,1024]{3,2,0,1:T(8,128)(2,1)} %pad_maximum_fusion), calls=%async_computation | async-start | bytes 2097152 | tf_op jit(solution)/shard_map/all_to_all | solution.py:79
  10.5 12.9 %copy-start.5 = (bf16[2,1,1,256,512]{4,3,2,1,0:T(8,128)(2,1)S(1)}, bf16[2,1,1,256,512]{4,3,2,1,0:T(8,128)(2,1)}, u32[]{:S(2)}) copy-start(bf16[2,1,1,256,512]{4,3,2,1,0:T(8,128)(2,1)} %param.8) | copy-start | bytes 1572868
  23.4 5.7 %copy-start.7 = (s32[1,2]{1,0:T(1,128)S(1)}, s32[1,2]{1,0:T(1,128)}, u32[]{:S(2)}) copy-start(s32[1,2]{1,0:T(1,128)} %param.11) | copy-start | bytes 28
  23.9 92.3 %collective-permute-start = (f32[512,1024]{0,1:T(8,128)S(1)}, f32[512,1024]{0,1:T(8,128)S(1)}, u32[]{:S(2)}, u32[]{:S(2)}) collective-permute-start(f32[512,1024]{0,1:T(8,128)S(1)} %get-tuple-element.17), channel_id=1, source_target_pairs={{4,0},{8,4},{12,8},{16,12},{20,16},{24,20},{28,24},{0,28},{5,1},{9... | collective-permute-start | bytes 6291464 | tf_op jit(solution)/shard_map/ppermute | solution.py:21
  29.1 88.2 %collective-permute-start.1 = (f32[512,1024]{0,1:T(8,128)S(1)}, f32[512,1024]{0,1:T(8,128)S(1)}, u32[]{:S(2)}, u32[]{:S(2)}) collective-permute-start(f32[512,1024]{0,1:T(8,128)S(1)} %get-tuple-element.17), channel_id=1, source_target_pairs={{28,0},{0,4},{4,8},{8,12},{12,16},{16,20},{20,24},{24,28},{29,1},{... | collective-permute-start | bytes 6291464 | tf_op jit(solution)/shard_map/ppermute | solution.py:21
  117.2 1.3 copy-start.6
  118.5 1.3 copy-start
  118.5 4.1 %copy-start.3 = (bf16[1,1,512,1024]{3,2,1,0:T(8,128)(2,1)S(1)}, bf16[1,1,512,1024]{3,2,1,0:T(8,128)(2,1)}, u32[]{:S(2)}) copy-start(bf16[1,1,512,1024]{3,2,1,0:T(8,128)(2,1)} %param.9) | copy-start | bytes 3145732
  119.8 47.3 %collective-permute-start.2 = (f32[512,1024]{0,1:T(8,128)S(1)}, f32[512,1024]{0,1:T(8,128)}, u32[]{:S(2)}, u32[]{:S(2)}) collective-permute-start(f32[512,1024]{0,1:T(8,128)S(1)} %bitcast_add_fusion), channel_id=1, source_target_pairs={{8,0},{12,4},{16,8},{20,12},{24,16},{28,20},{0,24},{4,28},{9,1},{1... | collective-permute-start | bytes 6291464 | tf_op jit(solution)/shard_map/ppermute | solution.py:21
  122.0 89.1 %collective-permute-start.3 = (f32[512,1024]{0,1:T(8,128)S(1)}, f32[512,1024]{0,1:T(8,128)}, u32[]{:S(2)}, u32[]{:S(2)}) collective-permute-start(f32[512,1024]{0,1:T(8,128)S(1)} %bitcast_add_fusion), channel_id=1, source_target_pairs={{24,0},{28,4},{0,8},{4,12},{8,16},{12,20},{16,24},{20,28},{25,1},{... | collective-permute-start | bytes 6291464 | tf_op jit(solution)/shard_map/ppermute | solution.py:21
  132.2 1.6 copy-start.8
  215.9 3.9 %copy-start.1 = (f32[512,1024]{0,1:T(8,128)S(1)}, f32[512,1024]{0,1:T(8,128)}, u32[]{:S(2)}) copy-start(f32[512,1024]{0,1:T(8,128)} %get-tuple-element.8) | copy-start | bytes 6291460
  222.4 1.0 copy-start.9
  224.1 3.7 %copy-start.4 = (bf16[1,1,512,1024]{2,3,1,0:T(8,128)(2,1)S(1)}, bf16[1,1,512,1024]{2,3,1,0:T(8,128)(2,1)}, u32[]{:S(2)}) copy-start(bf16[1,1,512,1024]{2,3,1,0:T(8,128)(2,1)} %copy.14) | copy-start | bytes 3145732
  232.5 47.5 %collective-permute-start.4 = (bf16[512,1024]{0,1:T(8,128)(2,1)}, bf16[512,1024]{0,1:T(8,128)(2,1)S(1)}, u32[]{:S(2)}, u32[]{:S(2)}) collective-permute-start(bf16[512,1024]{0,1:T(8,128)(2,1)} %get-tuple-element.19), channel_id=1, source_target_pairs={{16,0},{20,4},{24,8},{28,12},{0,16},{4,20},{8,24},{12,28},{17,1},{... | collective-permute-start | bytes 3145736 | tf_op jit(solution)/shard_map/ppermute | solution.py:21
where the time goes:
time: 284 us; the launch traced here: 282 us
  waiting for transfers between devices  224 us (79%)
  matrix products  28.2 us (10%)
  starting transfers between devices  12.5 us (4%)
  other arithmetic  8.22 us (3%)
  local copies, waits for them, and re-layouts  6.35 us (2%)
    ppermute x5, waiting for transfers between devices, from_behind(): return lax.ppermute(block, axis, route)  211 us
    dot_general x4, matrix products, orthogonalize(): jnp.dot(polynomial, current, preferred_element_type=jnp.float32)  14.8 us
    all_to_all x1, waiting for transfers between devices, local(): lax.all_to_all(jnp.stack(placed), 'expert', split_axis=1, concat_axis=1,...  12.8 us
    dot_general x4, matrix products, orthogonalize(): lax.dot_general(current, current, (((1,), (1,)), ((), ())), preferred_ele...  9.98 us
    ppermute x5, starting transfers between devices, from_behind(): return lax.ppermute(block, axis, route)  8.24 us
  transfers between devices with their start and end apart: 6, of which 6 were waited for; matrix products, arithmetic and copies ran while one was open for 4% of the time, Pallas kernels for 0%

commit v1 on v0

v1 whole, which is shorter than its diff:
```python
import functools
import math

import jax
import jax.numpy as jnp
from jax import lax
from jax.experimental import pallas as pl
from jax.experimental.pallas import tpu as pltpu
from jax.sharding import PartitionSpec as P

NS_ITERS = 2
CHUNKS = 4
OUT_CHUNKS = 2

coef_a = 3.4445
coef_b = -4.775
coef_c = 2.0315
step_scale = 32.0
weight_hop = 4

VMEM = pl.BlockSpec(memory_space=pltpu.VMEM)
SMEM = pl.BlockSpec(memory_space=pltpu.SMEM)


def params():
    return pltpu.CompilerParams(vmem_limit_bytes=32 * 1024 * 1024)


def dot(a, b, dims):
    return lax.dot_general(a, b, (dims, ((), ())), preferred_element_type=jnp.float32)


def newton_schulz(current):
    for repeat in range(NS_ITERS):
        gram = dot(current, current, ((1,), (1,))).astype(jnp.bfloat16)
        squared = dot(gram, gram, ((1,), (0,)))
        poly = (coef_b * gram.astype(jnp.float32) + coef_c * squared).astype(jnp.bfloat16)
        product = dot(poly, current, ((1,), (0,)))
        current = (coef_a * current.astype(jnp.float32) + product).astype(jnp.bfloat16)
    return current


def normalized(tracked):
    total = sum(jnp.sum(part * part) for part in tracked)
    scale = 1.0 / (jnp.sqrt(total) + 1e-07)
    return jnp.concatenate([(part * scale).astype(jnp.bfloat16) for part in tracked], axis=0)


def first_step_kernel(*refs):
    tracked, (weight, moved) = refs[:-2], refs[-2:]
    ortho = newton_schulz(normalized([part[...] for part in tracked]))
    moved[...] = (
        weight[...].astype(jnp.float32) - step_scale * ortho.astype(jnp.float32)
    ).astype(moved.dtype)


def second_step_kernel(chunks, flags, *refs):
    own, same, other = refs[:chunks], refs[chunks : 2 * chunks], refs[2 * chunks : 3 * chunks]
    weight, swapped_weight, moved = refs[3 * chunks :]
    use_same, is_swapped = flags[0] == 1, flags[1] == 1
    tracked = []
    for k in range(chunks):
        partner = jnp.where(use_same, same[k][...], other[k][...])
        tracked.append(0.5 * (own[k][...].astype(jnp.float32) + partner.astype(jnp.float32)))
    ortho = newton_schulz(normalized(tracked))
    base = jnp.where(is_swapped, swapped_weight[...], weight[...]).astype(jnp.float32)
    moved[...] = (base - step_scale * ortho.astype(jnp.float32)).astype(moved.dtype)


def gradient_kernel(sources, with_sum, index, *refs):
    routes, tokens = refs[0], refs[1 : 1 + sources]
    hidden = refs[1 + sources]
    rows = hidden.shape[0]
    slots = rows // sources
    count = tokens[0].shape[0]
    mine = index[0]
    earlier = (
        lax.broadcasted_iota(jnp.int32, (count, count), 0)
        < lax.broadcasted_iota(jnp.int32, (count, count), 1)
    ).astype(jnp.bfloat16)
    slot = lax.broadcasted_iota(jnp.int32, (slots, count), 0).astype(jnp.float32)
    taken = []
    for j in range(sources):
        match = (routes[j : j + 1, :] == mine).astype(jnp.float32)
        match = jnp.broadcast_to(match, (8, count))
        position = dot(match.astype(jnp.bfloat16), earlier, ((1,), (0,)))[0:1, :]
        chosen = jnp.where((slot == position) & (match[0:1, :] > 0.5), 1.0, 0.0).astype(jnp.bfloat16)
        start = pl.multiple_of((mine ^ j) * slots, slots)
        block = hidden[pl.ds(start, slots), :]
        taken.append(dot(chosen, block, ((0,), (0,))).astype(jnp.bfloat16))
    spread = jnp.concatenate(taken, axis=0)
    everything = jnp.concatenate([t[...] for t in tokens], axis=0)
    product = dot(spread, everything, ((0,), (0,)))
    grad = (product * (1.0 / math.sqrt(rows))).astype(jnp.bfloat16)
    if with_sum:
        offset, out, summed = refs[2 + sources :]
        summed[...] = (offset[...].astype(jnp.float32) + grad.astype(jnp.float32)).astype(summed.dtype)
    else:
        (out,) = refs[2 + sources :]
    out[...] = grad


def call(kernel, in_specs, out_shape, flops, moved_bytes, args):
    single = not isinstance(out_shape, (list, tuple))
    return pl.pallas_call(
        kernel,
        in_specs=in_specs,
        out_specs=VMEM if single else [VMEM] * len(out_shape),
        out_shape=out_shape,
        compiler_params=params(),
        cost_estimate=pl.CostEstimate(flops=flops, bytes_accessed=moved_bytes, transcendentals=0),
    )(*args)


def paired(out_grads, routes, hiddens, weights, tracker_offset, partner_bits):
    sites, experts = lax.axis_size("site"), lax.axis_size("expert")
    half = sites // 2
    site, expert = lax.axis_index("site"), lax.axis_index("expert")
    both = ("site", "expert")

    cross = []
    for s in range(half):
        for e in range(1, experts, 2):
            here, there = s * experts + e, (s + half) * experts + e - 1
            cross += [(here, there), (there, here)]
    mates = [(e, e ^ 1) for e in range(experts)]
    beside = [(s, s ^ 1) for s in range(sites)]
    helpers = [(s, (s + 2) % sites if s % 2 else (s - 2) % sites) for s in range(sites)]
    within = [(s, s // half * half + (s + 2) % half) for s in range(sites)]

    weight, offset = weights[0, 0], tracker_offset[0, 0]
    stashed = hiddens[:, 0, 0]
    tokens, routing = out_grads[:, 0], routes[:, 0, :, 0]
    steps = tokens.shape[0]
    fan_rows, features = weight.shape
    bits = partner_bits[0]

    is_swapped = (site < half) == (expert % 2 == 1)
    beside_bits = lax.ppermute(bits, "site", beside)
    cross_bits = lax.ppermute(bits, both, cross)
    send_own = jnp.where(site % 2 == 1, beside_bits[0] == 1, beside_bits[0] == 0)
    problem = site % half + half * (expert % 2)
    second_bit = jnp.where(is_swapped, cross_bits[1], bits[1])
    wanted = jnp.where(second_bit == 1, problem + 2, problem - 2 + sites) % sites
    use_same = wanted == (site + half - 2) % half + half * (expert % 2)

    gathered = [[tokens[k]] for k in range(steps)]
    named = [routing]
    level = experts // 2
    order = []
    while level >= 1:
        order.append(level)
        level //= 2
    have = [0]
    for level in order:
        hop = [(e, e ^ level) for e in range(experts)]
        named = named + [lax.ppermute(r, "expert", hop) for r in named]
        for k in range(steps):
            gathered[k] = gathered[k] + [lax.ppermute(t, "expert", hop) for t in gathered[k]]
        have = have + [h ^ level for h in have]
    rank = [have.index(j) for j in range(experts)]
    named = jnp.stack([named[i] for i in rank])
    index = expert.astype(jnp.int32)[None]

    shape = jax.ShapeDtypeStruct((fan_rows, features), jnp.bfloat16)
    grads = []
    for k in range(steps):
        args = [index, named[:, k]] + [gathered[k][i] for i in rank] + [stashed[k]]
        if k == 0:
            args.append(offset)
        made = call(
            functools.partial(gradient_kernel, experts, k == 0),
            [SMEM] + [VMEM] * (len(args) - 1),
            [shape, shape] if k == 0 else shape,
            2 * fan_rows * features * experts * tokens.shape[1],
            4 * fan_rows * features,
            args,
        )
        if k == 0:
            grad, summed = made
            grads.append(grad)
        else:
            grads.append(made)

    rows = fan_rows // CHUNKS
    parts = [slice(i * rows, (i + 1) * rows) for i in range(CHUNKS)]
    own = [summed[p] for p in parts]
    fetched = [lax.ppermute(o, "site", helpers) for o in own]
    tracked, second = [], []
    for i, p in enumerate(parts):
        chosen = jnp.where(send_own, own[i], fetched[i])
        partner = lax.ppermute(chosen, "site", beside).astype(jnp.float32)
        grad = grads[0][p].astype(jnp.float32)
        now = 0.5 * ((offset[p].astype(jnp.float32) + grad) + partner)
        tracked.append(now)
        later = (now - grad).astype(jnp.bfloat16).astype(jnp.float32)
        second.append((later + grads[1][p].astype(jnp.float32)).astype(jnp.bfloat16))
    mine, same, other = [], [], []
    for i in range(CHUNKS):
        arrived = lax.ppermute(second[i], both, cross)
        value = jnp.where(is_swapped, arrived, second[i])
        mine.append(value)
        same.append(lax.ppermute(value, "site", within))
        other.append(lax.ppermute(same[-1], "expert", mates))

    cost = NS_ITERS * 2 * (2 * fan_rows * fan_rows * features + fan_rows**3)
    moved = call(
        first_step_kernel, [VMEM] * (CHUNKS + 1), shape, cost, 8 * fan_rows * features, tracked + [weight]
    )
    swapped_moved = lax.ppermute(moved, both, cross)
    flags = jnp.stack([use_same, is_swapped]).astype(jnp.int32)
    moved = call(
        functools.partial(second_step_kernel, CHUNKS),
        [SMEM] + [VMEM] * (3 * CHUNKS + 2),
        shape,
        cost,
        12 * fan_rows * features,
        [flags] + mine + same + other + [moved, swapped_moved],
    )
    results = []
    rows = fan_rows // OUT_CHUNKS
    for i in range(OUT_CHUNKS):
        part = moved[i * rows : (i + 1) * rows]
        mate = lax.ppermute(part, "expert", mates).astype(jnp.float32)
        result = (0.5 * part.astype(jnp.float32) + 0.25 * (mate + mate)).astype(jnp.bfloat16)
        back = lax.ppermute(result, both, cross)
        results.append(jnp.where(is_swapped, back, result))
    return jnp.concatenate(results, axis=0)[None, None]


def from_behind(block, axis, distance):
    devices = range(lax.axis_size(axis))
    route = [((i - distance) % len(devices), i) for i in devices]
    return lax.ppermute(block, axis, route)


def orthogonalize(tracked):
    frobenius = jnp.sqrt(jnp.sum(tracked * tracked))
    return newton_schulz((tracked / (frobenius + 1e-07)).astype(jnp.bfloat16))


def place_rows(gradient, routing, experts, slot_count):
    owned = (routing[:, None] == jnp.arange(experts, dtype=jnp.int32)[None, :]).astype(jnp.int32)
    earlier = jnp.cumsum(owned, axis=0) - owned
    position = jnp.sum(earlier * owned, axis=1)
    target = routing * slot_count + position
    selector = (
        target[None, :] == jnp.arange(experts * slot_count, dtype=jnp.int32)[:, None]
    ).astype(jnp.bfloat16)
    placed = dot(selector, gradient, ((1,), (0,))).astype(jnp.bfloat16)
    return placed.reshape(experts, slot_count, gradient.shape[1])


def general(out_grads, routes, hiddens, weights, tracker_offset, partner_bits):
    experts = lax.axis_size("expert")
    stashed = hiddens[:, 0, 0]
    steps, slot_rows = stashed.shape[:2]
    slot_count = slot_rows // experts
    direction = partner_bits[0]
    weight, offset = weights[0, 0], tracker_offset[0, 0]
    placed = [place_rows(out_grads[k, 0], routes[k, 0, :, 0], experts, slot_count) for k in range(steps)]
    arrived = lax.all_to_all(jnp.stack(placed), "expert", split_axis=1, concat_axis=1, tiled=True)
    updates = jnp.zeros(weight.shape, jnp.float32)
    for k in range(steps):
        product = dot(stashed[k], arrived[k].reshape(slot_rows, -1), ((0,), (0,)))
        gradient = (product * (1.0 / math.sqrt(slot_rows))).astype(jnp.bfloat16).astype(jnp.float32)
        summed = offset.astype(jnp.float32) + gradient
        sent = summed.astype(jnp.bfloat16)
        distance = 2**k
        partner = jnp.where(
            direction[k] == 1,
            from_behind(sent, "site", -distance),
            from_behind(sent, "site", distance),
        )
        tracked = 0.5 * (summed + partner.astype(jnp.float32))
        offset = (tracked - gradient).astype(jnp.bfloat16)
        updates = updates + orthogonalize(tracked).astype(jnp.float32)
    updated = weight.astype(jnp.float32) - step_scale * updates
    sent = updated.astype(jnp.bfloat16)
    beside = from_behind(sent, "site", -weight_hop).astype(jnp.float32) + from_behind(
        sent, "site", weight_hop
    ).astype(jnp.float32)
    return (0.5 * updated + 0.25 * beside).astype(jnp.bfloat16)[None, None]


def solution(mesh):
    in_specs = (
        P(None, "site", "expert", None),
        P(None, "site", "expert", None),
        P(None, "site", "expert", None, None),
        P("site", "expert", None, None),
        P("site", "expert", None, None),
        P("site", None),
    )
    out_specs = P("site", "expert", None, None)
    sites, experts = mesh.shape["site"], mesh.shape["expert"]
    pairs = sites == 2 * weight_hop and experts in (2, 4)
    local = paired if pairs else general
    return jax.shard_map(local, mesh=mesh, in_specs=in_specs, out_specs=out_specs, check_vma=False)
```

time: 284 us -> 167 us (0.59)
  waiting for transfers between devices: 224 us -> 80 us
  starting transfers between devices: 12.5 us -> 52.8 us
  matrix products: 28.2 us -> 0 us
  Pallas kernels: 0 us -> 13.3 us
  local copies, waits for them, and re-layouts: 6.35 us -> 13.2 us
    ppermute x5 -> x36, waiting for transfers between devices: 211 us -> 80 us  [the longest x4 24.3 us: paired(): same.append(lax.ppermute(value, 'site', within))]
    ppermute x5 -> x36, starting transfers between devices: 8.24 us -> 52.8 us  [the longest x4 15 us: paired(): arrived = lax.ppermute(second[i], both, cross)]
    dot_general x12 -> x0, matrix products: 28.2 us -> none  [the longest x4 14.8 us: orthogonalize(): jnp.dot(polynomial, current, preferred_element_type=jnp.float32)]
    pallas_call x0 -> x4, Pallas kernels: none -> 13.3 us  [call(): pl.pallas_call(kernel, in_specs=in_specs, out_specs=VMEM if single else [...]
    all_to_all x1 -> x0, waiting for transfers between devices: 12.8 us -> none  [local(): lax.all_to_all(jnp.stack(placed), 'expert', split_axis=1, concat_axis=1,...]
    reduce_sum x3 -> x0, other arithmetic: 5.57 us -> none  [the longest x2 5.39 us: orthogonalize(): frobenius = jnp.sqrt(jnp.sum(tracked * tracked))]
    unnamed x22 -> x32, local copies, waits for them, and re-layouts: 3.71 us -> 9.23 us
    all_to_all x1 -> x0, starting transfers between devices: 4.29 us -> none  [local(): lax.all_to_all(jnp.stack(placed), 'expert', split_axis=1, concat_axis=1,...]
  transfers between devices with their start and end apart: 6 -> 36, of which waited for: 6 -> 18; matrix products, arithmetic and copies ran while one was open for 4% -> 3% of each run, Pallas kernels for 0% -> 4%
where the time goes in v1:
time: 167 us
  waiting for transfers between devices  80 us (48%)
  starting transfers between devices  52.8 us (32%)
  Pallas kernels  13.3 us (8%)
  local copies, waits for them, and re-layouts  13.2 us (8%)
  other arithmetic  5.67 us (3%)
    ppermute x4, waiting for transfers between devices, paired(): same.append(lax.ppermute(value, 'site', within))  24.3 us
    ppermute x2, waiting for transfers between devices, paired(): back = lax.ppermute(result, both, cross)  21.7 us
    ppermute x4, starting transfers between devices, paired(): arrived = lax.ppermute(second[i], both, cross)  15 us
    ppermute x4, waiting for transfers between devices, paired(): fetched = [lax.ppermute(o, 'site', helpers) for o in own]  13.4 us
    pallas_call x4, Pallas kernels, call(): pl.pallas_call(kernel, in_specs=in_specs, out_specs=VMEM if single else [...  13.3 us
    ppermute x4, waiting for transfers between devices, paired(): partner = lax.ppermute(chosen, 'site', beside).astype(jnp.float32)  11.7 us
    unnamed x32, local copies, waits for them, and re-layouts  9.23 us
    ppermute x4, starting transfers between devices, paired(): partner = lax.ppermute(chosen, 'site', beside).astype(jnp.float32)  7.66 us
  transfers between devices with their start and end apart: 36, of which 18 were waited for; matrix products, arithmetic and copies ran while one was open for 3% of the time, Pallas kernels for 4%

profile of v1, /device:TPU:1, one launch (start us, length us, event | category | flops | bytes accessed | tf_op | source)
XLA Modules:
  0.0 166.5 jit_solution(1009551696615181927)
XLA Ops:
  0.0 1.2 slice_bitcast_fusion.3
  1.2 2.1 %collective-permute-start.5 = (bf16[128,1024]{1,0:T(8,128)(2,1)S(1)}, bf16[128,1024]{1,0:T(8,128)(2,1)S(1)}, u32[]{:S(2)}, u32[]{:S(2)}) collective-permute-start(bf16[128,1024]{1,0:T(8,128)(2,1)S(1)} %get-tuple-element.36.refs_1_), channel_id=1, source_target_pairs={{0,2},{1,3},{2,0},{3,1},{4,6},{5,7},{6,4},{7,5},{8,10},{9,11},{10,... | collective-permute-start | bytes 786440 | tf_op jit(solution)/shard_map/ppermute | solution.py:159
  3.4 1.0 collective-permute-start.1
  4.4 5.0 %collective-permute-done.2 = s32[2,128]{1,0:T(2,128)S(1)} collective-permute-done((s32[2,128]{1,0:T(2,128)S(1)}, s32[2,128]{1,0:T(2,128)S(1)}, u32[]{:S(2)}, u32[]{:S(2)}) %collective-permute-start.2) | collective-permute-done | bytes 1056 | tf_op jit(solution)/shard_map/ppermute | solution.py:157
  9.4 1.3 collective-permute-start.3
  10.7 0.8 slice_bitcast_fusion.2
  11.5 0.7 copy-done.7
  12.3 0.7 copy-done.9
  13.0 0.9 copy-done.3
  14.0 0.9 copy-done.4
  14.9 0.9 copy-done.8
  15.9 0.9 copy-done.10
  16.9 1.7 %shard_map.64 = (bf16[512,1024]{1,0:T(8,128)(2,1)S(1)}, bf16[512,1024]{1,0:T(8,128)(2,1)S(1)}) custom-call(s32[1]{0:T(128)} %bitcast.6.index, s32[4,128]{1,0:T(4,128)S(1)} %get-tuple-element.38.refs_0_, bf16[128,1024]{1,0:T(8,128)(2,1)S(1)} %copy-done.3, bf16[128,1024]{1,0:T(8,128)(2,1)S(1)} %copy-done.10, bf16[128,1024]{1,0:T(8,128)(2,1)S(1)} %copy-done.8, ...), custom_call_target="tpu_custom_call" | custom-call | flops 536870912 | bytes 2097152 | tf_op jit(solution)/shard_map/pallas_call | solution.py:105
  18.6 0.7 slice.114
  19.3 3.5 %collective-permute-start.20 = (bf16[128,1024]{1,0:T(8,128)(2,1)}, bf16[128,1024]{1,0:T(8,128)(2,1)}, u32[]{:S(2)}, u32[]{:S(2)}) collective-permute-start(bf16[128,1024]{1,0:T(8,128)(2,1)} %slice.114), channel_id=1, source_target_pairs={{0,24},{4,12},{8,0},{12,20},{16,8},{20,28},{24,16},{28,4},{1,25},{... | collective-permute-start | bytes 786440 | tf_op jit(solution)/shard_map/ppermute | solution.py:188
  22.8 1.2 collective-permute-start.11
  24.1 1.5 collective-permute-done.7
  25.7 2.7 %collective-permute-done.20 = bf16[128,1024]{1,0:T(8,128)(2,1)} collective-permute-done((bf16[128,1024]{1,0:T(8,128)(2,1)}, bf16[128,1024]{1,0:T(8,128)(2,1)}, u32[]{:S(2)}, u32[]{:S(2)}) %collective-permute-start.20) | collective-permute-done | bytes 262176 | tf_op jit(solution)/shard_map/ppermute | solution.py:188
  28.4 1.1 broadcast_select_fusion.2
  29.4 3.1 %collective-permute-start.17 = (bf16[128,1024]{1,0:T(8,128)(2,1)S(1)}, bf16[128,1024]{1,0:T(8,128)(2,1)S(1)}, u32[]{:S(2)}, u32[]{:S(2)}) collective-permute-start(bf16[128,1024]{1,0:T(8,128)(2,1)S(1)} %get-tuple-element.28), channel_id=1, source_target_pairs={{0,24},{4,12},{8,0},{12,20},{16,8},{20,28},{24,16},{28,4},{1,25},{... | collective-permute-start | bytes 786440 | tf_op jit(solution)/shard_map/ppermute | solution.py:188
  32.7 1.6 collective-permute-start.10
  34.3 2.6 %collective-permute-done.17 = bf16[128,1024]{1,0:T(8,128)(2,1)S(1)} collective-permute-done((bf16[128,1024]{1,0:T(8,128)(2,1)S(1)}, bf16[128,1024]{1,0:T(8,128)(2,1)S(1)}, u32[]{:S(2)}, u32[]{:S(2)}) %collective-permute-start.17) | collective-permute-done | bytes 262176 | tf_op jit(solution)/shard_map/ppermute | solution.py:188
  36.9 3.1 %collective-permute-start.21 = (bf16[128,1024]{1,0:T(8,128)(2,1)S(1)}, bf16[128,1024]{1,0:T(8,128)(2,1)S(1)}, u32[]{:S(2)}, u32[]{:S(2)}) collective-permute-start(bf16[128,1024]{1,0:T(8,128)(2,1)S(1)} %get-tuple-element.27), channel_id=1, source_target_pairs={{0,4},{4,0},{8,12},{12,8},{16,20},{20,16},{24,28},{28,24},{1,5},{5... | collective-permute-start | bytes 786440 | tf_op jit(solution)/shard_map/ppermute | solution.py:192
  39.9 2.5 %collective-permute-done.14 = bf16[128,1024]{1,0:T(8,128)(2,1)S(1)} collective-permute-done((bf16[128,1024]{1,0:T(8,128)(2,1)S(1)}, bf16[128,1024]{1,0:T(8,128)(2,1)S(1)}, u32[]{:S(2)}, u32[]{:S(2)}) %collective-permute-start.14) | collective-permute-done | bytes 262176 | tf_op jit(solution)/shard_map/ppermute | solution.py:188
  42.5 5.6 %collective-permute-done.8 = bf16[128,1024]{1,0:T(8,128)(2,1)S(1)} collective-permute-done((bf16[128,1024]{1,0:T(8,128)(2,1)S(1)}, bf16[128,1024]{1,0:T(8,128)(2,1)S(1)}, u32[]{:S(2)}, u32[]{:S(2)}) %collective-permute-start.8) | collective-permute-done | bytes 262176 | tf_op jit(solution)/shard_map/ppermute | solution.py:188
  48.1 0.1 broadcast_select_fusion.3
  48.2 3.1 %collective-permute-start.18 = (bf16[128,1024]{1,0:T(8,128)(2,1)S(1)}, bf16[128,1024]{1,0:T(8,128)(2,1)S(1)}, u32[]{:S(2)}, u32[]{:S(2)}) collective-permute-start(bf16[128,1024]{1,0:T(8,128)(2,1)S(1)} %get-tuple-element.31), channel_id=1, source_target_pairs={{0,4},{4,0},{8,12},{12,8},{16,20},{20,16},{24,28},{28,24},{1,5},{5... | collective-permute-start | bytes 786440 | tf_op jit(solution)/shard_map/ppermute | solution.py:192
  51.4 1.4 collective-permute-start.9
  52.8 2.6 %shard_map.65 = bf16[512,1024]{1,0:T(8,128)(2,1)S(1)} custom-call(s32[1]{0:T(128)} %bitcast.6.index, s32[4,128]{1,0:T(4,128)S(1)} %get-tuple-element.39.refs_0_, bf16[128,1024]{1,0:T(8,128)(2,1)S(1)} %get-tuple-element.37.refs_1_, bf16[128,1024]{1,0:T(8,128)(2,1)S(1)} %collective-permute-done.10.refs_2_, bf16[128,1024]{1,0:T(8,128)(2,1)} %collective-permute-done.11.refs_3_, ...), custom_call_target="tpu_custom_call" | custom-call | flops 536870912 | bytes 2097152 | tf_op jit(solution)/shard_map/pallas_call | solution.py:105
  55.4 0.4 collective-permute-done.18
  55.8 5.6 %collective-permute-done.15 = bf16[128,1024]{1,0:T(8,128)(2,1)S(1)} collective-permute-done((bf16[128,1024]{1,0:T(8,128)(2,1)S(1)}, bf16[128,1024]{1,0:T(8,128)(2,1)S(1)}, u32[]{:S(2)}, u32[]{:S(2)}) %collective-permute-start.15) | collective-permute-done | bytes 262176 | tf_op jit(solution)/shard_map/ppermute | solution.py:192
  61.4 5.6 %collective-permute-done.9 = bf16[128,1024]{1,0:T(8,128)(2,1)S(1)} collective-permute-done((bf16[128,1024]{1,0:T(8,128)(2,1)S(1)}, bf16[128,1024]{1,0:T(8,128)(2,1)S(1)}, u32[]{:S(2)}, u32[]{:S(2)}) %collective-permute-start.9) | collective-permute-done | bytes 262176 | tf_op jit(solution)/shard_map/ppermute | solution.py:192
  67.1 1.7 %add_convert_fusion.2 = (bf16[128,1024]{1,0:T(8,128)(2,1)}, f32[128,1024]{1,0:T(8,128)S(1)}, bf16[128,1024]{1,0:T(8,128)(2,1)}, f32[128,1024]{1,0:T(8,128)S(1)},...) fusion(bf16[512,1024]{1,0:T(8,128)(2,1)S(1)} %shard_map.65, ...), kind=kLoop, calls=%fused_computation.23 | loop fusion | flops 6291456 | bytes 7340032 | tf_op jit(solution)/shard_map/convert_element_type | solution.py:197
  68.8 4.2 %collective-permute-start.22 = (bf16[128,1024]{1,0:T(8,128)(2,1)}, bf16[128,1024]{1,0:T(8,128)(2,1)S(1)}, u32[]{:S(2)}, u32[]{:S(2)}) collective-permute-start(bf16[128,1024]{1,0:T(8,128)(2,1)} %get-tuple-element.9), channel_id=1, source_target_pairs={{1,16},{16,1},{3,18},{18,3},{5,20},{20,5},{7,22},{22,7},{9,24},{24... | collective-permute-start | bytes 786440 | tf_op jit(solution)/shard_map/ppermute | solution.py:200
  73.0 2.2 %collective-permute-start = (s32[2]{0:T(128)S(1)}, s32[2]{0:T(128)S(1)}, u32[]{:S(2)}, u32[]{:S(2)}) collective-permute-start(s32[2]{0:T(128)S(1)} %bitcast.59), channel_id=1, source_target_pairs={{1,16},{16,1},{3,18},{18,3},{5,20},{20,5},{7,22},{22,7},{9,24},{24... | collective-permute-start | bytes 32 | tf_op jit(solution)/shard_map/ppermute | solution.py:140
  75.3 4.3 %collective-permute-start.19 = (bf16[128,1024]{1,0:T(8,128)(2,1)}, bf16[128,1024]{1,0:T(8,128)(2,1)S(1)}, u32[]{:S(2)}, u32[]{:S(2)}) collective-permute-start(bf16[128,1024]{1,0:T(8,128)(2,1)} %get-tuple-element.17), channel_id=1, source_target_pairs={{1,16},{16,1},{3,18},{18,3},{5,20},{20,5},{7,22},{22,7},{9,24},{24... | collective-permute-start | bytes 786440 | tf_op jit(solution)/shard_map/ppermute | solution.py:200
  79.5 2.2 %collective-permute-start.16 = (bf16[128,1024]{1,0:T(8,128)(2,1)}, bf16[128,1024]{1,0:T(8,128)(2,1)S(1)}, u32[]{:S(2)}, u32[]{:S(2)}) collective-permute-start(bf16[128,1024]{1,0:T(8,128)(2,1)} %get-tuple-element.19), channel_id=1, source_target_pairs={{1,16},{16,1},{3,18},{18,3},{5,20},{20,5},{7,22},{22,7},{9,24},{24... | collective-permute-start | bytes 786440 | tf_op jit(solution)/shard_map/ppermute | solution.py:200
  81.7 4.3 %collective-permute-start.13 = (bf16[128,1024]{1,0:T(8,128)(2,1)}, bf16[128,1024]{1,0:T(8,128)(2,1)S(1)}, u32[]{:S(2)}, u32[]{:S(2)}) collective-permute-start(bf16[128,1024]{1,0:T(8,128)(2,1)} %get-tuple-element.21), channel_id=1, source_target_pairs={{1,16},{16,1},{3,18},{18,3},{5,20},{20,5},{7,22},{22,7},{9,24},{24... | collective-permute-start | bytes 786440 | tf_op jit(solution)/shard_map/ppermute | solution.py:200
  86.0 1.0 copy-done.5
  87.1 1.0 copy-done.6
  88.1 1.2 copy-done.11
  89.3 3.6 %shard_map.66.refs_12_ = bf16[512,1024]{1,0:T(8,128)(2,1)S(1)} custom-call(f32[128,1024]{1,0:T(8,128)S(1)} %copy-done.6, f32[128,1024]{1,0:T(8,128)S(1)} %copy-done.5, f32[128,1024]{1,0:T(8,128)S(1)} %get-tuple-element.18.refs_2_, f32[128,1024]{1,0:T(8,128)S(1)} %get-tuple-element.10.refs_3_, bf16[512,1024]{1,0:T(8,128)(2,1)S(1)} %bitcast.51), custom_call_target="tpu_custom_call" | custom-call | flops 2684354560 | bytes 4194304 | tf_op jit(solution)/shard_map/pallas_call | solution.py:105
  93.0 0.7 copy-done.13
  93.7 2.4 %collective-permute-start.31 = (bf16[512,1024]{1,0:T(8,128)(2,1)S(1)}, bf16[512,1024]{1,0:T(8,128)(2,1)S(1)}, u32[]{:S(2)}, u32[]{:S(2)}) collective-permute-start(bf16[512,1024]{1,0:T(8,128)(2,1)S(1)} %shard_map.66.refs_12_), channel_id=1, source_target_pairs={{1,16},{16,1},{3,18},{18,3},{5,20},{20,5},{7,22},{22,7},{9,24},{24... | collective-permute-start | bytes 3145736 | tf_op jit(solution)/shard_map/ppermute | solution.py:210
  96.1 1.0 broadcast_select_fusion.6.refs_3_
  97.1 2.8 %collective-permute-start.26 = (bf16[128,1024]{1,0:T(8,128)(2,1)S(1)}, bf16[128,1024]{1,0:T(8,128)(2,1)S(1)}, u32[]{:S(2)}, u32[]{:S(2)}) collective-permute-start(bf16[128,1024]{1,0:T(8,128)(2,1)S(1)} %broadcast_select_fusion.6.refs_3_), channel_id=1, source_target_pairs={{0,8},{4,12},{8,0},{12,4},{16,24},{20,28},{24,16},{28,20},{1,9},{5... | collective-permute-start | bytes 786440 | tf_op jit(solution)/shard_map/ppermute | solution.py:203
  100.0 1.5 collective-permute-start.24
  101.6 0.1 collective-permute-start.23
  101.7 12.4 %collective-permute-done.26.refs_7_ = bf16[128,1024]{1,0:T(8,128)(2,1)S(1)} collective-permute-done((bf16[128,1024]{1,0:T(8,128)(2,1)S(1)}, bf16[128,1024]{1,0:T(8,128)(2,1)S(1)}, u32[]{:S(2)}, u32[]{:S(2)}) %collective-permute-start.26) | collective-permute-done | bytes 262176 | tf_op jit(solution)/shard_map/ppermute | solution.py:203
  114.0 2.8 %collective-permute-done.25.refs_6_ = bf16[128,1024]{1,0:T(8,128)(2,1)} collective-permute-done((bf16[128,1024]{1,0:T(8,128)(2,1)S(1)}, bf16[128,1024]{1,0:T(8,128)(2,1)}, u32[]{:S(2)}, u32[]{:S(2)}) %collective-permute-start.25) | collective-permute-done | bytes 262176 | tf_op jit(solution)/shard_map/ppermute | solution.py:203
  116.8 6.3 %collective-permute-done.24.refs_5_ = bf16[128,1024]{1,0:T(8,128)(2,1)} collective-permute-done((bf16[128,1024]{1,0:T(8,128)(2,1)S(1)}, bf16[128,1024]{1,0:T(8,128)(2,1)}, u32[]{:S(2)}, u32[]{:S(2)}) %collective-permute-start.24) | collective-permute-done | bytes 262176 | tf_op jit(solution)/shard_map/ppermute | solution.py:203
  123.1 2.8 %collective-permute-done.23.refs_4_ = bf16[128,1024]{1,0:T(8,128)(2,1)} collective-permute-done((bf16[128,1024]{1,0:T(8,128)(2,1)S(1)}, bf16[128,1024]{1,0:T(8,128)(2,1)}, u32[]{:S(2)}, u32[]{:S(2)}) %collective-permute-start.23) | collective-permute-done | bytes 262176 | tf_op jit(solution)/shard_map/ppermute | solution.py:203
  126.0 0.5 slice.92
  126.5 0.6 slice.91
  128.4 5.3 %shard_map.67 = bf16[512,1024]{1,0:T(8,128)(2,1)S(1)} custom-call(s32[2]{0:T(128)S(1)} %add_convert_fusion.6.flags, bf16[128,1024]{1,0:T(8,128)(2,1)S(1)} %broadcast_select_fusion.9.refs_0_, bf16[128,1024]{1,0:T(8,128)(2,1)S(1)} %broadcast_select_fusion.8.refs_1_, bf16[128,1024]{1,0:T(8,128)(2,1)S(1)} %broadcast_select_fusion.7.refs_2_, ...), custom_call_target="tpu_custom_call" | custom-call | flops 2684354560 | bytes 6291456 | tf_op jit(solution)/shard_map/pallas_call | solution.py:105
  133.8 0.6 collective-permute-start.32
  134.5 1.5 collective-permute-done.32
  135.9 0.7 collective-permute-done.34
  136.7 0.5 add_convert_fusion.1
  137.2 3.0 %collective-permute-start.33 = (bf16[256,1024]{1,0:T(8,128)(2,1)S(1)}, bf16[256,1024]{1,0:T(8,128)(2,1)S(1)}, u32[]{:S(2)}, u32[]{:S(2)}) collective-permute-start(bf16[256,1024]{1,0:T(8,128)(2,1)S(1)} %get-tuple-element.23), channel_id=1, source_target_pairs={{1,16},{16,1},{3,18},{18,3},{5,20},{20,5},{7,22},{22,7},{9,24},{24... | collective-permute-start | bytes 1572872 | tf_op jit(solution)/shard_map/ppermute | solution.py:226
  140.2 3.5 %collective-permute-start.35 = (bf16[256,1024]{1,0:T(8,128)(2,1)S(1)}, bf16[256,1024]{1,0:T(8,128)(2,1)S(1)}, u32[]{:S(2)}, u32[]{:S(2)}) collective-permute-start(bf16[256,1024]{1,0:T(8,128)(2,1)S(1)} %get-tuple-element.24), channel_id=1, source_target_pairs={{1,16},{16,1},{3,18},{18,3},{5,20},{20,5},{7,22},{22,7},{9,24},{24... | collective-permute-start | bytes 1572872 | tf_op jit(solution)/shard_map/ppermute | solution.py:226
  143.6 16.2 %collective-permute-done.33 = bf16[256,1024]{1,0:T(8,128)(2,1)S(1)} collective-permute-done((bf16[256,1024]{1,0:T(8,128)(2,1)S(1)}, bf16[256,1024]{1,0:T(8,128)(2,1)S(1)}, u32[]{:S(2)}, u32[]{:S(2)}) %collective-permute-start.33) | collective-permute-done | bytes 524320 | tf_op jit(solution)/shard_map/ppermute | solution.py:226
  159.9 5.6 %collective-permute-done.35 = bf16[256,1024]{1,0:T(8,128)(2,1)S(1)} collective-permute-done((bf16[256,1024]{1,0:T(8,128)(2,1)S(1)}, bf16[256,1024]{1,0:T(8,128)(2,1)S(1)}, u32[]{:S(2)}, u32[]{:S(2)}) %collective-permute-start.35) | collective-permute-done | bytes 524320 | tf_op jit(solution)/shard_map/ppermute | solution.py:226
  165.5 1.0 maximum_bitcast_fusion
  (64 shorter events, 1.0 us)
Async XLA Ops:
  0.0 3.3 %copy-start.14 = (s32[2,1,128,1]{2,3,1,0:T(1,128)S(1)}, s32[2,1,128,1]{2,3,1,0:T(1,128)}, u32[]{:S(2)}) copy-start(s32[2,1,128,1]{2,3,1,0:T(1,128)} %param.7) | copy-start | bytes 3076
  0.0 10.7 %copy-start.12 = (bf16[2,1,1,256,512]{4,3,2,1,0:T(8,128)(2,1)S(1)}, bf16[2,1,1,256,512]{4,3,2,1,0:T(8,128)(2,1)}, u32[]{:S(2)}) copy-start(bf16[2,1,1,256,512]{4,3,2,1,0:T(8,128)(2,1)} %param.8) | copy-start | bytes 1572868
  0.0 13.0 %copy-start = (bf16[1,1,512,1024]{3,2,1,0:T(8,128)(2,1)S(1)}, bf16[1,1,512,1024]{3,2,1,0:T(8,128)(2,1)}, u32[]{:S(2)}) copy-start(bf16[1,1,512,1024]{3,2,1,0:T(8,128)(2,1)} %param.10) | copy-start | bytes 3145732
  1.2 11.8 %copy-start.2 = (bf16[128,1024]{1,0:T(8,128)(2,1)}, bf16[128,1024]{1,0:T(8,128)(2,1)S(1)}, u32[]{:S(2)}) copy-start(bf16[128,1024]{1,0:T(8,128)(2,1)S(1)} %get-tuple-element.36.refs_1_) | copy-start | bytes 786436
  1.2 10.3 %collective-permute-start.5 = (bf16[128,1024]{1,0:T(8,128)(2,1)S(1)}, bf16[128,1024]{1,0:T(8,128)(2,1)S(1)}, u32[]{:S(2)}, u32[]{:S(2)}) collective-permute-start(bf16[128,1024]{1,0:T(8,128)(2,1)S(1)} %get-tuple-element.36.refs_1_), channel_id=1, source_target_pairs={{0,2},{1,3},{2,0},{3,1},{4,6},{5,7},{6,4},{7,5},{8,10},{9,11},{10,... | collective-permute-start | bytes 786440 | tf_op jit(solution)/shard_map/ppermute | solution.py:159
  3.3 6.0 %collective-permute-start.2 = (s32[2,128]{1,0:T(2,128)S(1)}, s32[2,128]{1,0:T(2,128)S(1)}, u32[]{:S(2)}, u32[]{:S(2)}) collective-permute-start(s32[2,128]{1,0:T(2,128)S(1)} %bitcast.52), channel_id=1, source_target_pairs={{0,2},{1,3},{2,0},{3,1},{4,6},{5,7},{6,4},{7,5},{8,10},{9,11},{10,... | collective-permute-start | bytes 3080 | tf_op jit(solution)/shard_map/ppermute | solution.py:157
  3.4 8.8 %collective-permute-start.1 = (s32[2,128]{1,0:T(2,128)S(1)}, s32[2,128]{1,0:T(2,128)S(1)}, u32[]{:S(2)}, u32[]{:S(2)}) collective-permute-start(s32[2,128]{1,0:T(2,128)S(1)} %bitcast.53), channel_id=1, source_target_pairs={{0,1},{1,0},{2,3},{3,2},{4,5},{5,4},{6,7},{7,6},{8,9},{9,8},{10,11... | collective-permute-start | bytes 3080 | tf_op jit(solution)/shard_map/ppermute | solution.py:157
  4.4 7.9 %collective-permute-start.4 = (bf16[128,1024]{1,0:T(8,128)(2,1)S(1)}, bf16[128,1024]{1,0:T(8,128)(2,1)S(1)}, u32[]{:S(2)}, u32[]{:S(2)}) collective-permute-start(bf16[128,1024]{1,0:T(8,128)(2,1)S(1)} %get-tuple-element.36.refs_1_), channel_id=1, source_target_pairs={{0,1},{1,0},{2,3},{3,2},{4,5},{5,4},{6,7},{7,6},{8,9},{9,8},{10,11... | collective-permute-start | bytes 786440 | tf_op jit(solution)/shard_map/ppermute | solution.py:159
  9.4 2.8 %collective-permute-start.3 = (s32[2,128]{1,0:T(2,128)S(1)}, s32[2,128]{1,0:T(2,128)S(1)}, u32[]{:S(2)}, u32[]{:S(2)}) collective-permute-start(s32[2,128]{1,0:T(2,128)S(1)} %collective-permute-done.2), channel_id=1, source_target_pairs={{0,1},{1,0},{2,3},{3,2},{4,5},{5,4},{6,7},{7,6},{8,9},{9,8},{10,11... | collective-permute-start | bytes 3080 | tf_op jit(solution)/shard_map/ppermute | solution.py:157
  11.5 1.5 collective-permute-start.6
  11.5 0.7 copy-start.7
  12.3 0.7 copy-start.9
  13.0 1.0 copy-start.3
  14.0 0.9 copy-start.4
  14.9 0.9 copy-start.8
  15.9 0.9 copy-start.10
  16.8 6.0 %copy-start.15 = (s32[1,2]{1,0:T(1,128)S(1)}, s32[1,2]{1,0:T(1,128)}, u32[]{:S(2)}) copy-start(s32[1,2]{1,0:T(1,128)} %param.11) | copy-start | bytes 28
  19.3 9.1 %collective-permute-start.20 = (bf16[128,1024]{1,0:T(8,128)(2,1)}, bf16[128,1024]{1,0:T(8,128)(2,1)}, u32[]{:S(2)}, u32[]{:S(2)}) collective-permute-start(bf16[128,1024]{1,0:T(8,128)(2,1)} %slice.114), channel_id=1, source_target_pairs={{0,24},{4,12},{8,0},{12,20},{16,8},{20,28},{24,16},{28,4},{1,25},{... | collective-permute-start | bytes 786440 | tf_op jit(solution)/shard_map/ppermute | solution.py:188
  22.8 2.8 %collective-permute-start.7 = (s32[2]{0:T(128)S(1)}, s32[2]{0:T(128)S(1)}, u32[]{:S(2)}, u32[]{:S(2)}) collective-permute-start(s32[2]{0:T(128)S(1)} %bitcast.58), channel_id=1, source_target_pairs={{0,4},{4,0},{8,12},{12,8},{16,20},{20,16},{24,28},{28,24},{1,5},{5... | collective-permute-start | bytes 32 | tf_op jit(solution)/shard_map/ppermute | solution.py:139
  22.8 11.4 %collective-permute-start.11 = (bf16[128,1024]{1,0:T(8,128)(2,1)S(1)}, bf16[128,1024]{1,0:T(8,128)(2,1)}, u32[]{:S(2)}, u32[]{:S(2)}) collective-permute-start(bf16[128,1024]{1,0:T(8,128)(2,1)S(1)} %get-tuple-element.37.refs_1_), channel_id=1, source_target_pairs={{0,2},{1,3},{2,0},{3,1},{4,6},{5,7},{6,4},{7,5},{8,10},{9,11},{10,... | collective-permute-start | bytes 786440 | tf_op jit(solution)/shard_map/ppermute | solution.py:159
  29.4 7.4 %collective-permute-start.17 = (bf16[128,1024]{1,0:T(8,128)(2,1)S(1)}, bf16[128,1024]{1,0:T(8,128)(2,1)S(1)}, u32[]{:S(2)}, u32[]{:S(2)}) collective-permute-start(bf16[128,1024]{1,0:T(8,128)(2,1)S(1)} %get-tuple-element.28), channel_id=1, source_target_pairs={{0,24},{4,12},{8,0},{12,20},{16,8},{20,28},{24,16},{28,4},{1,25},{... | collective-permute-start | bytes 786440 | tf_op jit(solution)/shard_map/ppermute | solution.py:188
  32.6 9.9 %collective-permute-start.14 = (bf16[128,1024]{1,0:T(8,128)(2,1)S(1)}, bf16[128,1024]{1,0:T(8,128)(2,1)S(1)}, u32[]{:S(2)}, u32[]{:S(2)}) collective-permute-start(bf16[128,1024]{1,0:T(8,128)(2,1)S(1)} %get-tuple-element.29), channel_id=1, source_target_pairs={{0,24},{4,12},{8,0},{12,20},{16,8},{20,28},{24,16},{28,4},{1,25},{... | collective-permute-start | bytes 786440 | tf_op jit(solution)/shard_map/ppermute | solution.py:188
  32.6 15.5 %collective-permute-start.8 = (bf16[128,1024]{1,0:T(8,128)(2,1)S(1)}, bf16[128,1024]{1,0:T(8,128)(2,1)S(1)}, u32[]{:S(2)}, u32[]{:S(2)}) collective-permute-start(bf16[128,1024]{1,0:T(8,128)(2,1)S(1)} %get-tuple-element.30), channel_id=1, source_target_pairs={{0,24},{4,12},{8,0},{12,20},{16,8},{20,28},{24,16},{28,4},{1,25},{... | collective-permute-start | bytes 786440 | tf_op jit(solution)/shard_map/ppermute | solution.py:188
  32.7 18.7 %collective-permute-start.10 = (bf16[128,1024]{1,0:T(8,128)(2,1)S(1)}, bf16[128,1024]{1,0:T(8,128)(2,1)S(1)}, u32[]{:S(2)}, u32[]{:S(2)}) collective-permute-start(bf16[128,1024]{1,0:T(8,128)(2,1)S(1)} %get-tuple-element.37.refs_1_), channel_id=1, source_target_pairs={{0,1},{1,0},{2,3},{3,2},{4,5},{5,4},{6,7},{7,6},{8,9},{9,8},{10,11... | collective-permute-start | bytes 786440 | tf_op jit(solution)/shard_map/ppermute | solution.py:159
  34.3 18.5 %collective-permute-start.12 = (bf16[128,1024]{1,0:T(8,128)(2,1)}, bf16[128,1024]{1,0:T(8,128)(2,1)S(1)}, u32[]{:S(2)}, u32[]{:S(2)}) collective-permute-start(bf16[128,1024]{1,0:T(8,128)(2,1)} %collective-permute-done.11.refs_3_), channel_id=1, source_target_pairs={{0,1},{1,0},{2,3},{3,2},{4,5},{5,4},{6,7},{7,6},{8,9},{9,8},{10,11... | collective-permute-start | bytes 786440 | tf_op jit(solution)/shard_map/ppermute | solution.py:159
  36.9 15.9 %copy-start.1 = (bf16[256,512]{1,0:T(8,128)(2,1)S(1)}, bf16[256,512]{1,0:T(8,128)(2,1)}, u32[]{:S(2)}) copy-start(bf16[256,512]{1,0:T(8,128)(2,1)} %get-tuple-element.35.refs_5_) | copy-start | bytes 786436
  36.9 18.5 %collective-permute-start.21 = (bf16[128,1024]{1,0:T(8,128)(2,1)S(1)}, bf16[128,1024]{1,0:T(8,128)(2,1)S(1)}, u32[]{:S(2)}, u32[]{:S(2)}) collective-permute-start(bf16[128,1024]{1,0:T(8,128)(2,1)S(1)} %get-tuple-element.27), channel_id=1, source_target_pairs={{0,4},{4,0},{8,12},{12,8},{16,20},{20,16},{24,28},{28,24},{1,5},{5... | collective-permute-start | bytes 786440 | tf_op jit(solution)/shard_map/ppermute | solution.py:192
  48.2 7.6 %collective-permute-start.18 = (bf16[128,1024]{1,0:T(8,128)(2,1)S(1)}, bf16[128,1024]{1,0:T(8,128)(2,1)S(1)}, u32[]{:S(2)}, u32[]{:S(2)}) collective-permute-start(bf16[128,1024]{1,0:T(8,128)(2,1)S(1)} %get-tuple-element.31), channel_id=1, source_target_pairs={{0,4},{4,0},{8,12},{12,8},{16,20},{20,16},{24,28},{28,24},{1,5},{5... | collective-permute-start | bytes 786440 | tf_op jit(solution)/shard_map/ppermute | solution.py:192
  51.3 10.1 %collective-permute-start.15 = (bf16[128,1024]{1,0:T(8,128)(2,1)S(1)}, bf16[128,1024]{1,0:T(8,128)(2,1)S(1)}, u32[]{:S(2)}, u32[]{:S(2)}) collective-permute-start(bf16[128,1024]{1,0:T(8,128)(2,1)S(1)} %get-tuple-element.32), channel_id=1, source_target_pairs={{0,4},{4,0},{8,12},{12,8},{16,20},{20,16},{24,28},{28,24},{1,5},{5... | collective-permute-start | bytes 786440 | tf_op jit(solution)/shard_map/ppermute | solution.py:192
  51.4 15.6 %collective-permute-start.9 = (bf16[128,1024]{1,0:T(8,128)(2,1)S(1)}, bf16[128,1024]{1,0:T(8,128)(2,1)S(1)}, u32[]{:S(2)}, u32[]{:S(2)}) collective-permute-start(bf16[128,1024]{1,0:T(8,128)(2,1)S(1)} %get-tuple-element.33), channel_id=1, source_target_pairs={{0,4},{4,0},{8,12},{12,8},{16,20},{20,16},{24,28},{28,24},{1,5},{5... | collective-permute-start | bytes 786440 | tf_op jit(solution)/shard_map/ppermute | solution.py:192
  68.8 24.2 %collective-permute-start.22 = (bf16[128,1024]{1,0:T(8,128)(2,1)}, bf16[128,1024]{1,0:T(8,128)(2,1)S(1)}, u32[]{:S(2)}, u32[]{:S(2)}) collective-permute-start(bf16[128,1024]{1,0:T(8,128)(2,1)} %get-tuple-element.9), channel_id=1, source_target_pairs={{1,16},{16,1},{3,18},{18,3},{5,20},{20,5},{7,22},{22,7},{9,24},{24... | collective-permute-start | bytes 786440 | tf_op jit(solution)/shard_map/ppermute | solution.py:200
  73.0 28.5 %collective-permute-start = (s32[2]{0:T(128)S(1)}, s32[2]{0:T(128)S(1)}, u32[]{:S(2)}, u32[]{:S(2)}) collective-permute-start(s32[2]{0:T(128)S(1)} %bitcast.59), channel_id=1, source_target_pairs={{1,16},{16,1},{3,18},{18,3},{5,20},{20,5},{7,22},{22,7},{9,24},{24... | collective-permute-start | bytes 32 | tf_op jit(solution)/shard_map/ppermute | solution.py:140
  75.3 21.8 %collective-permute-start.19 = (bf16[128,1024]{1,0:T(8,128)(2,1)}, bf16[128,1024]{1,0:T(8,128)(2,1)S(1)}, u32[]{:S(2)}, u32[]{:S(2)}) collective-permute-start(bf16[128,1024]{1,0:T(8,128)(2,1)} %get-tuple-element.17), channel_id=1, source_target_pairs={{1,16},{16,1},{3,18},{18,3},{5,20},{20,5},{7,22},{22,7},{9,24},{24... | collective-permute-start | bytes 786440 | tf_op jit(solution)/shard_map/ppermute | solution.py:200
  79.5 20.3 %collective-permute-start.16 = (bf16[128,1024]{1,0:T(8,128)(2,1)}, bf16[128,1024]{1,0:T(8,128)(2,1)S(1)}, u32[]{:S(2)}, u32[]{:S(2)}) collective-permute-start(bf16[128,1024]{1,0:T(8,128)(2,1)} %get-tuple-element.19), channel_id=1, source_target_pairs={{1,16},{16,1},{3,18},{18,3},{5,20},{20,5},{7,22},{22,7},{9,24},{24... | collective-permute-start | bytes 786440 | tf_op jit(solution)/shard_map/ppermute | solution.py:200
  81.7 18.3 %collective-permute-start.13 = (bf16[128,1024]{1,0:T(8,128)(2,1)}, bf16[128,1024]{1,0:T(8,128)(2,1)S(1)}, u32[]{:S(2)}, u32[]{:S(2)}) collective-permute-start(bf16[128,1024]{1,0:T(8,128)(2,1)} %get-tuple-element.21), channel_id=1, source_target_pairs={{1,16},{16,1},{3,18},{18,3},{5,20},{20,5},{7,22},{22,7},{9,24},{24... | collective-permute-start | bytes 786440 | tf_op jit(solution)/shard_map/ppermute | solution.py:200
  86.0 1.0 copy-start.5
  87.1 1.0 copy-start.6
  88.1 1.2 copy-start.11
  93.0 0.7 copy-start.13
  93.7 34.7 %collective-permute-start.31 = (bf16[512,1024]{1,0:T(8,128)(2,1)S(1)}, bf16[512,1024]{1,0:T(8,128)(2,1)S(1)}, u32[]{:S(2)}, u32[]{:S(2)}) collective-permute-start(bf16[512,1024]{1,0:T(8,128)(2,1)S(1)} %shard_map.66.refs_12_), channel_id=1, source_target_pairs={{1,16},{16,1},{3,18},{18,3},{5,20},{20,5},{7,22},{22,7},{9,24},{24... | collective-permute-start | bytes 3145736 | tf_op jit(solution)/shard_map/ppermute | solution.py:210
  97.1 17.0 %collective-permute-start.26 = (bf16[128,1024]{1,0:T(8,128)(2,1)S(1)}, bf16[128,1024]{1,0:T(8,128)(2,1)S(1)}, u32[]{:S(2)}, u32[]{:S(2)}) collective-permute-start(bf16[128,1024]{1,0:T(8,128)(2,1)S(1)} %broadcast_select_fusion.6.refs_3_), channel_id=1, source_target_pairs={{0,8},{4,12},{8,0},{12,4},{16,24},{20,28},{24,16},{28,20},{1,9},{5... | collective-permute-start | bytes 786440 | tf_op jit(solution)/shard_map/ppermute | solution.py:203
  99.9 17.0 %collective-permute-start.25 = (bf16[128,1024]{1,0:T(8,128)(2,1)S(1)}, bf16[128,1024]{1,0:T(8,128)(2,1)}, u32[]{:S(2)}, u32[]{:S(2)}) collective-permute-start(bf16[128,1024]{1,0:T(8,128)(2,1)S(1)} %broadcast_select_fusion.7.refs_2_), channel_id=1, source_target_pairs={{0,8},{4,12},{8,0},{12,4},{16,24},{20,28},{24,16},{28,20},{1,9},{5... | collective-permute-start | bytes 786440 | tf_op jit(solution)/shard_map/ppermute | solution.py:203
  100.0 23.1 %collective-permute-start.24 = (bf16[128,1024]{1,0:T(8,128)(2,1)S(1)}, bf16[128,1024]{1,0:T(8,128)(2,1)}, u32[]{:S(2)}, u32[]{:S(2)}) collective-permute-start(bf16[128,1024]{1,0:T(8,128)(2,1)S(1)} %broadcast_select_fusion.8.refs_1_), channel_id=1, source_target_pairs={{0,8},{4,12},{8,0},{12,4},{16,24},{20,28},{24,16},{28,20},{1,9},{5... | collective-permute-start | bytes 786440 | tf_op jit(solution)/shard_map/ppermute | solution.py:203
  101.6 24.4 %collective-permute-start.23 = (bf16[128,1024]{1,0:T(8,128)(2,1)S(1)}, bf16[128,1024]{1,0:T(8,128)(2,1)}, u32[]{:S(2)}, u32[]{:S(2)}) collective-permute-start(bf16[128,1024]{1,0:T(8,128)(2,1)S(1)} %broadcast_select_fusion.9.refs_0_), channel_id=1, source_target_pairs={{0,8},{4,12},{8,0},{12,4},{16,24},{20,28},{24,16},{28,20},{1,9},{5... | collective-permute-start | bytes 786440 | tf_op jit(solution)/shard_map/ppermute | solution.py:203
  114.0 14.4 %collective-permute-start.30 = (bf16[128,1024]{1,0:T(8,128)(2,1)S(1)}, bf16[128,1024]{1,0:T(8,128)(2,1)}, u32[]{:S(2)}, u32[]{:S(2)}) collective-permute-start(bf16[128,1024]{1,0:T(8,128)(2,1)S(1)} %collective-permute-done.26.refs_7_), channel_id=1, source_target_pairs={{0,1},{1,0},{2,3},{3,2},{4,5},{5,4},{6,7},{7,6},{8,9},{9,8},{10,11... | collective-permute-start | bytes 786440 | tf_op jit(solution)/shard_map/ppermute | solution.py:204
  116.8 11.6 %collective-permute-start.29 = (bf16[128,1024]{1,0:T(8,128)(2,1)}, bf16[128,1024]{1,0:T(8,128)(2,1)}, u32[]{:S(2)}, u32[]{:S(2)}) collective-permute-start(bf16[128,1024]{1,0:T(8,128)(2,1)} %collective-permute-done.25.refs_6_), channel_id=1, source_target_pairs={{0,1},{1,0},{2,3},{3,2},{4,5},{5,4},{6,7},{7,6},{8,9},{9,8},{10,11... | collective-permute-start | bytes 786440 | tf_op jit(solution)/shard_map/ppermute | solution.py:204
  123.1 5.2 %collective-permute-start.28 = (bf16[128,1024]{1,0:T(8,128)(2,1)}, bf16[128,1024]{1,0:T(8,128)(2,1)}, u32[]{:S(2)}, u32[]{:S(2)}) collective-permute-start(bf16[128,1024]{1,0:T(8,128)(2,1)} %collective-permute-done.24.refs_5_), channel_id=1, source_target_pairs={{0,1},{1,0},{2,3},{3,2},{4,5},{5,4},{6,7},{7,6},{8,9},{9,8},{10,11... | collective-permute-start | bytes 786440 | tf_op jit(solution)/shard_map/ppermute | solution.py:204
  126.0 2.4 %collective-permute-start.27 = (bf16[128,1024]{1,0:T(8,128)(2,1)}, bf16[128,1024]{1,0:T(8,128)(2,1)}, u32[]{:S(2)}, u32[]{:S(2)}) collective-permute-start(bf16[128,1024]{1,0:T(8,128)(2,1)} %collective-permute-done.23.refs_4_), channel_id=1, source_target_pairs={{0,1},{1,0},{2,3},{3,2},{4,5},{5,4},{6,7},{7,6},{8,9},{9,8},{10,11... | collective-permute-start | bytes 786440 | tf_op jit(solution)/shard_map/ppermute | solution.py:204
  133.8 2.1 %collective-permute-start.32 = (bf16[256,1024]{1,0:T(8,128)(2,1)S(1)}, bf16[256,1024]{1,0:T(8,128)(2,1)S(1)}, u32[]{:S(2)}, u32[]{:S(2)}) collective-permute-start(bf16[256,1024]{1,0:T(8,128)(2,1)S(1)} %get-tuple-element.25), channel_id=1, source_target_pairs={{0,1},{1,0},{2,3},{3,2},{4,5},{5,4},{6,7},{7,6},{8,9},{9,8},{10,11... | collective-permute-start | bytes 1572872 | tf_op jit(solution)/shard_map/ppermute | solution.py:224
  134.4 2.3 %collective-permute-start.34 = (bf16[256,1024]{1,0:T(8,128)(2,1)S(1)}, bf16[256,1024]{1,0:T(8,128)(2,1)S(1)}, u32[]{:S(2)}, u32[]{:S(2)}) collective-permute-start(bf16[256,1024]{1,0:T(8,128)(2,1)S(1)} %get-tuple-element.26), channel_id=1, source_target_pairs={{0,1},{1,0},{2,3},{3,2},{4,5},{5,4},{6,7},{7,6},{8,9},{9,8},{10,11... | collective-permute-start | bytes 1572872 | tf_op jit(solution)/shard_map/ppermute | solution.py:224
  137.2 22.6 %collective-permute-start.33 = (bf16[256,1024]{1,0:T(8,128)(2,1)S(1)}, bf16[256,1024]{1,0:T(8,128)(2,1)S(1)}, u32[]{:S(2)}, u32[]{:S(2)}) collective-permute-start(bf16[256,1024]{1,0:T(8,128)(2,1)S(1)} %get-tuple-element.23), channel_id=1, source_target_pairs={{1,16},{16,1},{3,18},{18,3},{5,20},{20,5},{7,22},{22,7},{9,24},{24... | collective-permute-start | bytes 1572872 | tf_op jit(solution)/shard_map/ppermute | solution.py:226
  140.2 25.3 %collective-permute-start.35 = (bf16[256,1024]{1,0:T(8,128)(2,1)S(1)}, bf16[256,1024]{1,0:T(8,128)(2,1)S(1)}, u32[]{:S(2)}, u32[]{:S(2)}) collective-permute-start(bf16[256,1024]{1,0:T(8,128)(2,1)S(1)} %get-tuple-element.24), channel_id=1, source_target_pairs={{1,16},{16,1},{3,18},{18,3},{5,20},{20,5},{7,22},{22,7},{9,24},{24... | collective-permute-start | bytes 1572872 | tf_op jit(solution)/shard_map/ppermute | solution.py:226

commit v2 on v1

v2 whole, which is shorter than its diff:
```python
import functools
import math

import jax
import jax.numpy as jnp
from jax import lax
from jax.experimental import pallas as pl
from jax.experimental.pallas import tpu as pltpu
from jax.sharding import PartitionSpec as P

NS_ITERS = 2
CHUNKS = 2
SERIAL_X = False
LAG_X = 9
SERIAL_T = True
LAG_T = 9
SERIAL_W = True
NS_AFTER = 0
GATE = False
VMEM_LIMIT = 32 * 1024 * 1024

coef_a = 3.4445
coef_b = -4.775
coef_c = 2.0315
step_scale = 32.0
weight_hop = 4

ANY = pl.BlockSpec(memory_space=pl.ANY)
VMEM = pl.BlockSpec(memory_space=pltpu.VMEM)


def dot(a, b, dims):
    return lax.dot_general(a, b, (dims, ((), ())), preferred_element_type=jnp.float32)


def newton_schulz(current):
    for repeat in range(NS_ITERS):
        gram = dot(current, current, ((1,), (1,))).astype(jnp.bfloat16)
        squared = dot(gram, gram, ((1,), (0,)))
        poly = (coef_b * gram.astype(jnp.float32) + coef_c * squared).astype(jnp.bfloat16)
        product = dot(poly, current, ((1,), (0,)))
        current = (coef_a * current.astype(jnp.float32) + product).astype(jnp.bfloat16)
    return current


def normalized(tracked):
    total = sum(jnp.sum(part * part) for part in tracked)
    scale = 1.0 / (jnp.sqrt(total) + 1e-07)
    return jnp.concatenate([(part * scale).astype(jnp.bfloat16) for part in tracked], axis=0)


def first_step_kernel(chunks, *refs):
    offset, grads, partners = refs[0], refs[1 : 1 + chunks], refs[1 + chunks : 1 + 2 * chunks]
    weight, moved = refs[1 + 2 * chunks :]
    rows = grads[0].shape[0]
    tracked = []
    for k in range(chunks):
        own = offset[k * rows : (k + 1) * rows, :].astype(jnp.float32) + grads[k][...].astype(jnp.float32)
        tracked.append(0.5 * (own + partners[k][...].astype(jnp.float32)))
    ortho = newton_schulz(normalized(tracked))
    moved[...] = (
        weight[...].astype(jnp.float32) - step_scale * ortho.astype(jnp.float32)
    ).astype(moved.dtype)


def second_step_kernel(chunks, flag, *refs):
    own, same, other = refs[:chunks], refs[chunks : 2 * chunks], refs[2 * chunks : 3 * chunks]
    (ortho,) = refs[3 * chunks :]
    use_same = flag[0:1, 0:1] == 1
    tracked = []
    for k in range(chunks):
        partner = jnp.where(use_same, same[k][...].astype(jnp.float32), other[k][...].astype(jnp.float32))
        tracked.append(0.5 * (own[k][...].astype(jnp.float32) + partner))
    ortho[...] = newton_schulz(normalized(tracked))


def gradient_kernel(sources, with_sum, *refs):
    tokens, hidden, refs = refs[:sources], refs[sources], refs[sources + 1 :]
    rows = hidden.shape[0]
    slots = rows // sources
    count = tokens[0].shape[0] - 16
    mine = lax.axis_index("expert")
    earlier = (
        lax.broadcasted_iota(jnp.int32, (count, count), 0)
        < lax.broadcasted_iota(jnp.int32, (count, count), 1)
    ).astype(jnp.bfloat16)
    slot = lax.broadcasted_iota(jnp.int32, (slots, count), 0).astype(jnp.float32)
    taken = []
    for j in range(sources):
        named = tokens[j][count : count + 16, :count].astype(jnp.float32)
        match = jnp.where(named == mine.astype(jnp.float32), 1.0, 0.0)
        position = dot(match.astype(jnp.bfloat16), earlier, ((1,), (0,)))[0:1, :]
        chosen = jnp.where((slot == position) & (match[0:1, :] > 0.5), 1.0, 0.0).astype(jnp.bfloat16)
        start = pl.multiple_of((mine ^ j) * slots, slots)
        taken.append(dot(chosen, hidden[pl.ds(start, slots), :], ((0,), (0,))).astype(jnp.bfloat16))
    spread = jnp.concatenate(taken, axis=0)
    everything = jnp.concatenate([t[:count, :] for t in tokens], axis=0)
    product = dot(spread, everything, ((0,), (0,)))
    grad = (product * (1.0 / math.sqrt(rows))).astype(jnp.bfloat16)
    if with_sum:
        offset, refs = refs[0], refs[1:]
        summed = (offset[...].astype(jnp.float32) + grad.astype(jnp.float32)).astype(jnp.bfloat16)
        refs, sums = refs[: len(refs) // 2], refs[len(refs) // 2 :]
    depth = refs[0].shape[0]
    for k, out in enumerate(refs):
        out[...] = grad[k * depth : (k + 1) * depth, :]
        if with_sum:
            sums[k][...] = summed[k * depth : (k + 1) * depth, :]


def call(kernel, operands, out_shapes, flops):
    arrays = [a[0] if isinstance(a, tuple) else a for a in operands]
    fetched = {i: a[1] for i, a in enumerate(operands) if isinstance(a, tuple)}
    shapes = [a.shape if fetched.get(i) is None else a.shape[1:] for i, a in enumerate(arrays)]
    count, results, copied = len(arrays), len(out_shapes), list(fetched)

    def body(*refs):
        sources, targets = list(refs[:count]), refs[count : count + results]
        copies = []
        for n, i in enumerate(copied):
            source = sources[i] if fetched[i] is None else sources[i].at[fetched[i]]
            buffer = refs[count + results + n]
            copies.append(pltpu.make_async_copy(source, buffer, refs[-1].at[n]))
            sources[i] = buffer
        for copy in copies:
            copy.start()
        for copy in copies:
            copy.wait()
        kernel(*sources, *targets)

    moved = sum(math.prod(s) * a.dtype.itemsize for s, a in zip(shapes, arrays))
    moved += sum(math.prod(s.shape) * s.dtype.itemsize for s in out_shapes)
    return pl.pallas_call(
        body,
        in_specs=[ANY if i in fetched else VMEM for i in range(count)],
        out_specs=[VMEM] * results,
        out_shape=out_shapes,
        scratch_shapes=[pltpu.VMEM(shapes[i], arrays[i].dtype) for i in copied]
        + [pltpu.SemaphoreType.DMA((max(1, len(copied)),))],
        compiler_params=pltpu.CompilerParams(vmem_limit_bytes=VMEM_LIMIT),
        cost_estimate=pl.CostEstimate(flops=flops, bytes_accessed=moved, transcendentals=0),
    )(*arrays)


def after(value, earlier):
    return lax.optimization_barrier((value, earlier))[0]


def paired(out_grads, routes, hiddens, weights, tracker_offset, partner_bits):
    sites, experts = lax.axis_size("site"), lax.axis_size("expert")
    half = sites // 2
    site, expert = lax.axis_index("site"), lax.axis_index("expert")
    both = ("site", "expert")

    cross, kept, from_mate, lent = [], [], [], []
    for s in range(half):
        for e in range(0, experts, 2):
            low, high = s * experts + e, (s + half) * experts + e
            cross += [(low + 1, high), (high, low + 1)]
            kept += [(low, low), (high + 1, high + 1)]
            from_mate += [(low, low + 1), (high + 1, high)]
            lent += [(high, low), (low + 1, high + 1)]
    swap = cross + kept
    mates = [(e, e ^ 1) for e in range(experts)]
    beside = [(s, s ^ 1) for s in range(sites)]
    helpers = [(s, (s + 2) % sites if s % 2 else (s - 2) % sites) for s in range(sites)]
    within = [(s, s // half * half + (s + 2) % half) for s in range(sites)]

    weight, offset = weights[0, 0], tracker_offset[0, 0]
    stashed = hiddens[:, 0, 0]
    tokens, routing = out_grads[:, 0], routes[:, 0, :, 0]
    steps = tokens.shape[0]
    fan_rows, features = weight.shape
    bits = partner_bits[0]
    is_swapped = (site < half) == (expert % 2 == 1)

    beside_bits = lax.ppermute(bits, "site", beside)
    swap_bits = lax.ppermute(bits, both, swap)
    send_own = jnp.where(site % 2 == 1, beside_bits[0] == 1, beside_bits[0] == 0)
    problem = site % half + half * (expert % 2)
    wanted = jnp.where(swap_bits[1] == 1, problem + 2, problem - 2 + sites) % sites
    use_same = wanted == (site + half - 2) % half + half * (expert % 2)
    use_same = jnp.full((8, 128), use_same.astype(jnp.int32))

    count = tokens.shape[1]
    named = routing.astype(jnp.bfloat16).reshape(steps, 1, count)
    named = jnp.pad(named, ((0, 0), (0, 15), (0, features - count)))
    gathered = [{0: jnp.concatenate([tokens[k], named[k]], axis=0)} for k in range(steps)]
    top = experts // 2
    for k in range(steps):
        level = top
        if k > 0:
            gathered[k][0] = after(gathered[k][0], gathered[k - 1][top])
        while level >= 1:
            hop = [(e, e ^ level) for e in range(experts)]
            gathered[k].update({j ^ level: lax.ppermute(t, "expert", hop) for j, t in gathered[k].items()})
            if k == 0 and level == top:
                gathered[k][top], (send_own, use_same) = lax.optimization_barrier(
                    (gathered[k][top], (send_own, use_same))
                )
            level //= 2

    rows = fan_rows // CHUNKS
    parts = [slice(i * rows, (i + 1) * rows) for i in range(CHUNKS)]
    chunk = [jax.ShapeDtypeStruct((rows, features), jnp.bfloat16)] * CHUNKS
    whole = [jax.ShapeDtypeStruct((fan_rows, features), jnp.bfloat16)]
    cost = 2 * fan_rows * features * experts * count
    operands = [gathered[0][j] for j in range(experts)] + [(stashed, 0), (offset, None)]
    made = call(functools.partial(gradient_kernel, experts, True), operands, chunk * 2, cost)
    first, own = made[:CHUNKS], list(made[CHUNKS:])
    fetched = [lax.ppermute(o, "site", helpers) for o in own]
    operands = [gathered[1][j] for j in range(experts)] + [(stashed, 1)]
    last = call(functools.partial(gradient_kernel, experts, False), operands, chunk, cost)

    chosen, partners, second, mine, same, other = [], [], [], [], [], []
    for i in range(CHUNKS):
        arrived = after(fetched[i], last[0] if i == 0 else chosen[i - 1])
        chosen.append(jnp.where(send_own, own[i], arrived))
    for i in range(CHUNKS):
        if i > 0:
            chosen[i] = after(chosen[i], partners[i - 1]) if SERIAL_X else chosen[i]
        if i >= LAG_X:
            chosen[i] = after(chosen[i], mine[i - LAG_X])
        partners.append(lax.ppermute(chosen[i], "site", beside))
        partner = partners[i] if i == 0 else after(partners[i], second[i - 1])
        grad = first[i].astype(jnp.float32)
        tracked = 0.5 * ((offset[parts[i]].astype(jnp.float32) + grad) + partner.astype(jnp.float32))
        later = (tracked - grad).astype(jnp.bfloat16).astype(jnp.float32)
        second.append((later + last[i].astype(jnp.float32)).astype(jnp.bfloat16))
        if i > 0 and SERIAL_T:
            second[i] = after(second[i], mine[i - 1])
        if i >= LAG_T:
            second[i] = after(second[i], same[i - LAG_T])
        mine.append(lax.ppermute(second[i], both, swap))
        if i < CHUNKS - 1:
            value = mine[i]
            if i > 0 and SERIAL_W:
                value = after(value, same[i - 1])
            same.append(lax.ppermute(value, "site", within))

    cost = NS_ITERS * 2 * (2 * fan_rows * fan_rows * features + fan_rows**3)
    held = [after(partners[-1], mine[NS_AFTER])]
    (moved,) = call(
        functools.partial(first_step_kernel, CHUNKS),
        [(offset, None), *first, *partners[:-1], *held, (weight, None)],
        whole,
        cost,
    )
    value = after(mine[-1], moved)
    if SERIAL_W:
        value = after(value, same[-1])
    same.append(lax.ppermute(value, "site", within))
    other = [lax.ppermute(value, "expert", mates) for value in same]
    borrowed = lax.ppermute(after(moved, mine[-1]), both, lent)
    if GATE:
        other[-1] = after(other[-1], borrowed)
    shared = (moved.astype(jnp.float32) + borrowed.astype(jnp.float32)).astype(jnp.bfloat16)
    given = lax.ppermute(shared, both, from_mate)
    shared = jnp.where(is_swapped, given, shared)
    (ortho,) = call(
        functools.partial(second_step_kernel, CHUNKS), [use_same, *mine, *same, *other], whole, cost
    )
    paired_ortho = lax.ppermute(ortho, "expert", mates)
    result = 0.5 * shared.astype(jnp.float32) - 0.5 * step_scale * (
        ortho.astype(jnp.float32) + paired_ortho.astype(jnp.float32)
    )
    return lax.ppermute(result.astype(jnp.bfloat16)[None, None], both, swap)


def from_behind(block, axis, distance):
    devices = range(lax.axis_size(axis))
    route = [((i - distance) % len(devices), i) for i in devices]
    return lax.ppermute(block, axis, route)


def orthogonalize(tracked):
    frobenius = jnp.sqrt(jnp.sum(tracked * tracked))
    return newton_schulz((tracked / (frobenius + 1e-07)).astype(jnp.bfloat16))


def place_rows(gradient, routing, experts, slot_count):
    owned = (routing[:, None] == jnp.arange(experts, dtype=jnp.int32)[None, :]).astype(jnp.int32)
    earlier = jnp.cumsum(owned, axis=0) - owned
    position = jnp.sum(earlier * owned, axis=1)
    target = routing * slot_count + position
    selector = (
        target[None, :] == jnp.arange(experts * slot_count, dtype=jnp.int32)[:, None]
    ).astype(jnp.bfloat16)
    placed = dot(selector, gradient, ((1,), (0,))).astype(jnp.bfloat16)
    return placed.reshape(experts, slot_count, gradient.shape[1])


def general(out_grads, routes, hiddens, weights, tracker_offset, partner_bits):
    experts = lax.axis_size("expert")
    stashed = hiddens[:, 0, 0]
    steps, slot_rows = stashed.shape[:2]
    slot_count = slot_rows // experts
    direction = partner_bits[0]
    weight, offset = weights[0, 0], tracker_offset[0, 0]
    placed = [place_rows(out_grads[k, 0], routes[k, 0, :, 0], experts, slot_count) for k in range(steps)]
    arrived = lax.all_to_all(jnp.stack(placed), "expert", split_axis=1, concat_axis=1, tiled=True)
    updates = jnp.zeros(weight.shape, jnp.float32)
    for k in range(steps):
        product = dot(stashed[k], arrived[k].reshape(slot_rows, -1), ((0,), (0,)))
        gradient = (product * (1.0 / math.sqrt(slot_rows))).astype(jnp.bfloat16).astype(jnp.float32)
        summed = offset.astype(jnp.float32) + gradient
        sent = summed.astype(jnp.bfloat16)
        distance = 2**k
        partner = jnp.where(
            direction[k] == 1,
            from_behind(sent, "site", -distance),
            from_behind(sent, "site", distance),
        )
        tracked = 0.5 * (summed + partner.astype(jnp.float32))
        offset = (tracked - gradient).astype(jnp.bfloat16)
        updates = updates + orthogonalize(tracked).astype(jnp.float32)
    updated = weight.astype(jnp.float32) - step_scale * updates
    sent = updated.astype(jnp.bfloat16)
    beside = from_behind(sent, "site", -weight_hop).astype(jnp.float32) + from_behind(
        sent, "site", weight_hop
    ).astype(jnp.float32)
    return (0.5 * updated + 0.25 * beside).astype(jnp.bfloat16)[None, None]


def solution(mesh):
    in_specs = (
        P(None, "site", "expert", None),
        P(None, "site", "expert", None),
        P(None, "site", "expert", None, None),
        P("site", "expert", None, None),
        P("site", "expert", None, None),
        P("site", None),
    )
    out_specs = P("site", "expert", None, None)
    sites, experts = mesh.shape["site"], mesh.shape["expert"]
    pairs = sites == 2 * weight_hop and experts in (2, 4)
    local = paired if pairs else general
    return jax.shard_map(local, mesh=mesh, in_specs=in_specs, out_specs=out_specs, check_vma=False)
```

time: 167 us -> 144 us (0.86)
  starting transfers between devices: 52.8 us -> 38.4 us
  local copies, waits for them, and re-layouts: 13.2 us -> 2.76 us
  waiting for transfers between devices: 80 us -> 86 us
    ppermute x21 -> x11, starting transfers between devices: 36.6 us -> 19.9 us  [the longest x2 6.68 us: paired(): mine.append(lax.ppermute(second[i], both, swap))]
    ppermute x21 -> x11, waiting for transfers between devices: 40.6 us -> 56.6 us  [the longest x1 23.3 us: paired(): return lax.ppermute(result.astype(jnp.bfloat16)[None, None], both, swap)]
    ppermute x4 -> x2, waiting for transfers between devices: 24.3 us -> 14.8 us  [paired(): same.append(lax.ppermute(value, 'site', within))]
    unnamed x32 -> x9, local copies, waits for them, and re-layouts: 9.23 us -> 0.99 us
    select_n x8 -> x2, other arithmetic: 2.36 us -> 0.11 us  [paired(): chosen.append(jnp.where(send_own, own[i], arrived))]
    ppermute x6, waiting for transfers between devices: 0.08 us -> 1.95 us  [paired(): lax.ppermute(t, 'expert', hop)]
    ppermute x4 -> x2, starting transfers between devices: 4.45 us -> 5.59 us  [paired(): same.append(lax.ppermute(value, 'site', within))]
    ppermute x4 -> x2, waiting for transfers between devices: 13.4 us -> 12.6 us  [paired(): fetched = [lax.ppermute(o, 'site', helpers) for o in own]]
  transfers between devices with their start and end apart: 36 -> 22, of which waited for: 18 -> 14; matrix products, arithmetic and copies ran while one was open for 3% -> 1% of each run, Pallas kernels for 4% -> 8%
where the time goes in v2:
time: 144 us
  waiting for transfers between devices  86 us (60%)
  starting transfers between devices  38.4 us (27%)
  Pallas kernels  11.8 us (8%)
  other arithmetic  4.18 us (3%)
  local copies, waits for them, and re-layouts  2.76 us (2%)
    ppermute x1, waiting for transfers between devices, paired(): return lax.ppermute(result.astype(jnp.bfloat16)[None, None], both, swap)  23.3 us
    ppermute x2, waiting for transfers between devices, paired(): same.append(lax.ppermute(value, 'site', within))  14.8 us
    ppermute x2, waiting for transfers between devices, paired(): mine.append(lax.ppermute(second[i], both, swap))  13.6 us
    ppermute x2, waiting for transfers between devices, paired(): fetched = [lax.ppermute(o, 'site', helpers) for o in own]  12.6 us
    pallas_call x4, Pallas kernels, call(): pl.pallas_call(body, in_specs=[ANY if i in fetched else VMEM for i in ran...  11.8 us
    ppermute x1, waiting for transfers between devices, paired(): given = lax.ppermute(shared, both, from_mate)  10.3 us
    ppermute x2, starting transfers between devices, paired(): fetched = [lax.ppermute(o, 'site', helpers) for o in own]  7.18 us
    ppermute x2, starting transfers between devices, paired(): mine.append(lax.ppermute(second[i], both, swap))  6.68 us
  transfers between devices with their start and end apart: 22, of which 14 were waited for; matrix products, arithmetic and copies ran while one was open for 1% of the time, Pallas kernels for 8%

profile of v2, /device:TPU:1, one launch (start us, length us, event | category | flops | bytes accessed | tf_op | source)
XLA Modules:
  0.0 144.2 jit_solution(15310384932244033970)
XLA Ops:
  0.0 0.0 copy-start.3
  0.0 0.7 convert_bitcast_fusion
  0.7 0.0 copy-start.1
  0.7 1.2 slice_bitcast_fusion
  1.9 2.1 %collective-permute-start.1 = (bf16[144,1024]{1,0:T(8,128)(2,1)S(1)}, bf16[144,1024]{1,0:T(8,128)(2,1)S(1)}, u32[]{:S(2)}, u32[]{:S(2)}) collective-permute-start(bf16[144,1024]{1,0:T(8,128)(2,1)S(1)} %pad_maximum_fusion.refs_0_), channel_id=1, source_target_pairs={{0,2},{1,3},{2,0},{3,1},{4,6},{5,7},{6,4},{7,5},{8,10},{9,11},{10,... | collective-permute-start | bytes 884744 | tf_op jit(solution)/shard_map/ppermute | solution.py:196
  4.1 0.0 copy-done.3
  4.1 1.2 collective-permute-start.2
  5.3 5.3 %collective-permute-start.3 = (s32[2]{0:T(128)S(1)}, s32[2]{0:T(128)S(1)}, u32[]{:S(2)}, u32[]{:S(2)}) collective-permute-start(s32[2]{0:T(128)S(1)} %bitcast.32), channel_id=1, source_target_pairs={{1,16},{16,1},{3,18},{18,3},{5,20},{20,5},{7,22},{22,7},{9,24},{24... | collective-permute-start | bytes 32 | tf_op jit(solution)/shard_map/ppermute | solution.py:178
  10.6 0.1 collective-permute-start
  10.7 1.1 collective-permute-done.3
  11.8 0.6 slice.32
  13.1 0.0 collective-permute-done.2
  13.2 0.0 collective-permute-done.1.refs_2_
  13.2 0.1 collective-permute-start.4
  13.3 0.3 collective-permute-start.7
  13.6 0.0 collective-permute-done.refs_1_
  13.6 1.2 collective-permute-done.4.refs_3_
  14.8 0.0 copy-done
  14.9 0.0 copy-done.1
  14.9 1.8 %shard_map.64 = (bf16[256,1024]{1,0:T(8,128)(2,1)S(1)}, bf16[256,1024]{1,0:T(8,128)(2,1)S(1)}, bf16[256,1024]{1,0:T(8,128)(2,1)S(1)}, bf16[256,1024]{1,0:T(8,128)(2,1)S(1)}) custom-call(bf16[144,1024]{1,0:T(8,128)(2,1)S(1)} %pad_maximum_fusion.refs_0_, bf16[144,1024]{1,0:T(8,128)(2,1)S(1)} %collective-permute-done.refs_1_, ...), custom_call_target="tpu_custom_call" | custom-call | flops 536870912 | bytes 4587520 | tf_op jit(solution)/shard_map/pallas_call | solution.py:133
  16.7 3.4 %collective-permute-start.5 = (bf16[256,1024]{1,0:T(8,128)(2,1)S(1)}, bf16[256,1024]{1,0:T(8,128)(2,1)S(1)}, u32[]{:S(2)}, u32[]{:S(2)}) collective-permute-start(bf16[256,1024]{1,0:T(8,128)(2,1)S(1)} %get-tuple-element.27), channel_id=1, source_target_pairs={{0,24},{4,12},{8,0},{12,20},{16,8},{20,28},{24,16},{28,4},{1,25},{... | collective-permute-start | bytes 1572872 | tf_op jit(solution)/shard_map/ppermute | solution.py:211
  20.1 0.7 collective-permute-start.6
  20.8 0.7 collective-permute-done.7.refs_2_
  21.5 1.3 collective-permute-start.8
  22.8 3.7 %collective-permute-start.10 = (bf16[256,1024]{1,0:T(8,128)(2,1)S(1)}, bf16[256,1024]{1,0:T(8,128)(2,1)S(1)}, u32[]{:S(2)}, u32[]{:S(2)}) collective-permute-start(bf16[256,1024]{1,0:T(8,128)(2,1)S(1)} %get-tuple-element.31), channel_id=1, source_target_pairs={{0,24},{4,12},{8,0},{12,20},{16,8},{20,28},{24,16},{28,4},{1,25},{... | collective-permute-start | bytes 1572872 | tf_op jit(solution)/shard_map/ppermute | solution.py:211
  26.5 0.0 collective-permute-done.6.refs_1_
  26.5 0.0 collective-permute-done.8.refs_3_
  26.5 1.6 %shard_map.65 = (bf16[256,1024]{1,0:T(8,128)(2,1)S(1)}, bf16[256,1024]{1,0:T(8,128)(2,1)S(1)}) custom-call(bf16[144,1024]{1,0:T(8,128)(2,1)S(1)} %pad_maximum_fusion.1.refs_0_, bf16[144,1024]{1,0:T(8,128)(2,1)S(1)} %collective-permute-done.6.refs_1_, bf16[144,1024]{1,0:T(8,128)(2,1)S(1)} %collective-permute-done.7.refs_2_, ...), custom_call_target="tpu_custom_call" | custom-call | flops 536870912 | bytes 2490368 | tf_op jit(solution)/shard_map/pallas_call | solution.py:133
  28.2 2.8 %collective-permute-done.5 = bf16[256,1024]{1,0:T(8,128)(2,1)S(1)} collective-permute-done((bf16[256,1024]{1,0:T(8,128)(2,1)S(1)}, bf16[256,1024]{1,0:T(8,128)(2,1)S(1)}, u32[]{:S(2)}, u32[]{:S(2)}) %collective-permute-start.5) | collective-permute-done | bytes 524320 | tf_op jit(solution)/shard_map/ppermute | solution.py:211
  31.0 0.1 broadcast_select_fusion.1
  31.1 1.4 collective-permute-start.9
  32.5 9.8 %collective-permute-done.10 = bf16[256,1024]{1,0:T(8,128)(2,1)S(1)} collective-permute-done((bf16[256,1024]{1,0:T(8,128)(2,1)S(1)}, bf16[256,1024]{1,0:T(8,128)(2,1)S(1)}, u32[]{:S(2)}, u32[]{:S(2)}) %collective-permute-start.10) | collective-permute-done | bytes 524320 | tf_op jit(solution)/shard_map/ppermute | solution.py:211
  42.3 0.1 broadcast_select_fusion
  42.3 1.4 collective-permute-start.11
  43.7 0.0 collective-permute-done.9.refs_3_
  43.7 0.4 add_convert_fusion.2
  44.1 4.8 %collective-permute-start.12 = (bf16[256,1024]{1,0:T(8,128)(2,1)S(1)}, bf16[256,1024]{1,0:T(8,128)(2,1)S(1)}, u32[]{:S(2)}, u32[]{:S(2)}) collective-permute-start(bf16[256,1024]{1,0:T(8,128)(2,1)S(1)} %add_convert_fusion.2), channel_id=1, source_target_pairs={{1,16},{16,1},{3,18},{18,3},{5,20},{20,5},{7,22},{22,7},{9,24},{24... | collective-permute-start | bytes 1572872 | tf_op jit(solution)/shard_map/ppermute | solution.py:234
  48.9 5.7 %collective-permute-done.11.refs_4_ = bf16[256,1024]{1,0:T(8,128)(2,1)S(1)} collective-permute-done((bf16[256,1024]{1,0:T(8,128)(2,1)S(1)}, bf16[256,1024]{1,0:T(8,128)(2,1)S(1)}, u32[]{:S(2)}, u32[]{:S(2)}) %collective-permute-start.11) | collective-permute-done | bytes 524320 | tf_op jit(solution)/shard_map/ppermute | solution.py:224
  54.6 0.4 add_convert_fusion.1
  55.0 6.4 %collective-permute-done.12.refs_1_ = bf16[256,1024]{1,0:T(8,128)(2,1)S(1)} collective-permute-done((bf16[256,1024]{1,0:T(8,128)(2,1)S(1)}, bf16[256,1024]{1,0:T(8,128)(2,1)S(1)}, u32[]{:S(2)}, u32[]{:S(2)}) %collective-permute-start.12) | collective-permute-done | bytes 524320 | tf_op jit(solution)/shard_map/ppermute | solution.py:234
  61.4 1.9 %collective-permute-start.13 = (bf16[256,1024]{1,0:T(8,128)(2,1)S(1)}, bf16[256,1024]{1,0:T(8,128)(2,1)S(1)}, u32[]{:S(2)}, u32[]{:S(2)}) collective-permute-start(bf16[256,1024]{1,0:T(8,128)(2,1)S(1)} %add_convert_fusion.1), channel_id=1, source_target_pairs={{1,16},{16,1},{3,18},{18,3},{5,20},{20,5},{7,22},{22,7},{9,24},{24... | collective-permute-start | bytes 1572872 | tf_op jit(solution)/shard_map/ppermute | solution.py:234
  63.3 3.9 %collective-permute-start.16 = (bf16[256,1024]{1,0:T(8,128)(2,1)S(1)}, bf16[256,1024]{1,0:T(8,128)(2,1)S(1)}, u32[]{:S(2)}, u32[]{:S(2)}) collective-permute-start(bf16[256,1024]{1,0:T(8,128)(2,1)S(1)} %collective-permute-done.12.refs_1_), channel_id=1, source_target_pairs={{0,8},{4,12},{8,0},{12,4},{16,24},{20,28},{24,16},{28,20},{1,9},{5... | collective-permute-start | bytes 1572872 | tf_op jit(solution)/shard_map/ppermute | solution.py:239
  67.2 0.0 copy-done.2
  67.2 4.1 %shard_map.66 = bf16[512,1024]{1,0:T(8,128)(2,1)S(1)} custom-call(bf16[512,1024]{1,0:T(8,128)(2,1)S(1)} %bitcast.27, bf16[256,1024]{1,0:T(8,128)(2,1)S(1)} %get-tuple-element.24.refs_1_, bf16[256,1024]{1,0:T(8,128)(2,1)S(1)} %get-tuple-element.25.refs_2_, bf16[256,1024]{1,0:T(8,128)(2,1)S(1)} %collective-permute-done.9.refs_3_, ...), custom_call_target="tpu_custom_call" | custom-call | flops 2684354560 | bytes 5242880 | tf_op jit(solution)/shard_map/pallas_call | solution.py:133
  71.4 7.2 %collective-permute-done.13.refs_2_ = bf16[256,1024]{1,0:T(8,128)(2,1)S(1)} collective-permute-done((bf16[256,1024]{1,0:T(8,128)(2,1)S(1)}, bf16[256,1024]{1,0:T(8,128)(2,1)S(1)}, u32[]{:S(2)}, u32[]{:S(2)}) %collective-permute-start.13) | collective-permute-done | bytes 524320 | tf_op jit(solution)/shard_map/ppermute | solution.py:234
  78.5 3.5 %collective-permute-done.16.refs_3_ = bf16[256,1024]{1,0:T(8,128)(2,1)S(1)} collective-permute-done((bf16[256,1024]{1,0:T(8,128)(2,1)S(1)}, bf16[256,1024]{1,0:T(8,128)(2,1)S(1)}, u32[]{:S(2)}, u32[]{:S(2)}) %collective-permute-start.16) | collective-permute-done | bytes 524320 | tf_op jit(solution)/shard_map/ppermute | solution.py:239
  82.0 1.7 %collective-permute-start.17 = (bf16[256,1024]{1,0:T(8,128)(2,1)S(1)}, bf16[256,1024]{1,0:T(8,128)(2,1)S(1)}, u32[]{:S(2)}, u32[]{:S(2)}) collective-permute-start(bf16[256,1024]{1,0:T(8,128)(2,1)S(1)} %collective-permute-done.13.refs_2_), channel_id=1, source_target_pairs={{0,8},{4,12},{8,0},{12,4},{16,24},{20,28},{24,16},{28,20},{1,9},{5... | collective-permute-start | bytes 1572872 | tf_op jit(solution)/shard_map/ppermute | solution.py:252
  83.7 1.3 collective-permute-start.14
  85.0 0.1 collective-permute-start.18
  85.1 11.3 %collective-permute-done.17.refs_4_ = bf16[256,1024]{1,0:T(8,128)(2,1)S(1)} collective-permute-done((bf16[256,1024]{1,0:T(8,128)(2,1)S(1)}, bf16[256,1024]{1,0:T(8,128)(2,1)S(1)}, u32[]{:S(2)}, u32[]{:S(2)}) %collective-permute-start.17) | collective-permute-done | bytes 524320 | tf_op jit(solution)/shard_map/ppermute | solution.py:252
  96.4 0.0 collective-permute-start.19
  96.4 0.0 collective-permute-done.18.refs_5_
  96.4 1.9 %collective-permute-done.19.refs_6_ = bf16[256,1024]{1,0:T(8,128)(2,1)S(1)} collective-permute-done((bf16[256,1024]{1,0:T(8,128)(2,1)S(1)}, bf16[256,1024]{1,0:T(8,128)(2,1)S(1)}, u32[]{:S(2)}, u32[]{:S(2)}) %collective-permute-start.19) | collective-permute-done | bytes 524320 | tf_op jit(solution)/shard_map/ppermute | solution.py:253
  98.3 4.3 %shard_map.67 = bf16[512,1024]{1,0:T(8,128)(2,1)S(1)} custom-call(s32[8,128]{1,0:T(8,128)S(1)} %broadcast_in_dim.6.refs_0_, bf16[256,1024]{1,0:T(8,128)(2,1)S(1)} %collective-permute-done.12.refs_1_, bf16[256,1024]{1,0:T(8,128)(2,1)S(1)} %collective-permute-done.13.refs_2_, bf16[256,1024]{1,0:T(8,128)(2,1)S(1)} %collective-permute-done.16.refs_3_, ...), custom_call_target="tpu_custom_call" | custom-call | flops 2684354560 | bytes 4198400 | tf_op jit(solution)/shard_map/pallas_call | solution.py:133
  102.6 0.2 collective-permute-start.20
  102.8 0.0 collective-permute-done.14
  102.8 0.4 add_convert_fusion
  103.2 1.3 collective-permute-start.15
  104.5 0.8 collective-permute-done.20
  105.3 10.3 %collective-permute-done.15 = bf16[512,1024]{1,0:T(8,128)(2,1)} collective-permute-done((bf16[512,1024]{1,0:T(8,128)(2,1)S(1)}, bf16[512,1024]{1,0:T(8,128)(2,1)}, u32[]{:S(2)}, u32[]{:S(2)}) %collective-permute-start.15) | collective-permute-done | bytes 1048608 | tf_op jit(solution)/shard_map/ppermute | solution.py:258
  115.6 2.2 %fusion.6 = bf16[1,1,512,1024]{3,2,1,0:T(8,128)(2,1)S(1)} fusion(bf16[512,1024]{1,0:T(8,128)(2,1)S(1)} %collective-permute-done.20, bf16[512,1024]{1,0:T(8,128)(2,1)S(1)} %shard_map.67, bf16[512,1024]{1,0:T(8,128)(2,1)} %collective-permute-done.15, bf16[512,1024]{1,0:T(8,128)(2,1)S(1)} %add_convert_fusion, pred[]{:T(512)S(6)} %eq.39), kind=kLoop, calls=%fused_computation.12 | loop fusion | flops 4718592 | bytes 5242881 | tf_op jit(solution)/shard_map/broadcast_in_dim | solution.py:267
  117.7 2.2 %collective-permute-start.21 = (bf16[1,1,512,1024]{3,2,1,0:T(8,128)(2,1)S(1)}, bf16[1,1,512,1024]{3,2,1,0:T(8,128)(2,1)S(1)}, u32[]{:S(2)}, u32[]{:S(2)}) collective-permute-start(bf16[1,1,512,1024]{3,2,1,0:T(8,128)(2,1)S(1)} %fusion.6), channel_id=1, source_target_pairs={{1,16},{16,1},{3,18},{18,3},{5,20},{20,5},{7,22},{22,7},{9,24},{24... | collective-permute-start | bytes 3145736 | tf_op jit(solution)/shard_map/ppermute | solution.py:267
  119.9 23.3 %collective-permute-done.21 = bf16[1,1,512,1024]{3,2,1,0:T(8,128)(2,1)S(1)} collective-permute-done((bf16[1,1,512,1024]{3,2,1,0:T(8,128)(2,1)S(1)}, bf16[1,1,512,1024]{3,2,1,0:T(8,128)(2,1)S(1)}, u32[]{:S(2)}, u32[]{:S(2)}) %collective-permute-start.21) | collective-permute-done | bytes 1048608 | tf_op jit(solution)/shard_map/ppermute | solution.py:267
  143.2 1.0 copy.10
  (6 shorter events, 0.1 us)
Async XLA Ops:
  0.0 4.1 %copy-start.3 = (s32[1,2]{1,0:T(1,128)S(1)}, s32[1,2]{1,0:T(1,128)}, u32[]{:S(2)}) copy-start(s32[1,2]{1,0:T(1,128)} %param.11) | copy-start | bytes 28
  0.7 14.1 %copy-start = (bf16[1,1,512,1024]{3,2,1,0:T(8,128)(2,1)S(1)}, bf16[1,1,512,1024]{3,2,1,0:T(8,128)(2,1)}, u32[]{:S(2)}) copy-start(bf16[1,1,512,1024]{3,2,1,0:T(8,128)(2,1)} %param.10) | copy-start | bytes 3145732
  0.7 14.1 %copy-start.1 = (bf16[2,1,1,256,512]{4,3,2,1,0:T(8,128)(2,1)S(1)}, bf16[2,1,1,256,512]{4,3,2,1,0:T(8,128)(2,1)}, u32[]{:S(2)}) copy-start(bf16[2,1,1,256,512]{4,3,2,1,0:T(8,128)(2,1)} %param.8) | copy-start | bytes 1572868
  1.9 11.2 %collective-permute-start.1 = (bf16[144,1024]{1,0:T(8,128)(2,1)S(1)}, bf16[144,1024]{1,0:T(8,128)(2,1)S(1)}, u32[]{:S(2)}, u32[]{:S(2)}) collective-permute-start(bf16[144,1024]{1,0:T(8,128)(2,1)S(1)} %pad_maximum_fusion.refs_0_), channel_id=1, source_target_pairs={{0,2},{1,3},{2,0},{3,1},{4,6},{5,7},{6,4},{7,5},{8,10},{9,11},{10,... | collective-permute-start | bytes 884744 | tf_op jit(solution)/shard_map/ppermute | solution.py:196
  4.1 9.0 %collective-permute-start.2 = (s32[2]{0:T(128)S(1)}, s32[2]{0:T(128)S(1)}, u32[]{:S(2)}, u32[]{:S(2)}) collective-permute-start(s32[2]{0:T(128)S(1)} %bitcast.31), channel_id=1, source_target_pairs={{0,4},{4,0},{8,12},{12,8},{16,20},{20,16},{24,28},{28,24},{1,5},{5... | collective-permute-start | bytes 32 | tf_op jit(solution)/shard_map/ppermute | solution.py:177
  5.3 6.5 %collective-permute-start.3 = (s32[2]{0:T(128)S(1)}, s32[2]{0:T(128)S(1)}, u32[]{:S(2)}, u32[]{:S(2)}) collective-permute-start(s32[2]{0:T(128)S(1)} %bitcast.32), channel_id=1, source_target_pairs={{1,16},{16,1},{3,18},{18,3},{5,20},{20,5},{7,22},{22,7},{9,24},{24... | collective-permute-start | bytes 32 | tf_op jit(solution)/shard_map/ppermute | solution.py:178
  10.6 3.0 %collective-permute-start = (bf16[144,1024]{1,0:T(8,128)(2,1)S(1)}, bf16[144,1024]{1,0:T(8,128)(2,1)S(1)}, u32[]{:S(2)}, u32[]{:S(2)}) collective-permute-start(bf16[144,1024]{1,0:T(8,128)(2,1)S(1)} %pad_maximum_fusion.refs_0_), channel_id=1, source_target_pairs={{0,1},{1,0},{2,3},{3,2},{4,5},{5,4},{6,7},{7,6},{8,9},{9,8},{10,11... | collective-permute-start | bytes 884744 | tf_op jit(solution)/shard_map/ppermute | solution.py:196
  13.2 1.6 %collective-permute-start.4 = (bf16[144,1024]{1,0:T(8,128)(2,1)S(1)}, bf16[144,1024]{1,0:T(8,128)(2,1)S(1)}, u32[]{:S(2)}, u32[]{:S(2)}) collective-permute-start(bf16[144,1024]{1,0:T(8,128)(2,1)S(1)} %collective-permute-done.1.refs_2_), channel_id=1, source_target_pairs={{0,1},{1,0},{2,3},{3,2},{4,5},{5,4},{6,7},{7,6},{8,9},{9,8},{10,11... | collective-permute-start | bytes 884744 | tf_op jit(solution)/shard_map/ppermute | solution.py:196
  13.3 8.2 %collective-permute-start.7 = (bf16[144,1024]{1,0:T(8,128)(2,1)S(1)}, bf16[144,1024]{1,0:T(8,128)(2,1)S(1)}, u32[]{:S(2)}, u32[]{:S(2)}) collective-permute-start(bf16[144,1024]{1,0:T(8,128)(2,1)S(1)} %pad_maximum_fusion.1.refs_0_), channel_id=1, source_target_pairs={{0,2},{1,3},{2,0},{3,1},{4,6},{5,7},{6,4},{7,5},{8,10},{9,11},{10,... | collective-permute-start | bytes 884744 | tf_op jit(solution)/shard_map/ppermute | solution.py:196
  16.7 14.4 %collective-permute-start.5 = (bf16[256,1024]{1,0:T(8,128)(2,1)S(1)}, bf16[256,1024]{1,0:T(8,128)(2,1)S(1)}, u32[]{:S(2)}, u32[]{:S(2)}) collective-permute-start(bf16[256,1024]{1,0:T(8,128)(2,1)S(1)} %get-tuple-element.27), channel_id=1, source_target_pairs={{0,24},{4,12},{8,0},{12,20},{16,8},{20,28},{24,16},{28,4},{1,25},{... | collective-permute-start | bytes 1572872 | tf_op jit(solution)/shard_map/ppermute | solution.py:211
  20.1 6.4 %collective-permute-start.6 = (bf16[144,1024]{1,0:T(8,128)(2,1)S(1)}, bf16[144,1024]{1,0:T(8,128)(2,1)S(1)}, u32[]{:S(2)}, u32[]{:S(2)}) collective-permute-start(bf16[144,1024]{1,0:T(8,128)(2,1)S(1)} %pad_maximum_fusion.1.refs_0_), channel_id=1, source_target_pairs={{0,1},{1,0},{2,3},{3,2},{4,5},{5,4},{6,7},{7,6},{8,9},{9,8},{10,11... | collective-permute-start | bytes 884744 | tf_op jit(solution)/shard_map/ppermute | solution.py:196
  21.5 5.1 %collective-permute-start.8 = (bf16[144,1024]{1,0:T(8,128)(2,1)S(1)}, bf16[144,1024]{1,0:T(8,128)(2,1)S(1)}, u32[]{:S(2)}, u32[]{:S(2)}) collective-permute-start(bf16[144,1024]{1,0:T(8,128)(2,1)S(1)} %collective-permute-done.7.refs_2_), channel_id=1, source_target_pairs={{0,1},{1,0},{2,3},{3,2},{4,5},{5,4},{6,7},{7,6},{8,9},{9,8},{10,11... | collective-permute-start | bytes 884744 | tf_op jit(solution)/shard_map/ppermute | solution.py:196
  22.8 19.5 %collective-permute-start.10 = (bf16[256,1024]{1,0:T(8,128)(2,1)S(1)}, bf16[256,1024]{1,0:T(8,128)(2,1)S(1)}, u32[]{:S(2)}, u32[]{:S(2)}) collective-permute-start(bf16[256,1024]{1,0:T(8,128)(2,1)S(1)} %get-tuple-element.31), channel_id=1, source_target_pairs={{0,24},{4,12},{8,0},{12,20},{16,8},{20,28},{24,16},{28,4},{1,25},{... | collective-permute-start | bytes 1572872 | tf_op jit(solution)/shard_map/ppermute | solution.py:211
  31.1 12.6 %collective-permute-start.9 = (bf16[256,1024]{1,0:T(8,128)(2,1)S(1)}, bf16[256,1024]{1,0:T(8,128)(2,1)S(1)}, u32[]{:S(2)}, u32[]{:S(2)}) collective-permute-start(bf16[256,1024]{1,0:T(8,128)(2,1)S(1)} %broadcast_select_fusion.1), channel_id=1, source_target_pairs={{0,4},{4,0},{8,12},{12,8},{16,20},{20,16},{24,28},{28,24},{1,5},{5... | collective-permute-start | bytes 1572872 | tf_op jit(solution)/shard_map/ppermute | solution.py:224
  42.3 12.3 %collective-permute-start.11 = (bf16[256,1024]{1,0:T(8,128)(2,1)S(1)}, bf16[256,1024]{1,0:T(8,128)(2,1)S(1)}, u32[]{:S(2)}, u32[]{:S(2)}) collective-permute-start(bf16[256,1024]{1,0:T(8,128)(2,1)S(1)} %broadcast_select_fusion), channel_id=1, source_target_pairs={{0,4},{4,0},{8,12},{12,8},{16,20},{20,16},{24,28},{28,24},{1,5},{5... | collective-permute-start | bytes 1572872 | tf_op jit(solution)/shard_map/ppermute | solution.py:224
  44.1 17.3 %collective-permute-start.12 = (bf16[256,1024]{1,0:T(8,128)(2,1)S(1)}, bf16[256,1024]{1,0:T(8,128)(2,1)S(1)}, u32[]{:S(2)}, u32[]{:S(2)}) collective-permute-start(bf16[256,1024]{1,0:T(8,128)(2,1)S(1)} %add_convert_fusion.2), channel_id=1, source_target_pairs={{1,16},{16,1},{3,18},{18,3},{5,20},{20,5},{7,22},{22,7},{9,24},{24... | collective-permute-start | bytes 1572872 | tf_op jit(solution)/shard_map/ppermute | solution.py:234
  54.6 12.6 %copy-start.2 = (bf16[1,1,512,1024]{3,2,1,0:T(8,128)(2,1)S(1)}, bf16[1,1,512,1024]{3,2,1,0:T(8,128)(2,1)}, u32[]{:S(2)}) copy-start(bf16[1,1,512,1024]{3,2,1,0:T(8,128)(2,1)} %param.9) | copy-start | bytes 3145732
  61.4 17.1 %collective-permute-start.13 = (bf16[256,1024]{1,0:T(8,128)(2,1)S(1)}, bf16[256,1024]{1,0:T(8,128)(2,1)S(1)}, u32[]{:S(2)}, u32[]{:S(2)}) collective-permute-start(bf16[256,1024]{1,0:T(8,128)(2,1)S(1)} %add_convert_fusion.1), channel_id=1, source_target_pairs={{1,16},{16,1},{3,18},{18,3},{5,20},{20,5},{7,22},{22,7},{9,24},{24... | collective-permute-start | bytes 1572872 | tf_op jit(solution)/shard_map/ppermute | solution.py:234
  63.3 18.6 %collective-permute-start.16 = (bf16[256,1024]{1,0:T(8,128)(2,1)S(1)}, bf16[256,1024]{1,0:T(8,128)(2,1)S(1)}, u32[]{:S(2)}, u32[]{:S(2)}) collective-permute-start(bf16[256,1024]{1,0:T(8,128)(2,1)S(1)} %collective-permute-done.12.refs_1_), channel_id=1, source_target_pairs={{0,8},{4,12},{8,0},{12,4},{16,24},{20,28},{24,16},{28,20},{1,9},{5... | collective-permute-start | bytes 1572872 | tf_op jit(solution)/shard_map/ppermute | solution.py:239
  82.0 14.4 %collective-permute-start.17 = (bf16[256,1024]{1,0:T(8,128)(2,1)S(1)}, bf16[256,1024]{1,0:T(8,128)(2,1)S(1)}, u32[]{:S(2)}, u32[]{:S(2)}) collective-permute-start(bf16[256,1024]{1,0:T(8,128)(2,1)S(1)} %collective-permute-done.13.refs_2_), channel_id=1, source_target_pairs={{0,8},{4,12},{8,0},{12,4},{16,24},{20,28},{24,16},{28,20},{1,9},{5... | collective-permute-start | bytes 1572872 | tf_op jit(solution)/shard_map/ppermute | solution.py:252
  83.7 19.1 %collective-permute-start.14 = (bf16[512,1024]{1,0:T(8,128)(2,1)S(1)}, bf16[512,1024]{1,0:T(8,128)(2,1)S(1)}, u32[]{:S(2)}, u32[]{:S(2)}) collective-permute-start(bf16[512,1024]{1,0:T(8,128)(2,1)S(1)} %shard_map.66), channel_id=1, source_target_pairs={{16,0},{1,17},{18,2},{3,19},{20,4},{5,21},{22,6},{7,23},{24,8},{9,... | collective-permute-start | bytes 3145736 | tf_op jit(solution)/shard_map/ppermute | solution.py:254
  85.0 11.4 %collective-permute-start.18 = (bf16[256,1024]{1,0:T(8,128)(2,1)S(1)}, bf16[256,1024]{1,0:T(8,128)(2,1)S(1)}, u32[]{:S(2)}, u32[]{:S(2)}) collective-permute-start(bf16[256,1024]{1,0:T(8,128)(2,1)S(1)} %collective-permute-done.16.refs_3_), channel_id=1, source_target_pairs={{0,1},{1,0},{2,3},{3,2},{4,5},{5,4},{6,7},{7,6},{8,9},{9,8},{10,11... | collective-permute-start | bytes 1572872 | tf_op jit(solution)/shard_map/ppermute | solution.py:253
  96.4 1.9 %collective-permute-start.19 = (bf16[256,1024]{1,0:T(8,128)(2,1)S(1)}, bf16[256,1024]{1,0:T(8,128)(2,1)S(1)}, u32[]{:S(2)}, u32[]{:S(2)}) collective-permute-start(bf16[256,1024]{1,0:T(8,128)(2,1)S(1)} %collective-permute-done.17.refs_4_), channel_id=1, source_target_pairs={{0,1},{1,0},{2,3},{3,2},{4,5},{5,4},{6,7},{7,6},{8,9},{9,8},{10,11... | collective-permute-start | bytes 1572872 | tf_op jit(solution)/shard_map/ppermute | solution.py:253
  102.6 2.7 %collective-permute-start.20 = (bf16[512,1024]{1,0:T(8,128)(2,1)S(1)}, bf16[512,1024]{1,0:T(8,128)(2,1)S(1)}, u32[]{:S(2)}, u32[]{:S(2)}) collective-permute-start(bf16[512,1024]{1,0:T(8,128)(2,1)S(1)} %shard_map.67), channel_id=1, source_target_pairs={{0,1},{1,0},{2,3},{3,2},{4,5},{5,4},{6,7},{7,6},{8,9},{9,8},{10,11... | collective-permute-start | bytes 3145736 | tf_op jit(solution)/shard_map/ppermute | solution.py:263
  103.2 12.4 %collective-permute-start.15 = (bf16[512,1024]{1,0:T(8,128)(2,1)S(1)}, bf16[512,1024]{1,0:T(8,128)(2,1)}, u32[]{:S(2)}, u32[]{:S(2)}) collective-permute-start(bf16[512,1024]{1,0:T(8,128)(2,1)S(1)} %add_convert_fusion), channel_id=1, source_target_pairs={{0,1},{17,16},{2,3},{19,18},{4,5},{21,20},{6,7},{23,22},{8,9},{25,... | collective-permute-start | bytes 3145736 | tf_op jit(solution)/shard_map/ppermute | solution.py:258
  117.7 25.4 %collective-permute-start.21 = (bf16[1,1,512,1024]{3,2,1,0:T(8,128)(2,1)S(1)}, bf16[1,1,512,1024]{3,2,1,0:T(8,128)(2,1)S(1)}, u32[]{:S(2)}, u32[]{:S(2)}) collective-permute-start(bf16[1,1,512,1024]{3,2,1,0:T(8,128)(2,1)S(1)} %fusion.6), channel_id=1, source_target_pairs={{1,16},{16,1},{3,18},{18,3},{5,20},{20,5},{7,22},{22,7},{9,24},{24... | collective-permute-start | bytes 3145736 | tf_op jit(solution)/shard_map/ppermute | solution.py:267

commit v3 on v2

--- a/solution.py
+++ b/solution.py
@@ -10,9 +10,11 @@
 
 NS_ITERS = 2
 CHUNKS = 2
+BLOCKS = 2
 SERIAL_X = False
 LAG_X = 9
-SERIAL_T = True
+LAG_S = 9
+SERIAL_T = False
 LAG_T = 9
 SERIAL_W = True
 NS_AFTER = 0
@@ -52,10 +54,11 @@
 def first_step_kernel(chunks, *refs):
     offset, grads, partners = refs[0], refs[1 : 1 + chunks], refs[1 + chunks : 1 + 2 * chunks]
     weight, moved = refs[1 + 2 * chunks :]
-    rows = grads[0].shape[0]
-    tracked = []
+    start, tracked = 0, []
     for k in range(chunks):
-        own = offset[k * rows : (k + 1) * rows, :].astype(jnp.float32) + grads[k][...].astype(jnp.float32)
+        part = slice(start, start + grads[k].shape[0])
+        start = part.stop
+        own = offset[part, :].astype(jnp.float32) + grads[k][...].astype(jnp.float32)
         tracked.append(0.5 * (own + partners[k][...].astype(jnp.float32)))
     ortho = newton_schulz(normalized(tracked))
     moved[...] = (
@@ -63,15 +66,36 @@
     ).astype(moved.dtype)
 
 
-def second_step_kernel(chunks, flag, *refs):
+def second_step_kernel(chunks, bits, *refs):
     own, same, other = refs[:chunks], refs[chunks : 2 * chunks], refs[2 * chunks : 3 * chunks]
-    (ortho,) = refs[3 * chunks :]
-    use_same = flag[0:1, 0:1] == 1
+    blocks = refs[3 * chunks :]
+    sites, site, core = lax.axis_size("site"), lax.axis_index("site"), lax.axis_index("expert") % 2
+    half = sites // 2
+    problem, source = site % half + half * core, (site + half - 2) % half + half * core
+    ahead_same = ((problem + 2) % sites == source).astype(jnp.int32)
+    use_same = bits[0:1, 1:2] == ahead_same
     tracked = []
     for k in range(chunks):
         partner = jnp.where(use_same, same[k][...].astype(jnp.float32), other[k][...].astype(jnp.float32))
         tracked.append(0.5 * (own[k][...].astype(jnp.float32) + partner))
-    ortho[...] = newton_schulz(normalized(tracked))
+    ortho = newton_schulz(normalized(tracked))
+    rows = blocks[0].shape[0]
+    for k, block in enumerate(blocks):
+        block[...] = ortho[k * rows : (k + 1) * rows, :]
+
+
+def last_kernel(blocks, ready, *refs):
+    back, out, buffer, semaphores = refs[:blocks], *refs[blocks:]
+    rows = back[0].shape[0]
+    copies = []
+    for k in range(blocks):
+        part = pl.ds(k * rows, rows)
+        value = ready[part, :].astype(jnp.float32) + 0.5 * back[k][...].astype(jnp.float32)
+        buffer[part, :] = value.astype(buffer.dtype)
+        copies.append(pltpu.make_async_copy(buffer.at[part], out.at[0, 0, part], semaphores.at[k]))
+        copies[-1].start()
+    for copy in copies:
+        copy.wait()
 
 
 def gradient_kernel(sources, with_sum, *refs):
@@ -101,11 +125,13 @@
         offset, refs = refs[0], refs[1:]
         summed = (offset[...].astype(jnp.float32) + grad.astype(jnp.float32)).astype(jnp.bfloat16)
         refs, sums = refs[: len(refs) // 2], refs[len(refs) // 2 :]
-    depth = refs[0].shape[0]
+    start = 0
     for k, out in enumerate(refs):
-        out[...] = grad[k * depth : (k + 1) * depth, :]
+        part = slice(start, start + out.shape[0])
+        start = part.stop
+        out[...] = grad[part, :]
         if with_sum:
-            sums[k][...] = summed[k * depth : (k + 1) * depth, :]
+            sums[k][...] = summed[part, :]
 
 
 def call(kernel, operands, out_shapes, flops):
@@ -152,14 +178,15 @@
     site, expert = lax.axis_index("site"), lax.axis_index("expert")
     both = ("site", "expert")
 
-    cross, kept, from_mate, lent = [], [], [], []
+    cross, kept, to_mate, lent, returned = [], [], [], [], []
     for s in range(half):
         for e in range(0, experts, 2):
             low, high = s * experts + e, (s + half) * experts + e
             cross += [(low + 1, high), (high, low + 1)]
             kept += [(low, low), (high + 1, high + 1)]
-            from_mate += [(low, low + 1), (high + 1, high)]
+            to_mate += [(low + 1, low), (high, high + 1)]
             lent += [(high, low), (low + 1, high + 1)]
+            returned += [(low, high), (high + 1, low + 1)]
     swap = cross + kept
     mates = [(e, e ^ 1) for e in range(experts)]
     beside = [(s, s ^ 1) for s in range(sites)]
@@ -176,11 +203,8 @@
 
     beside_bits = lax.ppermute(bits, "site", beside)
     swap_bits = lax.ppermute(bits, both, swap)
-    send_own = jnp.where(site % 2 == 1, beside_bits[0] == 1, beside_bits[0] == 0)
-    problem = site % half + half * (expert % 2)
-    wanted = jnp.where(swap_bits[1] == 1, problem + 2, problem - 2 + sites) % sites
-    use_same = wanted == (site + half - 2) % half + half * (expert % 2)
-    use_same = jnp.full((8, 128), use_same.astype(jnp.int32))
+    send_own = beside_bits.reshape(1, -1)[:, 0:1] == site % 2
+    swap_bits = swap_bits.reshape(1, -1)
 
     count = tokens.shape[1]
     named = routing.astype(jnp.bfloat16).reshape(steps, 1, count)
@@ -195,14 +219,14 @@
             hop = [(e, e ^ level) for e in range(experts)]
             gathered[k].update({j ^ level: lax.ppermute(t, "expert", hop) for j, t in gathered[k].items()})
             if k == 0 and level == top:
-                gathered[k][top], (send_own, use_same) = lax.optimization_barrier(
-                    (gathered[k][top], (send_own, use_same))
+                gathered[k][top], (send_own, swap_bits) = lax.optimization_barrier(
+                    (gathered[k][top], (send_own, swap_bits))
                 )
             level //= 2
 
-    rows = fan_rows // CHUNKS
-    parts = [slice(i * rows, (i + 1) * rows) for i in range(CHUNKS)]
-    chunk = [jax.ShapeDtypeStruct((rows, features), jnp.bfloat16)] * CHUNKS
+    edges = [fan_rows // 16 * i // CHUNKS * 16 for i in range(CHUNKS)] + [fan_rows]
+    parts = [slice(low, high) for low, high in zip(edges, edges[1:])]
+    chunk = [jax.ShapeDtypeStruct((p.stop - p.start, features), jnp.bfloat16) for p in parts]
     whole = [jax.ShapeDtypeStruct((fan_rows, features), jnp.bfloat16)]
     cost = 2 * fan_rows * features * experts * count
     operands = [gathered[0][j] for j in range(experts)] + [(stashed, 0), (offset, None)]
@@ -219,6 +243,8 @@
     for i in range(CHUNKS):
         if i > 0:
             chosen[i] = after(chosen[i], partners[i - 1]) if SERIAL_X else chosen[i]
+        if i >= LAG_S:
+            chosen[i] = after(chosen[i], second[i - LAG_S])
         if i >= LAG_X:
             chosen[i] = after(chosen[i], mine[i - LAG_X])
         partners.append(lax.ppermute(chosen[i], "site", beside))
@@ -254,17 +280,30 @@
     borrowed = lax.ppermute(after(moved, mine[-1]), both, lent)
     if GATE:
         other[-1] = after(other[-1], borrowed)
-    shared = (moved.astype(jnp.float32) + borrowed.astype(jnp.float32)).astype(jnp.bfloat16)
-    given = lax.ppermute(shared, both, from_mate)
-    shared = jnp.where(is_swapped, given, shared)
-    (ortho,) = call(
-        functools.partial(second_step_kernel, CHUNKS), [use_same, *mine, *same, *other], whole, cost
-    )
-    paired_ortho = lax.ppermute(ortho, "expert", mates)
-    result = 0.5 * shared.astype(jnp.float32) - 0.5 * step_scale * (
-        ortho.astype(jnp.float32) + paired_ortho.astype(jnp.float32)
-    )
-    return lax.ppermute(result.astype(jnp.bfloat16)[None, None], both, swap)
+    block_rows = fan_rows // BLOCKS
+    block = [jax.ShapeDtypeStruct((block_rows, features), jnp.bfloat16)] * BLOCKS
+    ortho = list(call(functools.partial(second_step_kernel, CHUNKS), [swap_bits, *mine, *same, *other], block, cost))
+    ortho[0] = after(ortho[0], borrowed)
+    paired_ortho = [lax.ppermute(o, both, to_mate) for o in ortho]
+    sent = []
+    for i in range(BLOCKS):
+        part = moved[i * block_rows : (i + 1) * block_rows].astype(jnp.float32)
+        met = paired_ortho[i] if i == 0 else after(paired_ortho[i], sent[i - 1])
+        sent.append(
+            (part - step_scale * (ortho[i].astype(jnp.float32) + met.astype(jnp.float32))).astype(jnp.bfloat16)
+        )
+    back = [lax.ppermute(x, both, returned) for x in sent]
+    halves = jnp.where(is_swapped, moved, jnp.concatenate(sent, axis=0)).astype(jnp.float32)
+    ready = 0.5 * jnp.where(is_swapped, halves, halves + borrowed.astype(jnp.float32))
+    return pl.pallas_call(
+        functools.partial(last_kernel, BLOCKS),
+        in_specs=[VMEM] * (1 + BLOCKS),
+        out_specs=ANY,
+        out_shape=jax.ShapeDtypeStruct((1, 1, fan_rows, features), jnp.bfloat16),
+        scratch_shapes=[pltpu.VMEM((fan_rows, features), jnp.bfloat16), pltpu.SemaphoreType.DMA((BLOCKS,))],
+        compiler_params=pltpu.CompilerParams(vmem_limit_bytes=VMEM_LIMIT),
+        cost_estimate=pl.CostEstimate(flops=0, bytes_accessed=8 * fan_rows * features, transcendentals=0),
+    )(ready.astype(jnp.bfloat16), *back)
 
 
 def from_behind(block, axis, distance):

time: 144 us -> 138 us (0.958)
  waiting for transfers between devices: 86 us -> 75.1 us
  starting transfers between devices: 38.4 us -> 45 us
  local copies, waits for them, and re-layouts: 2.76 us -> 1.22 us
    ppermute x3 -> x4, waiting for transfers between devices: 34.3 us -> 22.3 us  [the longest x2 21.1 us: paired(): back = [lax.ppermute(x, both, returned) for x in sent]]
    ppermute x2, waiting for transfers between devices: 14.8 us -> 22.6 us  [paired(): same.append(lax.ppermute(value, 'site', within))]
    ppermute x2, waiting for transfers between devices: 13.6 us -> 7.53 us  [paired(): mine.append(lax.ppermute(second[i], both, swap))]
    ppermute x3 -> x4, starting transfers between devices: 3.68 us -> 9 us  [the longest x2 6.42 us: paired(): paired_ortho = [lax.ppermute(o, both, to_mate) for o in ortho]]
    ppermute x2, starting transfers between devices: 5.59 us -> 1.4 us  [paired(): same.append(lax.ppermute(value, 'site', within))]
    broadcast_in_dim x1 -> x0, other arithmetic: 2.16 us -> none  [paired(): return lax.ppermute(result.astype(jnp.bfloat16)[None, None], both, swap)]
    convert_element_type x1 -> x3, other arithmetic: 0.4 us -> 2.45 us  [the longest x1 1.9 us: paired(): ready.astype(jnp.bfloat16)]
  transfers between devices with their start and end apart: 22 -> 23, of which waited for: 14 -> 14; matrix products, arithmetic and copies ran while one was open for 1% -> 2% of each run, Pallas kernels for 8% -> 9%
where the time goes in v3:
time: 138 us
  waiting for transfers between devices  75.1 us (54%)
  starting transfers between devices  45 us (33%)
  Pallas kernels  13 us (9%)
  other arithmetic  3.4 us (2%)
    ppermute x2, waiting for transfers between devices, paired(): same.append(lax.ppermute(value, 'site', within))  22.6 us
    ppermute x2, waiting for transfers between devices, paired(): back = [lax.ppermute(x, both, returned) for x in sent]  21.1 us
    ppermute x2, waiting for transfers between devices, paired(): fetched = [lax.ppermute(o, 'site', helpers) for o in own]  12.2 us
    pallas_call x4, Pallas kernels, call(): pl.pallas_call(body, in_specs=[ANY if i in fetched else VMEM for i in ran...  11.9 us
    ppermute x2, starting transfers between devices, paired(): mine.append(lax.ppermute(second[i], both, swap))  8.09 us
    ppermute x2, waiting for transfers between devices, paired(): mine.append(lax.ppermute(second[i], both, swap))  7.53 us
    ppermute x2, starting transfers between devices, paired(): fetched = [lax.ppermute(o, 'site', helpers) for o in own]  6.93 us
    ppermute x2, waiting for transfers between devices, paired(): partners.append(lax.ppermute(chosen[i], 'site', beside))  6.79 us
  transfers between devices with their start and end apart: 23, of which 14 were waited for; matrix products, arithmetic and copies ran while one was open for 2% of the time, Pallas kernels for 9%

profile of v3, /device:TPU:1, one launch (start us, length us, event | category | flops | bytes accessed | tf_op | source)
XLA Modules:
  0.0 138.1 jit_solution(6002818843758825543)
XLA Ops:
  0.0 0.0 copy-start
  0.0 1.2 slice_bitcast_fusion
  1.2 0.0 copy-done.4
  1.3 2.1 %collective-permute-start.1 = (bf16[144,1024]{1,0:T(8,128)(2,1)S(1)}, bf16[144,1024]{1,0:T(8,128)(2,1)S(1)}, u32[]{:S(2)}, u32[]{:S(2)}) collective-permute-start(bf16[144,1024]{1,0:T(8,128)(2,1)S(1)} %pad_maximum_fusion.refs_0_), channel_id=1, source_target_pairs={{0,2},{1,3},{2,0},{3,1},{4,6},{5,7},{6,4},{7,5},{8,10},{9,11},{10,... | collective-permute-start | bytes 884744 | tf_op jit(solution)/shard_map/ppermute | solution.py:220
  3.4 0.0 copy-done.5
  3.4 1.2 collective-permute-start.2
  4.6 5.3 %collective-permute-start.3 = (s32[2]{0:T(128)S(1)}, s32[2]{0:T(128)S(1)}, u32[]{:S(2)}, u32[]{:S(2)}) collective-permute-start(s32[2]{0:T(128)S(1)} %bitcast.32), channel_id=1, source_target_pairs={{1,16},{16,1},{3,18},{18,3},{5,20},{20,5},{7,22},{22,7},{9,24},{24... | collective-permute-start | bytes 32 | tf_op jit(solution)/shard_map/ppermute | solution.py:205
  10.0 0.1 collective-permute-start
  10.0 0.0 collective-permute-done.2
  10.1 1.1 collective-permute-done.3
  11.2 0.0 collective-permute-done.1.refs_2_
  11.2 0.2 collective-permute-start.4
  11.4 1.5 %collective-permute-start.7 = (bf16[144,1024]{1,0:T(8,128)(2,1)S(1)}, bf16[144,1024]{1,0:T(8,128)(2,1)S(1)}, u32[]{:S(2)}, u32[]{:S(2)}) collective-permute-start(bf16[144,1024]{1,0:T(8,128)(2,1)S(1)} %pad_maximum_fusion.1.refs_0_), channel_id=1, source_target_pairs={{0,2},{1,3},{2,0},{3,1},{4,6},{5,7},{6,4},{7,5},{8,10},{9,11},{10,... | collective-permute-start | bytes 884744 | tf_op jit(solution)/shard_map/ppermute | solution.py:220
  12.9 0.0 collective-permute-done.refs_1_
  12.9 0.0 collective-permute-done.4.refs_3_
  12.9 1.8 %shard_map.64 = (bf16[256,1024]{1,0:T(8,128)(2,1)S(1)}, bf16[256,1024]{1,0:T(8,128)(2,1)S(1)}, bf16[256,1024]{1,0:T(8,128)(2,1)S(1)}, bf16[256,1024]{1,0:T(8,128)(2,1)S(1)}) custom-call(bf16[144,1024]{1,0:T(8,128)(2,1)S(1)} %pad_maximum_fusion.refs_0_, bf16[144,1024]{1,0:T(8,128)(2,1)S(1)} %collective-permute-done.refs_1_, ...), custom_call_target="tpu_custom_call" | custom-call | flops 536870912 | bytes 4587520 | tf_op jit(solution)/shard_map/pallas_call | solution.py:159
  14.8 3.4 %collective-permute-start.5 = (bf16[256,1024]{1,0:T(8,128)(2,1)S(1)}, bf16[256,1024]{1,0:T(8,128)(2,1)S(1)}, u32[]{:S(2)}, u32[]{:S(2)}) collective-permute-start(bf16[256,1024]{1,0:T(8,128)(2,1)S(1)} %get-tuple-element.30), channel_id=1, source_target_pairs={{0,24},{4,12},{8,0},{12,20},{16,8},{20,28},{24,16},{28,4},{1,25},{... | collective-permute-start | bytes 1572872 | tf_op jit(solution)/shard_map/ppermute | solution.py:235
  18.1 0.6 collective-permute-start.6
  18.7 1.0 collective-permute-done.7.refs_2_
  19.7 1.1 collective-permute-start.8
  20.9 3.6 %collective-permute-start.10 = (bf16[256,1024]{1,0:T(8,128)(2,1)S(1)}, bf16[256,1024]{1,0:T(8,128)(2,1)S(1)}, u32[]{:S(2)}, u32[]{:S(2)}) collective-permute-start(bf16[256,1024]{1,0:T(8,128)(2,1)S(1)} %get-tuple-element.34), channel_id=1, source_target_pairs={{0,24},{4,12},{8,0},{12,20},{16,8},{20,28},{24,16},{28,4},{1,25},{... | collective-permute-start | bytes 1572872 | tf_op jit(solution)/shard_map/ppermute | solution.py:235
  24.4 0.0 collective-permute-done.6.refs_1_
  24.4 0.0 collective-permute-done.8.refs_3_
  24.4 1.6 %shard_map.65 = (bf16[256,1024]{1,0:T(8,128)(2,1)S(1)}, bf16[256,1024]{1,0:T(8,128)(2,1)S(1)}) custom-call(bf16[144,1024]{1,0:T(8,128)(2,1)S(1)} %pad_maximum_fusion.1.refs_0_, bf16[144,1024]{1,0:T(8,128)(2,1)S(1)} %collective-permute-done.6.refs_1_, bf16[144,1024]{1,0:T(8,128)(2,1)S(1)} %collective-permute-done.7.refs_2_, ...), custom_call_target="tpu_custom_call" | custom-call | flops 536870912 | bytes 2490368 | tf_op jit(solution)/shard_map/pallas_call | solution.py:159
  26.1 3.1 %collective-permute-done.5 = bf16[256,1024]{1,0:T(8,128)(2,1)S(1)} collective-permute-done((bf16[256,1024]{1,0:T(8,128)(2,1)S(1)}, bf16[256,1024]{1,0:T(8,128)(2,1)S(1)}, u32[]{:S(2)}, u32[]{:S(2)}) %collective-permute-start.5) | collective-permute-done | bytes 524320 | tf_op jit(solution)/shard_map/ppermute | solution.py:235
  29.2 0.1 broadcast_select_fusion.1
  29.2 2.1 %collective-permute-start.9 = (bf16[256,1024]{1,0:T(8,128)(2,1)S(1)}, bf16[256,1024]{1,0:T(8,128)(2,1)S(1)}, u32[]{:S(2)}, u32[]{:S(2)}) collective-permute-start(bf16[256,1024]{1,0:T(8,128)(2,1)S(1)} %broadcast_select_fusion.1), channel_id=1, source_target_pairs={{0,4},{4,0},{8,12},{12,8},{16,20},{20,16},{24,28},{28,24},{1,5},{5... | collective-permute-start | bytes 1572872 | tf_op jit(solution)/shard_map/ppermute | solution.py:250
  31.3 9.1 %collective-permute-done.10 = bf16[256,1024]{1,0:T(8,128)(2,1)S(1)} collective-permute-done((bf16[256,1024]{1,0:T(8,128)(2,1)S(1)}, bf16[256,1024]{1,0:T(8,128)(2,1)S(1)}, u32[]{:S(2)}, u32[]{:S(2)}) %collective-permute-start.10) | collective-permute-done | bytes 524320 | tf_op jit(solution)/shard_map/ppermute | solution.py:235
  40.4 0.1 broadcast_select_fusion
  40.5 2.1 %collective-permute-start.11 = (bf16[256,1024]{1,0:T(8,128)(2,1)S(1)}, bf16[256,1024]{1,0:T(8,128)(2,1)S(1)}, u32[]{:S(2)}, u32[]{:S(2)}) collective-permute-start(bf16[256,1024]{1,0:T(8,128)(2,1)S(1)} %broadcast_select_fusion), channel_id=1, source_target_pairs={{0,4},{4,0},{8,12},{12,8},{16,20},{20,16},{24,28},{28,24},{1,5},{5... | collective-permute-start | bytes 1572872 | tf_op jit(solution)/shard_map/ppermute | solution.py:250
  42.6 0.0 collective-permute-done.9.refs_3_
  42.6 0.4 add_convert_fusion.1
  43.0 4.0 %collective-permute-start.12 = (bf16[256,1024]{1,0:T(8,128)(2,1)S(1)}, bf16[256,1024]{1,0:T(8,128)(2,1)S(1)}, u32[]{:S(2)}, u32[]{:S(2)}) collective-permute-start(bf16[256,1024]{1,0:T(8,128)(2,1)S(1)} %add_convert_fusion.1), channel_id=1, source_target_pairs={{1,16},{16,1},{3,18},{18,3},{5,20},{20,5},{7,22},{22,7},{9,24},{24... | collective-permute-start | bytes 1572872 | tf_op jit(solution)/shard_map/ppermute | solution.py:260
  47.0 6.8 %collective-permute-done.11.refs_4_ = bf16[256,1024]{1,0:T(8,128)(2,1)S(1)} collective-permute-done((bf16[256,1024]{1,0:T(8,128)(2,1)S(1)}, bf16[256,1024]{1,0:T(8,128)(2,1)S(1)}, u32[]{:S(2)}, u32[]{:S(2)}) %collective-permute-start.11) | collective-permute-done | bytes 524320 | tf_op jit(solution)/shard_map/ppermute | solution.py:250
  53.8 0.4 add_convert_fusion
  54.2 4.0 %collective-permute-start.13 = (bf16[256,1024]{1,0:T(8,128)(2,1)S(1)}, bf16[256,1024]{1,0:T(8,128)(2,1)S(1)}, u32[]{:S(2)}, u32[]{:S(2)}) collective-permute-start(bf16[256,1024]{1,0:T(8,128)(2,1)S(1)} %add_convert_fusion), channel_id=1, source_target_pairs={{1,16},{16,1},{3,18},{18,3},{5,20},{20,5},{7,22},{22,7},{9,24},{24... | collective-permute-start | bytes 1572872 | tf_op jit(solution)/shard_map/ppermute | solution.py:260
  58.3 1.8 %collective-permute-done.12.refs_1_ = bf16[256,1024]{1,0:T(8,128)(2,1)S(1)} collective-permute-done((bf16[256,1024]{1,0:T(8,128)(2,1)S(1)}, bf16[256,1024]{1,0:T(8,128)(2,1)S(1)}, u32[]{:S(2)}, u32[]{:S(2)}) %collective-permute-start.12) | collective-permute-done | bytes 524320 | tf_op jit(solution)/shard_map/ppermute | solution.py:260
  60.0 1.4 %collective-permute-start.14 = (bf16[256,1024]{1,0:T(8,128)(2,1)S(1)}, bf16[256,1024]{1,0:T(8,128)(2,1)S(1)}, u32[]{:S(2)}, u32[]{:S(2)}) collective-permute-start(bf16[256,1024]{1,0:T(8,128)(2,1)S(1)} %collective-permute-done.12.refs_1_), channel_id=1, source_target_pairs={{0,8},{4,12},{8,0},{12,4},{16,24},{20,28},{24,16},{28,20},{1,9},{5... | collective-permute-start | bytes 1572872 | tf_op jit(solution)/shard_map/ppermute | solution.py:265
  61.4 0.0 copy-done.2
  61.4 4.2 %shard_map.66 = bf16[512,1024]{1,0:T(8,128)(2,1)S(1)} custom-call(bf16[512,1024]{1,0:T(8,128)(2,1)S(1)} %bitcast.26, bf16[256,1024]{1,0:T(8,128)(2,1)S(1)} %get-tuple-element.27.refs_1_, bf16[256,1024]{1,0:T(8,128)(2,1)S(1)} %get-tuple-element.28.refs_2_, bf16[256,1024]{1,0:T(8,128)(2,1)S(1)} %collective-permute-done.9.refs_3_, ...), custom_call_target="tpu_custom_call" | custom-call | flops 2684354560 | bytes 5242880 | tf_op jit(solution)/shard_map/pallas_call | solution.py:159
  65.6 5.8 %collective-permute-done.13.refs_2_ = bf16[256,1024]{1,0:T(8,128)(2,1)S(1)} collective-permute-done((bf16[256,1024]{1,0:T(8,128)(2,1)S(1)}, bf16[256,1024]{1,0:T(8,128)(2,1)S(1)}, u32[]{:S(2)}, u32[]{:S(2)}) %collective-permute-start.13) | collective-permute-done | bytes 524320 | tf_op jit(solution)/shard_map/ppermute | solution.py:260
  71.4 5.7 %collective-permute-done.14.refs_3_ = bf16[256,1024]{1,0:T(8,128)(2,1)S(1)} collective-permute-done((bf16[256,1024]{1,0:T(8,128)(2,1)S(1)}, bf16[256,1024]{1,0:T(8,128)(2,1)S(1)}, u32[]{:S(2)}, u32[]{:S(2)}) %collective-permute-start.14) | collective-permute-done | bytes 524320 | tf_op jit(solution)/shard_map/ppermute | solution.py:265
  77.0 0.0 collective-permute-start.15
  77.0 1.9 %collective-permute-start.18 = (bf16[512,1024]{1,0:T(8,128)(2,1)S(1)}, bf16[512,1024]{1,0:T(8,128)(2,1)S(1)}, u32[]{:S(2)}, u32[]{:S(2)}) collective-permute-start(bf16[512,1024]{1,0:T(8,128)(2,1)S(1)} %shard_map.66), channel_id=1, source_target_pairs={{16,0},{1,17},{18,2},{3,19},{20,4},{5,21},{22,6},{7,23},{24,8},{9,... | collective-permute-start | bytes 3145736 | tf_op jit(solution)/shard_map/ppermute | solution.py:280
  79.0 0.1 collective-permute-start.16
  79.1 17.0 %collective-permute-done.15.refs_4_ = bf16[256,1024]{1,0:T(8,128)(2,1)S(1)} collective-permute-done((bf16[256,1024]{1,0:T(8,128)(2,1)S(1)}, bf16[256,1024]{1,0:T(8,128)(2,1)S(1)}, u32[]{:S(2)}, u32[]{:S(2)}) %collective-permute-start.15) | collective-permute-done | bytes 524320 | tf_op jit(solution)/shard_map/ppermute | solution.py:278
  96.0 1.2 collective-permute-start.17
  97.3 0.0 collective-permute-done.16.refs_5_
  97.3 1.5 %collective-permute-done.17.refs_6_ = bf16[256,1024]{1,0:T(8,128)(2,1)S(1)} collective-permute-done((bf16[256,1024]{1,0:T(8,128)(2,1)S(1)}, bf16[256,1024]{1,0:T(8,128)(2,1)S(1)}, u32[]{:S(2)}, u32[]{:S(2)}) %collective-permute-start.17) | collective-permute-done | bytes 524320 | tf_op jit(solution)/shard_map/ppermute | solution.py:279
  98.8 4.3 %shard_map.67 = (bf16[256,1024]{1,0:T(8,128)(2,1)S(1)}, bf16[256,1024]{1,0:T(8,128)(2,1)S(1)}) custom-call(s32[1,2]{1,0:T(1,128)S(1)} %bitcast.30, bf16[256,1024]{1,0:T(8,128)(2,1)S(1)} %collective-permute-done.12.refs_1_, bf16[256,1024]{1,0:T(8,128)(2,1)S(1)} %collective-permute-done.13.refs_2_, bf16[256,1024]{1,0:T(8,128)(2,1)S(1)} %collective-permute-done.14.refs_3_, ...), custom_call_target="tpu_custom_call" | custom-call | flops 2684354560 | bytes 4194312 | tf_op jit(solution)/shard_map/pallas_call | solution.py:159
  103.1 0.0 collective-permute-done.18
  103.1 0.0 copy-start.3
  103.1 5.1 %collective-permute-start.19 = (bf16[256,1024]{1,0:T(8,128)(2,1)S(1)}, bf16[256,1024]{1,0:T(8,128)(2,1)S(1)}, u32[]{:S(2)}, u32[]{:S(2)}) collective-permute-start(bf16[256,1024]{1,0:T(8,128)(2,1)S(1)} %get-tuple-element.44), channel_id=1, source_target_pairs={{1,0},{16,17},{3,2},{18,19},{5,4},{20,21},{7,6},{22,23},{9,8},{24,... | collective-permute-start | bytes 1572872 | tf_op jit(solution)/shard_map/ppermute | solution.py:287
  108.2 1.3 collective-permute-start.20
  109.5 0.2 collective-permute-done.19
  109.7 0.3 subtract_convert_fusion.1
  110.0 1.0 collective-permute-done.20
  111.0 0.3 subtract_convert_fusion
  111.3 1.3 collective-permute-start.22
  112.6 1.3 collective-permute-start.21
  113.9 1.9 %fusion.1.ready = bf16[512,1024]{1,0:T(8,128)(2,1)S(1)} fusion(bf16[512,1024]{1,0:T(8,128)(2,1)} %copy-done.3, bf16[512,1024]{1,0:T(8,128)(2,1)S(1)} %shard_map.66, bf16[256,1024]{1,0:T(8,128)(2,1)S(1)} %subtract_convert_fusion, bf16[256,1024]{1,0:T(8,128)(2,1)S(1)} %subtract_convert_fusion.1, pred[]{:T(512)S(6)} %eq.16), kind=kLoop, calls=%fused_computation.2 | loop fusion | flops 5767168 | bytes 4194305 | tf_op jit(solution)/shard_map/convert_element_type | solution.py:306
  115.8 15.5 %collective-permute-done.22.refs_1_ = bf16[256,1024]{1,0:T(8,128)(2,1)S(1)} collective-permute-done((bf16[256,1024]{1,0:T(8,128)(2,1)S(1)}, bf16[256,1024]{1,0:T(8,128)(2,1)S(1)}, u32[]{:S(2)}, u32[]{:S(2)}) %collective-permute-start.22) | collective-permute-done | bytes 524320 | tf_op jit(solution)/shard_map/ppermute | solution.py:295
  131.3 5.6 %collective-permute-done.21.refs_0_ = bf16[256,1024]{1,0:T(8,128)(2,1)S(1)} collective-permute-done((bf16[256,1024]{1,0:T(8,128)(2,1)S(1)}, bf16[256,1024]{1,0:T(8,128)(2,1)S(1)}, u32[]{:S(2)}, u32[]{:S(2)}) %collective-permute-start.21) | collective-permute-done | bytes 524320 | tf_op jit(solution)/shard_map/ppermute | solution.py:295
  136.9 1.1 shard_map.68
  (11 shorter events, 0.1 us)
Async XLA Ops:
  0.0 1.2 copy-start.4
  0.0 3.4 %copy-start.5 = (s32[1,2]{1,0:T(1,128)S(1)}, s32[1,2]{1,0:T(1,128)}, u32[]{:S(2)}) copy-start(s32[1,2]{1,0:T(1,128)} %param.11) | copy-start | bytes 28
  0.0 12.9 %copy-start.1 = (bf16[2,1,1,256,512]{4,3,2,1,0:T(8,128)(2,1)S(1)}, bf16[2,1,1,256,512]{4,3,2,1,0:T(8,128)(2,1)}, u32[]{:S(2)}) copy-start(bf16[2,1,1,256,512]{4,3,2,1,0:T(8,128)(2,1)} %param.8) | copy-start | bytes 1572868
  0.0 12.9 %copy-start = (bf16[1,1,512,1024]{3,2,1,0:T(8,128)(2,1)S(1)}, bf16[1,1,512,1024]{3,2,1,0:T(8,128)(2,1)}, u32[]{:S(2)}) copy-start(bf16[1,1,512,1024]{3,2,1,0:T(8,128)(2,1)} %param.10) | copy-start | bytes 3145732
  1.3 9.9 %collective-permute-start.1 = (bf16[144,1024]{1,0:T(8,128)(2,1)S(1)}, bf16[144,1024]{1,0:T(8,128)(2,1)S(1)}, u32[]{:S(2)}, u32[]{:S(2)}) collective-permute-start(bf16[144,1024]{1,0:T(8,128)(2,1)S(1)} %pad_maximum_fusion.refs_0_), channel_id=1, source_target_pairs={{0,2},{1,3},{2,0},{3,1},{4,6},{5,7},{6,4},{7,5},{8,10},{9,11},{10,... | collective-permute-start | bytes 884744 | tf_op jit(solution)/shard_map/ppermute | solution.py:220
  3.4 6.6 %collective-permute-start.2 = (s32[2]{0:T(128)S(1)}, s32[2]{0:T(128)S(1)}, u32[]{:S(2)}, u32[]{:S(2)}) collective-permute-start(s32[2]{0:T(128)S(1)} %bitcast.31), channel_id=1, source_target_pairs={{0,4},{4,0},{8,12},{12,8},{16,20},{20,16},{24,28},{28,24},{1,5},{5... | collective-permute-start | bytes 32 | tf_op jit(solution)/shard_map/ppermute | solution.py:204
  4.6 6.5 %collective-permute-start.3 = (s32[2]{0:T(128)S(1)}, s32[2]{0:T(128)S(1)}, u32[]{:S(2)}, u32[]{:S(2)}) collective-permute-start(s32[2]{0:T(128)S(1)} %bitcast.32), channel_id=1, source_target_pairs={{1,16},{16,1},{3,18},{18,3},{5,20},{20,5},{7,22},{22,7},{9,24},{24... | collective-permute-start | bytes 32 | tf_op jit(solution)/shard_map/ppermute | solution.py:205
  10.0 3.0 %collective-permute-start = (bf16[144,1024]{1,0:T(8,128)(2,1)S(1)}, bf16[144,1024]{1,0:T(8,128)(2,1)S(1)}, u32[]{:S(2)}, u32[]{:S(2)}) collective-permute-start(bf16[144,1024]{1,0:T(8,128)(2,1)S(1)} %pad_maximum_fusion.refs_0_), channel_id=1, source_target_pairs={{0,1},{1,0},{2,3},{3,2},{4,5},{5,4},{6,7},{7,6},{8,9},{9,8},{10,11... | collective-permute-start | bytes 884744 | tf_op jit(solution)/shard_map/ppermute | solution.py:220
  11.2 1.8 %collective-permute-start.4 = (bf16[144,1024]{1,0:T(8,128)(2,1)S(1)}, bf16[144,1024]{1,0:T(8,128)(2,1)S(1)}, u32[]{:S(2)}, u32[]{:S(2)}) collective-permute-start(bf16[144,1024]{1,0:T(8,128)(2,1)S(1)} %collective-permute-done.1.refs_2_), channel_id=1, source_target_pairs={{0,1},{1,0},{2,3},{3,2},{4,5},{5,4},{6,7},{7,6},{8,9},{9,8},{10,11... | collective-permute-start | bytes 884744 | tf_op jit(solution)/shard_map/ppermute | solution.py:220
  11.4 8.4 %collective-permute-start.7 = (bf16[144,1024]{1,0:T(8,128)(2,1)S(1)}, bf16[144,1024]{1,0:T(8,128)(2,1)S(1)}, u32[]{:S(2)}, u32[]{:S(2)}) collective-permute-start(bf16[144,1024]{1,0:T(8,128)(2,1)S(1)} %pad_maximum_fusion.1.refs_0_), channel_id=1, source_target_pairs={{0,2},{1,3},{2,0},{3,1},{4,6},{5,7},{6,4},{7,5},{8,10},{9,11},{10,... | collective-permute-start | bytes 884744 | tf_op jit(solution)/shard_map/ppermute | solution.py:220
  14.8 14.4 %collective-permute-start.5 = (bf16[256,1024]{1,0:T(8,128)(2,1)S(1)}, bf16[256,1024]{1,0:T(8,128)(2,1)S(1)}, u32[]{:S(2)}, u32[]{:S(2)}) collective-permute-start(bf16[256,1024]{1,0:T(8,128)(2,1)S(1)} %get-tuple-element.30), channel_id=1, source_target_pairs={{0,24},{4,12},{8,0},{12,20},{16,8},{20,28},{24,16},{28,4},{1,25},{... | collective-permute-start | bytes 1572872 | tf_op jit(solution)/shard_map/ppermute | solution.py:235
  18.1 6.3 %collective-permute-start.6 = (bf16[144,1024]{1,0:T(8,128)(2,1)S(1)}, bf16[144,1024]{1,0:T(8,128)(2,1)S(1)}, u32[]{:S(2)}, u32[]{:S(2)}) collective-permute-start(bf16[144,1024]{1,0:T(8,128)(2,1)S(1)} %pad_maximum_fusion.1.refs_0_), channel_id=1, source_target_pairs={{0,1},{1,0},{2,3},{3,2},{4,5},{5,4},{6,7},{7,6},{8,9},{9,8},{10,11... | collective-permute-start | bytes 884744 | tf_op jit(solution)/shard_map/ppermute | solution.py:220
  19.7 4.7 %collective-permute-start.8 = (bf16[144,1024]{1,0:T(8,128)(2,1)S(1)}, bf16[144,1024]{1,0:T(8,128)(2,1)S(1)}, u32[]{:S(2)}, u32[]{:S(2)}) collective-permute-start(bf16[144,1024]{1,0:T(8,128)(2,1)S(1)} %collective-permute-done.7.refs_2_), channel_id=1, source_target_pairs={{0,1},{1,0},{2,3},{3,2},{4,5},{5,4},{6,7},{7,6},{8,9},{9,8},{10,11... | collective-permute-start | bytes 884744 | tf_op jit(solution)/shard_map/ppermute | solution.py:220
  20.9 19.5 %collective-permute-start.10 = (bf16[256,1024]{1,0:T(8,128)(2,1)S(1)}, bf16[256,1024]{1,0:T(8,128)(2,1)S(1)}, u32[]{:S(2)}, u32[]{:S(2)}) collective-permute-start(bf16[256,1024]{1,0:T(8,128)(2,1)S(1)} %get-tuple-element.34), channel_id=1, source_target_pairs={{0,24},{4,12},{8,0},{12,20},{16,8},{20,28},{24,16},{28,4},{1,25},{... | collective-permute-start | bytes 1572872 | tf_op jit(solution)/shard_map/ppermute | solution.py:235
  29.2 13.3 %collective-permute-start.9 = (bf16[256,1024]{1,0:T(8,128)(2,1)S(1)}, bf16[256,1024]{1,0:T(8,128)(2,1)S(1)}, u32[]{:S(2)}, u32[]{:S(2)}) collective-permute-start(bf16[256,1024]{1,0:T(8,128)(2,1)S(1)} %broadcast_select_fusion.1), channel_id=1, source_target_pairs={{0,4},{4,0},{8,12},{12,8},{16,20},{20,16},{24,28},{28,24},{1,5},{5... | collective-permute-start | bytes 1572872 | tf_op jit(solution)/shard_map/ppermute | solution.py:250
  40.5 13.3 %collective-permute-start.11 = (bf16[256,1024]{1,0:T(8,128)(2,1)S(1)}, bf16[256,1024]{1,0:T(8,128)(2,1)S(1)}, u32[]{:S(2)}, u32[]{:S(2)}) collective-permute-start(bf16[256,1024]{1,0:T(8,128)(2,1)S(1)} %broadcast_select_fusion), channel_id=1, source_target_pairs={{0,4},{4,0},{8,12},{12,8},{16,20},{20,16},{24,28},{28,24},{1,5},{5... | collective-permute-start | bytes 1572872 | tf_op jit(solution)/shard_map/ppermute | solution.py:250
  43.0 17.1 %collective-permute-start.12 = (bf16[256,1024]{1,0:T(8,128)(2,1)S(1)}, bf16[256,1024]{1,0:T(8,128)(2,1)S(1)}, u32[]{:S(2)}, u32[]{:S(2)}) collective-permute-start(bf16[256,1024]{1,0:T(8,128)(2,1)S(1)} %add_convert_fusion.1), channel_id=1, source_target_pairs={{1,16},{16,1},{3,18},{18,3},{5,20},{20,5},{7,22},{22,7},{9,24},{24... | collective-permute-start | bytes 1572872 | tf_op jit(solution)/shard_map/ppermute | solution.py:260
  53.8 7.6 %copy-start.2 = (bf16[1,1,512,1024]{3,2,1,0:T(8,128)(2,1)S(1)}, bf16[1,1,512,1024]{3,2,1,0:T(8,128)(2,1)}, u32[]{:S(2)}) copy-start(bf16[1,1,512,1024]{3,2,1,0:T(8,128)(2,1)} %param.9) | copy-start | bytes 3145732
  54.2 17.2 %collective-permute-start.13 = (bf16[256,1024]{1,0:T(8,128)(2,1)S(1)}, bf16[256,1024]{1,0:T(8,128)(2,1)S(1)}, u32[]{:S(2)}, u32[]{:S(2)}) collective-permute-start(bf16[256,1024]{1,0:T(8,128)(2,1)S(1)} %add_convert_fusion), channel_id=1, source_target_pairs={{1,16},{16,1},{3,18},{18,3},{5,20},{20,5},{7,22},{22,7},{9,24},{24... | collective-permute-start | bytes 1572872 | tf_op jit(solution)/shard_map/ppermute | solution.py:260
  60.0 17.0 %collective-permute-start.14 = (bf16[256,1024]{1,0:T(8,128)(2,1)S(1)}, bf16[256,1024]{1,0:T(8,128)(2,1)S(1)}, u32[]{:S(2)}, u32[]{:S(2)}) collective-permute-start(bf16[256,1024]{1,0:T(8,128)(2,1)S(1)} %collective-permute-done.12.refs_1_), channel_id=1, source_target_pairs={{0,8},{4,12},{8,0},{12,4},{16,24},{20,28},{24,16},{28,20},{1,9},{5... | collective-permute-start | bytes 1572872 | tf_op jit(solution)/shard_map/ppermute | solution.py:265
  77.0 19.0 %collective-permute-start.15 = (bf16[256,1024]{1,0:T(8,128)(2,1)S(1)}, bf16[256,1024]{1,0:T(8,128)(2,1)S(1)}, u32[]{:S(2)}, u32[]{:S(2)}) collective-permute-start(bf16[256,1024]{1,0:T(8,128)(2,1)S(1)} %collective-permute-done.13.refs_2_), channel_id=1, source_target_pairs={{0,8},{4,12},{8,0},{12,4},{16,24},{20,28},{24,16},{28,20},{1,9},{5... | collective-permute-start | bytes 1572872 | tf_op jit(solution)/shard_map/ppermute | solution.py:278
  77.0 26.1 %collective-permute-start.18 = (bf16[512,1024]{1,0:T(8,128)(2,1)S(1)}, bf16[512,1024]{1,0:T(8,128)(2,1)S(1)}, u32[]{:S(2)}, u32[]{:S(2)}) collective-permute-start(bf16[512,1024]{1,0:T(8,128)(2,1)S(1)} %shard_map.66), channel_id=1, source_target_pairs={{16,0},{1,17},{18,2},{3,19},{20,4},{5,21},{22,6},{7,23},{24,8},{9,... | collective-permute-start | bytes 3145736 | tf_op jit(solution)/shard_map/ppermute | solution.py:280
  79.0 18.3 %collective-permute-start.16 = (bf16[256,1024]{1,0:T(8,128)(2,1)S(1)}, bf16[256,1024]{1,0:T(8,128)(2,1)S(1)}, u32[]{:S(2)}, u32[]{:S(2)}) collective-permute-start(bf16[256,1024]{1,0:T(8,128)(2,1)S(1)} %collective-permute-done.14.refs_3_), channel_id=1, source_target_pairs={{0,1},{1,0},{2,3},{3,2},{4,5},{5,4},{6,7},{7,6},{8,9},{9,8},{10,11... | collective-permute-start | bytes 1572872 | tf_op jit(solution)/shard_map/ppermute | solution.py:279
  96.0 2.8 %collective-permute-start.17 = (bf16[256,1024]{1,0:T(8,128)(2,1)S(1)}, bf16[256,1024]{1,0:T(8,128)(2,1)S(1)}, u32[]{:S(2)}, u32[]{:S(2)}) collective-permute-start(bf16[256,1024]{1,0:T(8,128)(2,1)S(1)} %collective-permute-done.15.refs_4_), channel_id=1, source_target_pairs={{0,1},{1,0},{2,3},{3,2},{4,5},{5,4},{6,7},{7,6},{8,9},{9,8},{10,11... | collective-permute-start | bytes 1572872 | tf_op jit(solution)/shard_map/ppermute | solution.py:279
  103.1 6.9 %copy-start.3 = (bf16[512,1024]{1,0:T(8,128)(2,1)}, bf16[512,1024]{1,0:T(8,128)(2,1)S(1)}, u32[]{:S(2)}) copy-start(bf16[512,1024]{1,0:T(8,128)(2,1)S(1)} %collective-permute-done.18) | copy-start | bytes 3145732
  103.1 6.6 %collective-permute-start.19 = (bf16[256,1024]{1,0:T(8,128)(2,1)S(1)}, bf16[256,1024]{1,0:T(8,128)(2,1)S(1)}, u32[]{:S(2)}, u32[]{:S(2)}) collective-permute-start(bf16[256,1024]{1,0:T(8,128)(2,1)S(1)} %get-tuple-element.44), channel_id=1, source_target_pairs={{1,0},{16,17},{3,2},{18,19},{5,4},{20,21},{7,6},{22,23},{9,8},{24,... | collective-permute-start | bytes 1572872 | tf_op jit(solution)/shard_map/ppermute | solution.py:287
  108.2 2.8 %collective-permute-start.20 = (bf16[256,1024]{1,0:T(8,128)(2,1)S(1)}, bf16[256,1024]{1,0:T(8,128)(2,1)S(1)}, u32[]{:S(2)}, u32[]{:S(2)}) collective-permute-start(bf16[256,1024]{1,0:T(8,128)(2,1)S(1)} %get-tuple-element.45), channel_id=1, source_target_pairs={{1,0},{16,17},{3,2},{18,19},{5,4},{20,21},{7,6},{22,23},{9,8},{24,... | collective-permute-start | bytes 1572872 | tf_op jit(solution)/shard_map/ppermute | solution.py:287
  111.3 20.0 %collective-permute-start.22 = (bf16[256,1024]{1,0:T(8,128)(2,1)S(1)}, bf16[256,1024]{1,0:T(8,128)(2,1)S(1)}, u32[]{:S(2)}, u32[]{:S(2)}) collective-permute-start(bf16[256,1024]{1,0:T(8,128)(2,1)S(1)} %subtract_convert_fusion), channel_id=1, source_target_pairs={{0,16},{17,1},{2,18},{19,3},{4,20},{21,5},{6,22},{23,7},{8,24},{25... | collective-permute-start | bytes 1572872 | tf_op jit(solution)/shard_map/ppermute | solution.py:295
  112.6 24.3 %collective-permute-start.21 = (bf16[256,1024]{1,0:T(8,128)(2,1)S(1)}, bf16[256,1024]{1,0:T(8,128)(2,1)S(1)}, u32[]{:S(2)}, u32[]{:S(2)}) collective-permute-start(bf16[256,1024]{1,0:T(8,128)(2,1)S(1)} %subtract_convert_fusion.1), channel_id=1, source_target_pairs={{0,16},{17,1},{2,18},{19,3},{4,20},{21,5},{6,22},{23,7},{8,24},{25... | collective-permute-start | bytes 1572872 | tf_op jit(solution)/shard_map/ppermute | solution.py:295

commit v4 on v3

--- a/solution.py
+++ b/solution.py
@@ -11,14 +11,10 @@
 NS_ITERS = 2
 CHUNKS = 2
 BLOCKS = 2
-SERIAL_X = False
-LAG_X = 9
-LAG_S = 9
-SERIAL_T = False
-LAG_T = 9
-SERIAL_W = True
-NS_AFTER = 0
-GATE = False
+DIRECT = 1
+X_LATE = True
+NS_LATE = False
+B_LATE = False
 VMEM_LIMIT = 32 * 1024 * 1024
 
 coef_a = 3.4445
@@ -35,14 +31,16 @@
     return lax.dot_general(a, b, (dims, ((), ())), preferred_element_type=jnp.float32)
 
 
-def newton_schulz(current):
+def newton_schulz(*currents):
     for repeat in range(NS_ITERS):
-        gram = dot(current, current, ((1,), (1,))).astype(jnp.bfloat16)
-        squared = dot(gram, gram, ((1,), (0,)))
-        poly = (coef_b * gram.astype(jnp.float32) + coef_c * squared).astype(jnp.bfloat16)
-        product = dot(poly, current, ((1,), (0,)))
-        current = (coef_a * current.astype(jnp.float32) + product).astype(jnp.bfloat16)
-    return current
+        grams = [dot(c, c, ((1,), (1,))).astype(jnp.bfloat16) for c in currents]
+        squares = [dot(g, g, ((1,), (0,))) for g in grams]
+        polys = [
+            (coef_b * g.astype(jnp.float32) + coef_c * q).astype(jnp.bfloat16) for g, q in zip(grams, squares)
+        ]
+        products = [dot(p, c, ((1,), (0,))) for p, c in zip(polys, currents)]
+        currents = [(coef_a * c.astype(jnp.float32) + p).astype(jnp.bfloat16) for c, p in zip(currents, products)]
+    return currents
 
 
 def normalized(tracked):
@@ -53,45 +51,50 @@
 
 def first_step_kernel(chunks, *refs):
     offset, grads, partners = refs[0], refs[1 : 1 + chunks], refs[1 + chunks : 1 + 2 * chunks]
-    weight, moved = refs[1 + 2 * chunks :]
+    weight, blocks = refs[1 + 2 * chunks], refs[2 + 2 * chunks :]
     start, tracked = 0, []
     for k in range(chunks):
         part = slice(start, start + grads[k].shape[0])
         start = part.stop
         own = offset[part, :].astype(jnp.float32) + grads[k][...].astype(jnp.float32)
         tracked.append(0.5 * (own + partners[k][...].astype(jnp.float32)))
-    ortho = newton_schulz(normalized(tracked))
-    moved[...] = (
-        weight[...].astype(jnp.float32) - step_scale * ortho.astype(jnp.float32)
-    ).astype(moved.dtype)
-
-
-def second_step_kernel(chunks, bits, *refs):
-    own, same, other = refs[:chunks], refs[chunks : 2 * chunks], refs[2 * chunks : 3 * chunks]
-    blocks = refs[3 * chunks :]
-    sites, site, core = lax.axis_size("site"), lax.axis_index("site"), lax.axis_index("expert") % 2
-    half = sites // 2
-    problem, source = site % half + half * core, (site + half - 2) % half + half * core
-    ahead_same = ((problem + 2) % sites == source).astype(jnp.int32)
-    use_same = bits[0:1, 1:2] == ahead_same
-    tracked = []
-    for k in range(chunks):
-        partner = jnp.where(use_same, same[k][...].astype(jnp.float32), other[k][...].astype(jnp.float32))
-        tracked.append(0.5 * (own[k][...].astype(jnp.float32) + partner))
-    ortho = newton_schulz(normalized(tracked))
+    (ortho,) = newton_schulz(normalized(tracked))
     rows = blocks[0].shape[0]
     for k, block in enumerate(blocks):
-        block[...] = ortho[k * rows : (k + 1) * rows, :]
-
-
-def last_kernel(blocks, ready, *refs):
-    back, out, buffer, semaphores = refs[:blocks], *refs[blocks:]
-    rows = back[0].shape[0]
+        part = slice(k * rows, (k + 1) * rows)
+        value = weight[part, :].astype(jnp.float32) - step_scale * ortho[part, :].astype(jnp.float32)
+        block[...] = value.astype(block.dtype)
+
+
+def second_step_kernel(chunks, bits_first, bits_second, *refs):
+    groups = [refs[i * chunks : (i + 1) * chunks] for i in range(4)]
+    here0, here1, there0, there1 = groups
+    blocks = refs[4 * chunks :]
+    core = lax.axis_index("expert") % 2
+    starts = []
+    for own, use_here in (
+        (here1, bits_first[0:1, 1:2] == 1 - core),
+        (there0, bits_second[0:1, 1:2] == core),
+    ):
+        tracked = []
+        for k in range(chunks):
+            partner = jnp.where(use_here, here0[k][...].astype(jnp.float32), there1[k][...].astype(jnp.float32))
+            tracked.append(0.5 * (own[k][...].astype(jnp.float32) + partner))
+        starts.append(normalized(tracked))
+    first, second = newton_schulz(*starts)
+    total = -0.5 * step_scale * (first.astype(jnp.float32) + second.astype(jnp.float32))
+    rows = blocks[0].shape[0]
+    for k, block in enumerate(blocks):
+        block[...] = total[k * rows : (k + 1) * rows, :]
+
+
+def last_kernel(blocks, *refs):
+    first, second, out, buffer, semaphores = refs[:blocks], refs[blocks : 2 * blocks], *refs[2 * blocks :]
+    rows = first[0].shape[0]
     copies = []
     for k in range(blocks):
         part = pl.ds(k * rows, rows)
-        value = ready[part, :].astype(jnp.float32) + 0.5 * back[k][...].astype(jnp.float32)
-        buffer[part, :] = value.astype(buffer.dtype)
+        buffer[part, :] = first[k][...] + second[k][...]
         copies.append(pltpu.make_async_copy(buffer.at[part], out.at[0, 0, part], semaphores.at[k]))
         copies[-1].start()
     for copy in copies:
@@ -178,33 +181,34 @@
     site, expert = lax.axis_index("site"), lax.axis_index("expert")
     both = ("site", "expert")
 
-    cross, kept, to_mate, lent, returned = [], [], [], [], []
-    for s in range(half):
+    def at(site, expert):
+        return site * experts + expert
+
+    middle, outer, matched = [], [], []
+    for s in range(sites // 4):
+        near, far, last_site = s + half // 2, s + half, s + half + half // 2
         for e in range(0, experts, 2):
-            low, high = s * experts + e, (s + half) * experts + e
-            cross += [(low + 1, high), (high, low + 1)]
-            kept += [(low, low), (high + 1, high + 1)]
-            to_mate += [(low + 1, low), (high, high + 1)]
-            lent += [(high, low), (low + 1, high + 1)]
-            returned += [(low, high), (high + 1, low + 1)]
-    swap = cross + kept
+            for worker, owner in ((near, e), (far, e + 1)):
+                even, odd = at(worker, e), at(worker, e + 1)
+                middle += [(at(near, owner), even), (at(far, owner), odd)]
+                outer += [(at(s, owner), even), (at(last_site, owner), odd)]
+                matched += [(at(far, owner), even), (at(near, owner), odd)]
+    to_outer = [(b, a) for a, b in outer]
+    to_matched = [(b, a) for a, b in matched]
     mates = [(e, e ^ 1) for e in range(experts)]
     beside = [(s, s ^ 1) for s in range(sites)]
     helpers = [(s, (s + 2) % sites if s % 2 else (s - 2) % sites) for s in range(sites)]
-    within = [(s, s // half * half + (s + 2) % half) for s in range(sites)]
-
     weight, offset = weights[0, 0], tracker_offset[0, 0]
     stashed = hiddens[:, 0, 0]
     tokens, routing = out_grads[:, 0], routes[:, 0, :, 0]
     steps = tokens.shape[0]
     fan_rows, features = weight.shape
     bits = partner_bits[0]
-    is_swapped = (site < half) == (expert % 2 == 1)
 
     beside_bits = lax.ppermute(bits, "site", beside)
-    swap_bits = lax.ppermute(bits, both, swap)
     send_own = beside_bits.reshape(1, -1)[:, 0:1] == site % 2
-    swap_bits = swap_bits.reshape(1, -1)
+    first_bits = lax.ppermute(bits, both, outer).reshape(1, -1)
+    second_bits = lax.ppermute(bits, both, matched).reshape(1, -1)
 
     count = tokens.shape[1]
     named = routing.astype(jnp.bfloat16).reshape(steps, 1, count)
@@ -219,8 +223,8 @@
             hop = [(e, e ^ level) for e in range(experts)]
             gathered[k].update({j ^ level: lax.ppermute(t, "expert", hop) for j, t in gathered[k].items()})
             if k == 0 and level == top:
-                gathered[k][top], (send_own, swap_bits) = lax.optimization_barrier(
-                    (gathered[k][top], (send_own, swap_bits))
+                gathered[k][top], (send_own, first_bits, second_bits) = lax.optimization_barrier(
+                    (gathered[k][top], (send_own, first_bits, second_bits))
                 )
             level //= 2
 
@@ -232,78 +236,66 @@
     operands = [gathered[0][j] for j in range(experts)] + [(stashed, 0), (offset, None)]
     made = call(functools.partial(gradient_kernel, experts, True), operands, chunk * 2, cost)
     first, own = made[:CHUNKS], list(made[CHUNKS:])
-    fetched = [lax.ppermute(o, "site", helpers) for o in own]
+    ahead = [from_behind(o, "site", -1) for o in own[:DIRECT]]
+    behind = [from_behind(o, "site", 1) for o in own[:DIRECT]]
+    fetched = [lax.ppermute(o, "site", helpers) for o in own[DIRECT:]]
     operands = [gathered[1][j] for j in range(experts)] + [(stashed, 1)]
     last = call(functools.partial(gradient_kernel, experts, False), operands, chunk, cost)
 
-    chosen, partners, second, mine, same, other = [], [], [], [], [], []
+    use_ahead = bits.reshape(1, -1)[:, 0:1] == 1
+    partners, second, here0, here1 = [], [], [], []
     for i in range(CHUNKS):
-        arrived = after(fetched[i], last[0] if i == 0 else chosen[i - 1])
-        chosen.append(jnp.where(send_own, own[i], arrived))
-    for i in range(CHUNKS):
-        if i > 0:
-            chosen[i] = after(chosen[i], partners[i - 1]) if SERIAL_X else chosen[i]
-        if i >= LAG_S:
-            chosen[i] = after(chosen[i], second[i - LAG_S])
-        if i >= LAG_X:
-            chosen[i] = after(chosen[i], mine[i - LAG_X])
-        partners.append(lax.ppermute(chosen[i], "site", beside))
+        if i < DIRECT:
+            partners.append(jnp.where(use_ahead, ahead[i], after(behind[i], last[0])))
+        else:
+            arrived = after(fetched[i - DIRECT], last[0])
+            if i == DIRECT and i > 0 and X_LATE:
+                arrived = after(arrived, partners[-1])
+            partners.append(lax.ppermute(jnp.where(send_own, own[i], arrived), "site", beside))
         partner = partners[i] if i == 0 else after(partners[i], second[i - 1])
         grad = first[i].astype(jnp.float32)
         tracked = 0.5 * ((offset[parts[i]].astype(jnp.float32) + grad) + partner.astype(jnp.float32))
         later = (tracked - grad).astype(jnp.bfloat16).astype(jnp.float32)
         second.append((later + last[i].astype(jnp.float32)).astype(jnp.bfloat16))
-        if i > 0 and SERIAL_T:
-            second[i] = after(second[i], mine[i - 1])
-        if i >= LAG_T:
-            second[i] = after(second[i], same[i - LAG_T])
-        mine.append(lax.ppermute(second[i], both, swap))
-        if i < CHUNKS - 1:
-            value = mine[i]
-            if i > 0 and SERIAL_W:
-                value = after(value, same[i - 1])
-            same.append(lax.ppermute(value, "site", within))
+        here0.append(lax.ppermute(second[i], both, middle))
+        here1.append(lax.ppermute(second[i], both, outer))
 
     cost = NS_ITERS * 2 * (2 * fan_rows * fan_rows * features + fan_rows**3)
-    held = [after(partners[-1], mine[NS_AFTER])]
-    (moved,) = call(
+    held = after(partners[-1], (second[-1], here0[0]) if NS_LATE else second[-1])
+    rows = fan_rows // BLOCKS
+    moved = call(
         functools.partial(first_step_kernel, CHUNKS),
-        [(offset, None), *first, *partners[:-1], *held, (weight, None)],
-        whole,
+        [(offset, None), *first, *partners[:-1], held, (weight, None)],
+        [jax.ShapeDtypeStruct((rows, features), jnp.bfloat16)] * BLOCKS,
         cost,
     )
-    value = after(mine[-1], moved)
-    if SERIAL_W:
-        value = after(value, same[-1])
-    same.append(lax.ppermute(value, "site", within))
-    other = [lax.ppermute(value, "expert", mates) for value in same]
-    borrowed = lax.ppermute(after(moved, mine[-1]), both, lent)
-    if GATE:
-        other[-1] = after(other[-1], borrowed)
-    block_rows = fan_rows // BLOCKS
-    block = [jax.ShapeDtypeStruct((block_rows, features), jnp.bfloat16)] * BLOCKS
-    ortho = list(call(functools.partial(second_step_kernel, CHUNKS), [swap_bits, *mine, *same, *other], block, cost))
-    ortho[0] = after(ortho[0], borrowed)
-    paired_ortho = [lax.ppermute(o, both, to_mate) for o in ortho]
-    sent = []
+    here0[-1] = after(here0[-1], moved)
+    there0 = [lax.ppermute(h, "expert", mates) for h in here0]
+    there1 = [lax.ppermute(h, "expert", mates) for h in here1]
+    lent = [after(m, (here0[-1], here1[-1]) if B_LATE else second[-1]) for m in moved]
+    pairs = [(lax.ppermute(v, both, outer), lax.ppermute(v, both, matched)) for v in lent]
+
+    update = call(
+        functools.partial(second_step_kernel, CHUNKS),
+        [first_bits, second_bits, *here0, *here1, *there0, *there1],
+        [jax.ShapeDtypeStruct((rows, features), jnp.float32)] * BLOCKS,
+        2 * cost,
+    )
+    results = []
     for i in range(BLOCKS):
-        part = moved[i * block_rows : (i + 1) * block_rows].astype(jnp.float32)
-        met = paired_ortho[i] if i == 0 else after(paired_ortho[i], sent[i - 1])
-        sent.append(
-            (part - step_scale * (ortho[i].astype(jnp.float32) + met.astype(jnp.float32))).astype(jnp.bfloat16)
-        )
-    back = [lax.ppermute(x, both, returned) for x in sent]
-    halves = jnp.where(is_swapped, moved, jnp.concatenate(sent, axis=0)).astype(jnp.float32)
-    ready = 0.5 * jnp.where(is_swapped, halves, halves + borrowed.astype(jnp.float32))
+        pair = pairs[i] if i == 0 else after(pairs[i], results[-1])
+        pair = pair[0].astype(jnp.float32) + pair[1].astype(jnp.float32)
+        results.append((0.5 * pair + update[i]).astype(jnp.bfloat16))
+    arrived = [lax.ppermute(r, both, to_outer) for r in results] + [lax.ppermute(r, both, to_matched) for r in results]
     return pl.pallas_call(
         functools.partial(last_kernel, BLOCKS),
-        in_specs=[VMEM] * (1 + BLOCKS),
+        in_specs=[VMEM] * (2 * BLOCKS),
         out_specs=ANY,
         out_shape=jax.ShapeDtypeStruct((1, 1, fan_rows, features), jnp.bfloat16),
         scratch_shapes=[pltpu.VMEM((fan_rows, features), jnp.bfloat16), pltpu.SemaphoreType.DMA((BLOCKS,))],
         compiler_params=pltpu.CompilerParams(vmem_limit_bytes=VMEM_LIMIT),
         cost_estimate=pl.CostEstimate(flops=0, bytes_accessed=8 * fan_rows * features, transcendentals=0),
-    )(ready.astype(jnp.bfloat16), *back)
+    )(*arrived)
 
 
 def from_behind(block, axis, distance):
@@ -314,7 +306,7 @@
 
 def orthogonalize(tracked):
     frobenius = jnp.sqrt(jnp.sum(tracked * tracked))
-    return newton_schulz((tracked / (frobenius + 1e-07)).astype(jnp.bfloat16))
+    return newton_schulz((tracked / (frobenius + 1e-07)).astype(jnp.bfloat16))[0]
 
 
 def place_rows(gradient, routing, experts, slot_count):

time: 138 us -> 126 us (0.913)
  the two profiles are of different devices: /device:TPU:1 before, /device:TPU:9 now
where the time goes in v4:
time: 126 us
  waiting for transfers between devices  62 us (49%)
  starting transfers between devices  43.9 us (35%)
  Pallas kernels  15.8 us (13%)
  other arithmetic  2.21 us (2%)
    ppermute x2, waiting for transfers between devices, from_behind(): return lax.ppermute(block, axis, route)  16.7 us
    pallas_call x4, Pallas kernels, call(): pl.pallas_call(body, in_specs=[ANY if i in fetched else VMEM for i in ran...  14.8 us
    ppermute x2, waiting for transfers between devices, paired(): lax.ppermute(v, both, outer)  12.6 us
    ppermute x2, waiting for transfers between devices, paired(): lax.ppermute(r, both, to_matched)  9.9 us
    ppermute x2, starting transfers between devices, paired(): here0.append(lax.ppermute(second[i], both, middle))  8.06 us
    ppermute x1, waiting for transfers between devices, paired(): lax.ppermute(jnp.where(send_own, own[i], arrived), 'site', beside)  7.2 us
    ppermute x2, starting transfers between devices, paired(): lax.ppermute(v, both, matched)  6.04 us
    ppermute x6, starting transfers between devices, paired(): lax.ppermute(t, 'expert', hop)  5.74 us
  transfers between devices with their start and end apart: 29, of which 14 were waited for; matrix products, arithmetic and copies ran while one was open for 1% of the time, Pallas kernels for 12%

profile of v4, /device:TPU:9, one launch (start us, length us, event | category | flops | bytes accessed | tf_op | source)
XLA Modules:
  0.0 125.7 jit_solution(5712731333357626019)
XLA Ops:
  0.0 0.7 convert_bitcast_fusion
  0.7 1.2 slice_bitcast_fusion
  1.9 0.0 copy-start.1
  1.9 0.0 copy-start.3
  1.9 1.3 %collective-permute-start.1 = (bf16[144,1024]{1,0:T(8,128)(2,1)S(1)}, bf16[144,1024]{1,0:T(8,128)(2,1)S(1)}, u32[]{:S(2)}, u32[]{:S(2)}) collective-permute-start(bf16[144,1024]{1,0:T(8,128)(2,1)S(1)} %pad_maximum_fusion.refs_0_), channel_id=1, source_target_pairs={{0,2},{1,3},{2,0},{3,1},{4,6},{5,7},{6,4},{7,5},{8,10},{9,11},{10,... | collective-permute-start | bytes 884744 | tf_op jit(solution)/shard_map/ppermute | solution.py:224
  3.2 1.2 collective-permute-start.2
  4.4 1.3 %collective-permute-start.3 = (s32[2]{0:T(128)S(1)}, s32[2]{0:T(128)S(1)}, u32[]{:S(2)}, u32[]{:S(2)}) collective-permute-start(s32[2]{0:T(128)S(1)} %bitcast.36), channel_id=1, source_target_pairs={{0,8},{24,9},{1,16},{25,17},{2,10},{26,11},{3,18},{27,19},{4,12},{... | collective-permute-start | bytes 32 | tf_op jit(solution)/shard_map/ppermute | solution.py:210
  5.7 3.2 %collective-permute-start.4 = (s32[2]{0:T(128)S(1)}, s32[2]{0:T(128)S(1)}, u32[]{:S(2)}, u32[]{:S(2)}) collective-permute-start(s32[2]{0:T(128)S(1)} %bitcast.37), channel_id=1, source_target_pairs={{16,8},{8,9},{17,16},{9,17},{18,10},{10,11},{19,18},{11,19},{20,12... | collective-permute-start | bytes 32 | tf_op jit(solution)/shard_map/ppermute | solution.py:211
  8.9 0.1 collective-permute-start
  9.1 1.3 %collective-permute-done.3 = s32[2]{0:T(128)S(1)} collective-permute-done((s32[2]{0:T(128)S(1)}, s32[2]{0:T(128)S(1)}, u32[]{:S(2)}, u32[]{:S(2)}) %collective-permute-start.3) | collective-permute-done | bytes 40 | tf_op jit(solution)/shard_map/ppermute | solution.py:210
  10.3 0.0 collective-permute-done.4
  10.4 2.0 %collective-permute-start.5 = (bf16[144,1024]{1,0:T(8,128)(2,1)S(1)}, bf16[144,1024]{1,0:T(8,128)(2,1)S(1)}, u32[]{:S(2)}, u32[]{:S(2)}) collective-permute-start(bf16[144,1024]{1,0:T(8,128)(2,1)S(1)} %collective-permute-done.1.refs_2_), channel_id=1, source_target_pairs={{0,1},{1,0},{2,3},{3,2},{4,5},{5,4},{6,7},{7,6},{8,9},{9,8},{10,11... | collective-permute-start | bytes 884744 | tf_op jit(solution)/shard_map/ppermute | solution.py:224
  12.4 0.4 collective-permute-start.9
  12.8 0.0 collective-permute-done.refs_1_
  12.8 0.8 collective-permute-done.5.refs_3_
  13.6 1.8 %shard_map.64 = (bf16[256,1024]{1,0:T(8,128)(2,1)S(1)}, bf16[256,1024]{1,0:T(8,128)(2,1)S(1)}, bf16[256,1024]{1,0:T(8,128)(2,1)S(1)}, bf16[256,1024]{1,0:T(8,128)(2,1)S(1)}) custom-call(bf16[144,1024]{1,0:T(8,128)(2,1)S(1)} %pad_maximum_fusion.refs_0_, bf16[144,1024]{1,0:T(8,128)(2,1)S(1)} %collective-permute-done.refs_1_, ...), custom_call_target="tpu_custom_call" | custom-call | flops 536870912 | bytes 4587520 | tf_op jit(solution)/shard_map/pallas_call | solution.py:162
  15.4 0.4 collective-permute-start.7
  15.8 0.2 collective-permute-start.11
  16.0 2.3 %collective-permute-start.6 = (bf16[256,1024]{1,0:T(8,128)(2,1)S(1)}, bf16[256,1024]{1,0:T(8,128)(2,1)S(1)}, u32[]{:S(2)}, u32[]{:S(2)}) collective-permute-start(bf16[256,1024]{1,0:T(8,128)(2,1)S(1)} %get-tuple-element.33), channel_id=1, source_target_pairs={{4,0},{8,4},{12,8},{16,12},{20,16},{24,20},{28,24},{0,28},{5,1},{9... | collective-permute-start | bytes 1572872 | tf_op jit(solution)/shard_map/ppermute | solution.py:304
  18.3 1.1 collective-permute-start.8
  19.4 1.7 %collective-permute-done.9.refs_2_ = bf16[144,1024]{1,0:T(8,128)(2,1)S(1)} collective-permute-done((bf16[144,1024]{1,0:T(8,128)(2,1)S(1)}, bf16[144,1024]{1,0:T(8,128)(2,1)S(1)}, u32[]{:S(2)}, u32[]{:S(2)}) %collective-permute-start.9) | collective-permute-done | bytes 294944 | tf_op jit(solution)/shard_map/ppermute | solution.py:224
  21.1 0.8 collective-permute-start.10
  21.9 0.0 collective-permute-done.8.refs_1_
  22.0 1.2 collective-permute-done.10.refs_3_
  23.1 1.6 %shard_map.65 = (bf16[256,1024]{1,0:T(8,128)(2,1)S(1)}, bf16[256,1024]{1,0:T(8,128)(2,1)S(1)}) custom-call(bf16[144,1024]{1,0:T(8,128)(2,1)S(1)} %pad_maximum_fusion.1.refs_0_, bf16[144,1024]{1,0:T(8,128)(2,1)S(1)} %collective-permute-done.8.refs_1_, bf16[144,1024]{1,0:T(8,128)(2,1)S(1)} %collective-permute-done.9.refs_2_, ...), custom_call_target="tpu_custom_call" | custom-call | flops 536870912 | bytes 2490368 | tf_op jit(solution)/shard_map/pallas_call | solution.py:162
  24.8 4.8 %collective-permute-done.7 = bf16[256,1024]{1,0:T(8,128)(2,1)S(1)} collective-permute-done((bf16[256,1024]{1,0:T(8,128)(2,1)S(1)}, bf16[256,1024]{1,0:T(8,128)(2,1)S(1)}, u32[]{:S(2)}, u32[]{:S(2)}) %collective-permute-start.7) | collective-permute-done | bytes 524320 | tf_op jit(solution)/shard_map/ppermute | solution.py:304
  29.5 11.9 %collective-permute-done.6 = bf16[256,1024]{1,0:T(8,128)(2,1)S(1)} collective-permute-done((bf16[256,1024]{1,0:T(8,128)(2,1)S(1)}, bf16[256,1024]{1,0:T(8,128)(2,1)S(1)}, u32[]{:S(2)}, u32[]{:S(2)}) %collective-permute-start.6) | collective-permute-done | bytes 524320 | tf_op jit(solution)/shard_map/ppermute | solution.py:304
  41.4 0.5 add_convert_fusion.3
  42.0 0.1 broadcast_select_fusion
  42.1 0.1 collective-permute-start.12
  42.1 4.5 %collective-permute-start.15 = (bf16[256,1024]{1,0:T(8,128)(2,1)S(1)}, bf16[256,1024]{1,0:T(8,128)(2,1)S(1)}, u32[]{:S(2)}, u32[]{:S(2)}) collective-permute-start(bf16[256,1024]{1,0:T(8,128)(2,1)S(1)} %get-tuple-element.55), channel_id=1, source_target_pairs={{8,8},{16,9},{9,16},{17,17},{10,10},{18,11},{11,18},{19,19},{12,12... | collective-permute-start | bytes 1572872 | tf_op jit(solution)/shard_map/ppermute | solution.py:260
  46.6 1.3 %collective-permute-start.17 = (bf16[256,1024]{1,0:T(8,128)(2,1)S(1)}, bf16[256,1024]{1,0:T(8,128)(2,1)S(1)}, u32[]{:S(2)}, u32[]{:S(2)}) collective-permute-start(bf16[256,1024]{1,0:T(8,128)(2,1)S(1)} %get-tuple-element.55), channel_id=1, source_target_pairs={{0,8},{24,9},{1,16},{25,17},{2,10},{26,11},{3,18},{27,19},{4,12},{... | collective-permute-start | bytes 1572872 | tf_op jit(solution)/shard_map/ppermute | solution.py:261
  47.9 7.2 %collective-permute-done.12.refs_4_ = bf16[256,1024]{1,0:T(8,128)(2,1)S(1)} collective-permute-done((bf16[256,1024]{1,0:T(8,128)(2,1)S(1)}, bf16[256,1024]{1,0:T(8,128)(2,1)S(1)}, u32[]{:S(2)}, u32[]{:S(2)}) %collective-permute-start.12) | collective-permute-done | bytes 524320 | tf_op jit(solution)/shard_map/ppermute | solution.py:254
  55.1 0.4 add_convert_fusion.2
  55.5 3.6 %collective-permute-start.16 = (bf16[256,1024]{1,0:T(8,128)(2,1)S(1)}, bf16[256,1024]{1,0:T(8,128)(2,1)S(1)}, u32[]{:S(2)}, u32[]{:S(2)}) collective-permute-start(bf16[256,1024]{1,0:T(8,128)(2,1)S(1)} %add_convert_fusion.2), channel_id=1, source_target_pairs={{8,8},{16,9},{9,16},{17,17},{10,10},{18,11},{11,18},{19,19},{12,12... | collective-permute-start | bytes 1572872 | tf_op jit(solution)/shard_map/ppermute | solution.py:260
  59.1 1.3 %collective-permute-start.18 = (bf16[256,1024]{1,0:T(8,128)(2,1)S(1)}, bf16[256,1024]{1,0:T(8,128)(2,1)S(1)}, u32[]{:S(2)}, u32[]{:S(2)}) collective-permute-start(bf16[256,1024]{1,0:T(8,128)(2,1)S(1)} %add_convert_fusion.2), channel_id=1, source_target_pairs={{0,8},{24,9},{1,16},{25,17},{2,10},{26,11},{3,18},{27,19},{4,12},{... | collective-permute-start | bytes 1572872 | tf_op jit(solution)/shard_map/ppermute | solution.py:261
  60.4 0.0 collective-permute-done.15.refs_2_
  60.4 0.1 collective-permute-start.19
  60.5 4.1 %shard_map.66 = (bf16[256,1024]{1,0:T(8,128)(2,1)S(1)}, bf16[256,1024]{1,0:T(8,128)(2,1)S(1)}) custom-call(bf16[512,1024]{1,0:T(8,128)(2,1)S(1)} %bitcast.29, bf16[256,1024]{1,0:T(8,128)(2,1)S(1)} %get-tuple-element.31.refs_1_, bf16[256,1024]{1,0:T(8,128)(2,1)S(1)} %get-tuple-element.32.refs_2_, bf16[256,1024]{1,0:T(8,128)(2,1)S(1)} %get-tuple-element.56.refs_3_, ...), custom_call_target="tpu_custom_call" | custom-call | flops 2684354560 | bytes 5242880 | tf_op jit(solution)/shard_map/pallas_call | solution.py:162
  64.6 0.6 collective-permute-start.21
  65.2 2.6 %collective-permute-done.16.refs_3_ = bf16[256,1024]{1,0:T(8,128)(2,1)S(1)} collective-permute-done((bf16[256,1024]{1,0:T(8,128)(2,1)S(1)}, bf16[256,1024]{1,0:T(8,128)(2,1)S(1)}, u32[]{:S(2)}, u32[]{:S(2)}) %collective-permute-start.16) | collective-permute-done | bytes 524320 | tf_op jit(solution)/shard_map/ppermute | solution.py:260
  67.8 0.0 collective-permute-start.20
  67.8 4.1 %collective-permute-done.18.refs_5_ = bf16[256,1024]{1,0:T(8,128)(2,1)S(1)} collective-permute-done((bf16[256,1024]{1,0:T(8,128)(2,1)S(1)}, bf16[256,1024]{1,0:T(8,128)(2,1)S(1)}, u32[]{:S(2)}, u32[]{:S(2)}) %collective-permute-start.18) | collective-permute-done | bytes 524320 | tf_op jit(solution)/shard_map/ppermute | solution.py:261
  71.9 1.5 %collective-permute-start.22 = (bf16[256,1024]{1,0:T(8,128)(2,1)S(1)}, bf16[256,1024]{1,0:T(8,128)(2,1)S(1)}, u32[]{:S(2)}, u32[]{:S(2)}) collective-permute-start(bf16[256,1024]{1,0:T(8,128)(2,1)S(1)} %collective-permute-done.18.refs_5_), channel_id=1, source_target_pairs={{0,1},{1,0},{2,3},{3,2},{4,5},{5,4},{6,7},{7,6},{8,9},{9,8},{10,11... | collective-permute-start | bytes 1572872 | tf_op jit(solution)/shard_map/ppermute | solution.py:274
  73.4 3.9 %collective-permute-start.14 = (bf16[256,1024]{1,0:T(8,128)(2,1)S(1)}, bf16[256,1024]{1,0:T(8,128)(2,1)S(1)}, u32[]{:S(2)}, u32[]{:S(2)}) collective-permute-start(bf16[256,1024]{1,0:T(8,128)(2,1)S(1)} %get-tuple-element.45), channel_id=1, source_target_pairs={{16,8},{8,9},{17,16},{9,17},{18,10},{10,11},{19,18},{11,19},{20,12... | collective-permute-start | bytes 1572872 | tf_op jit(solution)/shard_map/ppermute | solution.py:276
  77.3 1.3 %collective-permute-start.13 = (bf16[256,1024]{1,0:T(8,128)(2,1)S(1)}, bf16[256,1024]{1,0:T(8,128)(2,1)S(1)}, u32[]{:S(2)}, u32[]{:S(2)}) collective-permute-start(bf16[256,1024]{1,0:T(8,128)(2,1)S(1)} %get-tuple-element.45), channel_id=1, source_target_pairs={{0,8},{24,9},{1,16},{25,17},{2,10},{26,11},{3,18},{27,19},{4,12},{... | collective-permute-start | bytes 1572872 | tf_op jit(solution)/shard_map/ppermute | solution.py:276
  78.6 0.0 collective-permute-done.21.refs_8_
  78.7 1.3 %collective-permute-start.24 = (bf16[256,1024]{1,0:T(8,128)(2,1)S(1)}, bf16[256,1024]{1,0:T(8,128)(2,1)S(1)}, u32[]{:S(2)}, u32[]{:S(2)}) collective-permute-start(bf16[256,1024]{1,0:T(8,128)(2,1)S(1)} %get-tuple-element.51), channel_id=1, source_target_pairs={{0,8},{24,9},{1,16},{25,17},{2,10},{26,11},{3,18},{27,19},{4,12},{... | collective-permute-start | bytes 1572872 | tf_op jit(solution)/shard_map/ppermute | solution.py:276
  80.0 0.0 collective-permute-done.20.refs_7_
  80.0 2.1 %collective-permute-start.25 = (bf16[256,1024]{1,0:T(8,128)(2,1)S(1)}, bf16[256,1024]{1,0:T(8,128)(2,1)S(1)}, u32[]{:S(2)}, u32[]{:S(2)}) collective-permute-start(bf16[256,1024]{1,0:T(8,128)(2,1)S(1)} %get-tuple-element.51), channel_id=1, source_target_pairs={{16,8},{8,9},{17,16},{9,17},{18,10},{10,11},{19,18},{11,19},{20,12... | collective-permute-start | bytes 1572872 | tf_op jit(solution)/shard_map/ppermute | solution.py:276
  82.1 0.0 collective-permute-done.22.refs_9_
  82.1 7.3 %shard_map.67 = (f32[256,1024]{1,0:T(8,128)S(1)}, f32[256,1024]{1,0:T(8,128)S(1)}) custom-call(s32[1,2]{1,0:T(1,128)S(1)} %bitcast.33, s32[1,2]{1,0:T(1,128)S(1)} %bitcast.34, bf16[256,1024]{1,0:T(8,128)(2,1)S(1)} %collective-permute-done.15.refs_2_, bf16[256,1024]{1,0:T(8,128)(2,1)S(1)} %collective-permute-done.16.refs_3_, ...), custom_call_target="tpu_custom_call" | custom-call | flops 5368709120 | bytes 6291472 | tf_op jit(solution)/shard_map/pallas_call | solution.py:162
  89.4 5.1 %collective-permute-done.13 = bf16[256,1024]{1,0:T(8,128)(2,1)S(1)} collective-permute-done((bf16[256,1024]{1,0:T(8,128)(2,1)S(1)}, bf16[256,1024]{1,0:T(8,128)(2,1)S(1)}, u32[]{:S(2)}, u32[]{:S(2)}) %collective-permute-start.13) | collective-permute-done | bytes 524320 | tf_op jit(solution)/shard_map/ppermute | solution.py:276
  94.4 0.2 add_convert_fusion.1
  94.7 1.8 %collective-permute-start.23 = (bf16[256,1024]{1,0:T(8,128)(2,1)S(1)}, bf16[256,1024]{1,0:T(8,128)(2,1)S(1)}, u32[]{:S(2)}, u32[]{:S(2)}) collective-permute-start(bf16[256,1024]{1,0:T(8,128)(2,1)S(1)} %add_convert_fusion.1), channel_id=1, source_target_pairs={{8,0},{9,24},{16,1},{17,25},{10,2},{11,26},{18,3},{19,27},{12,4},{... | collective-permute-start | bytes 1572872 | tf_op jit(solution)/shard_map/ppermute | solution.py:289
  96.5 7.5 %collective-permute-done.24 = bf16[256,1024]{1,0:T(8,128)(2,1)S(1)} collective-permute-done((bf16[256,1024]{1,0:T(8,128)(2,1)S(1)}, bf16[256,1024]{1,0:T(8,128)(2,1)S(1)}, u32[]{:S(2)}, u32[]{:S(2)}) %collective-permute-start.24) | collective-permute-done | bytes 524320 | tf_op jit(solution)/shard_map/ppermute | solution.py:276
  104.0 0.3 add_convert_fusion
  104.2 1.7 %collective-permute-start.26 = (bf16[256,1024]{1,0:T(8,128)(2,1)S(1)}, bf16[256,1024]{1,0:T(8,128)(2,1)S(1)}, u32[]{:S(2)}, u32[]{:S(2)}) collective-permute-start(bf16[256,1024]{1,0:T(8,128)(2,1)S(1)} %add_convert_fusion), channel_id=1, source_target_pairs={{8,0},{9,24},{16,1},{17,25},{10,2},{11,26},{18,3},{19,27},{12,4},{... | collective-permute-start | bytes 1572872 | tf_op jit(solution)/shard_map/ppermute | solution.py:289
  105.9 1.9 %collective-permute-start.27 = (bf16[256,1024]{1,0:T(8,128)(2,1)S(1)}, bf16[256,1024]{1,0:T(8,128)(2,1)S(1)}, u32[]{:S(2)}, u32[]{:S(2)}) collective-permute-start(bf16[256,1024]{1,0:T(8,128)(2,1)S(1)} %add_convert_fusion.1), channel_id=1, source_target_pairs={{8,16},{9,8},{16,17},{17,9},{10,18},{11,10},{18,19},{19,11},{12,20... | collective-permute-start | bytes 1572872 | tf_op jit(solution)/shard_map/ppermute | solution.py:289
  107.9 2.7 %collective-permute-start.28 = (bf16[256,1024]{1,0:T(8,128)(2,1)S(1)}, bf16[256,1024]{1,0:T(8,128)(2,1)S(1)}, u32[]{:S(2)}, u32[]{:S(2)}) collective-permute-start(bf16[256,1024]{1,0:T(8,128)(2,1)S(1)} %add_convert_fusion), channel_id=1, source_target_pairs={{8,16},{9,8},{16,17},{17,9},{10,18},{11,10},{18,19},{19,11},{12,20... | collective-permute-start | bytes 1572872 | tf_op jit(solution)/shard_map/ppermute | solution.py:289
  110.6 4.0 %collective-permute-done.26.refs_1_ = bf16[256,1024]{1,0:T(8,128)(2,1)S(1)} collective-permute-done((bf16[256,1024]{1,0:T(8,128)(2,1)S(1)}, bf16[256,1024]{1,0:T(8,128)(2,1)S(1)}, u32[]{:S(2)}, u32[]{:S(2)}) %collective-permute-start.26) | collective-permute-done | bytes 524320 | tf_op jit(solution)/shard_map/ppermute | solution.py:289
  114.6 4.3 %collective-permute-done.27.refs_2_ = bf16[256,1024]{1,0:T(8,128)(2,1)S(1)} collective-permute-done((bf16[256,1024]{1,0:T(8,128)(2,1)S(1)}, bf16[256,1024]{1,0:T(8,128)(2,1)S(1)}, u32[]{:S(2)}, u32[]{:S(2)}) %collective-permute-start.27) | collective-permute-done | bytes 524320 | tf_op jit(solution)/shard_map/ppermute | solution.py:289
  118.9 5.6 %collective-permute-done.28.refs_3_ = bf16[256,1024]{1,0:T(8,128)(2,1)S(1)} collective-permute-done((bf16[256,1024]{1,0:T(8,128)(2,1)S(1)}, bf16[256,1024]{1,0:T(8,128)(2,1)S(1)}, u32[]{:S(2)}, u32[]{:S(2)}) %collective-permute-start.28) | collective-permute-done | bytes 524320 | tf_op jit(solution)/shard_map/ppermute | solution.py:289
  124.5 1.0 shard_map.68
  (17 shorter events, 0.1 us)
Async XLA Ops:
  0.7 12.9 %copy-start = (bf16[1,1,512,1024]{3,2,1,0:T(8,128)(2,1)S(1)}, bf16[1,1,512,1024]{3,2,1,0:T(8,128)(2,1)}, u32[]{:S(2)}) copy-start(bf16[1,1,512,1024]{3,2,1,0:T(8,128)(2,1)} %param.10) | copy-start | bytes 3145732
  1.9 11.8 %copy-start.1 = (bf16[2,1,1,256,512]{4,3,2,1,0:T(8,128)(2,1)S(1)}, bf16[2,1,1,256,512]{4,3,2,1,0:T(8,128)(2,1)}, u32[]{:S(2)}) copy-start(bf16[2,1,1,256,512]{4,3,2,1,0:T(8,128)(2,1)} %param.8) | copy-start | bytes 1572868
  1.9 1.3 %copy-start.3 = (s32[1,2]{1,0:T(1,128)S(1)}, s32[1,2]{1,0:T(1,128)}, u32[]{:S(2)}) copy-start(s32[1,2]{1,0:T(1,128)} %param.11) | copy-start | bytes 28
  1.9 8.4 %collective-permute-start.1 = (bf16[144,1024]{1,0:T(8,128)(2,1)S(1)}, bf16[144,1024]{1,0:T(8,128)(2,1)S(1)}, u32[]{:S(2)}, u32[]{:S(2)}) collective-permute-start(bf16[144,1024]{1,0:T(8,128)(2,1)S(1)} %pad_maximum_fusion.refs_0_), channel_id=1, source_target_pairs={{0,2},{1,3},{2,0},{3,1},{4,6},{5,7},{6,4},{7,5},{8,10},{9,11},{10,... | collective-permute-start | bytes 884744 | tf_op jit(solution)/shard_map/ppermute | solution.py:224
  3.2 5.8 %collective-permute-start.2 = (s32[2]{0:T(128)S(1)}, s32[2]{0:T(128)S(1)}, u32[]{:S(2)}, u32[]{:S(2)}) collective-permute-start(s32[2]{0:T(128)S(1)} %bitcast.35), channel_id=1, source_target_pairs={{0,4},{4,0},{8,12},{12,8},{16,20},{20,16},{24,28},{28,24},{1,5},{5... | collective-permute-start | bytes 32 | tf_op jit(solution)/shard_map/ppermute | solution.py:208
  4.4 5.9 %collective-permute-start.3 = (s32[2]{0:T(128)S(1)}, s32[2]{0:T(128)S(1)}, u32[]{:S(2)}, u32[]{:S(2)}) collective-permute-start(s32[2]{0:T(128)S(1)} %bitcast.36), channel_id=1, source_target_pairs={{0,8},{24,9},{1,16},{25,17},{2,10},{26,11},{3,18},{27,19},{4,12},{... | collective-permute-start | bytes 32 | tf_op jit(solution)/shard_map/ppermute | solution.py:210
  5.7 4.6 %collective-permute-start.4 = (s32[2]{0:T(128)S(1)}, s32[2]{0:T(128)S(1)}, u32[]{:S(2)}, u32[]{:S(2)}) collective-permute-start(s32[2]{0:T(128)S(1)} %bitcast.37), channel_id=1, source_target_pairs={{16,8},{8,9},{17,16},{9,17},{18,10},{10,11},{19,18},{11,19},{20,12... | collective-permute-start | bytes 32 | tf_op jit(solution)/shard_map/ppermute | solution.py:211
  8.9 3.9 %collective-permute-start = (bf16[144,1024]{1,0:T(8,128)(2,1)S(1)}, bf16[144,1024]{1,0:T(8,128)(2,1)S(1)}, u32[]{:S(2)}, u32[]{:S(2)}) collective-permute-start(bf16[144,1024]{1,0:T(8,128)(2,1)S(1)} %pad_maximum_fusion.refs_0_), channel_id=1, source_target_pairs={{0,1},{1,0},{2,3},{3,2},{4,5},{5,4},{6,7},{7,6},{8,9},{9,8},{10,11... | collective-permute-start | bytes 884744 | tf_op jit(solution)/shard_map/ppermute | solution.py:224
  10.4 3.2 %collective-permute-start.5 = (bf16[144,1024]{1,0:T(8,128)(2,1)S(1)}, bf16[144,1024]{1,0:T(8,128)(2,1)S(1)}, u32[]{:S(2)}, u32[]{:S(2)}) collective-permute-start(bf16[144,1024]{1,0:T(8,128)(2,1)S(1)} %collective-permute-done.1.refs_2_), channel_id=1, source_target_pairs={{0,1},{1,0},{2,3},{3,2},{4,5},{5,4},{6,7},{7,6},{8,9},{9,8},{10,11... | collective-permute-start | bytes 884744 | tf_op jit(solution)/shard_map/ppermute | solution.py:224
  12.4 8.7 %collective-permute-start.9 = (bf16[144,1024]{1,0:T(8,128)(2,1)S(1)}, bf16[144,1024]{1,0:T(8,128)(2,1)S(1)}, u32[]{:S(2)}, u32[]{:S(2)}) collective-permute-start(bf16[144,1024]{1,0:T(8,128)(2,1)S(1)} %pad_maximum_fusion.1.refs_0_), channel_id=1, source_target_pairs={{0,2},{1,3},{2,0},{3,1},{4,6},{5,7},{6,4},{7,5},{8,10},{9,11},{10,... | collective-permute-start | bytes 884744 | tf_op jit(solution)/shard_map/ppermute | solution.py:224
  15.4 14.1 %collective-permute-start.7 = (bf16[256,1024]{1,0:T(8,128)(2,1)S(1)}, bf16[256,1024]{1,0:T(8,128)(2,1)S(1)}, u32[]{:S(2)}, u32[]{:S(2)}) collective-permute-start(bf16[256,1024]{1,0:T(8,128)(2,1)S(1)} %get-tuple-element.33), channel_id=1, source_target_pairs={{28,0},{0,4},{4,8},{8,12},{12,16},{16,20},{20,24},{24,28},{29,1},{... | collective-permute-start | bytes 1572872 | tf_op jit(solution)/shard_map/ppermute | solution.py:304
  15.8 13.7 %collective-permute-start.11 = (bf16[256,1024]{1,0:T(8,128)(2,1)S(1)}, bf16[256,1024]{1,0:T(8,128)(2,1)S(1)}, u32[]{:S(2)}, u32[]{:S(2)}) collective-permute-start(bf16[256,1024]{1,0:T(8,128)(2,1)S(1)} %get-tuple-element.38), channel_id=1, source_target_pairs={{0,24},{4,12},{8,0},{12,20},{16,8},{20,28},{24,16},{28,4},{1,25},{... | collective-permute-start | bytes 1572872 | tf_op jit(solution)/shard_map/ppermute | solution.py:241
  16.0 25.5 %collective-permute-start.6 = (bf16[256,1024]{1,0:T(8,128)(2,1)S(1)}, bf16[256,1024]{1,0:T(8,128)(2,1)S(1)}, u32[]{:S(2)}, u32[]{:S(2)}) collective-permute-start(bf16[256,1024]{1,0:T(8,128)(2,1)S(1)} %get-tuple-element.33), channel_id=1, source_target_pairs={{4,0},{8,4},{12,8},{16,12},{20,16},{24,20},{28,24},{0,28},{5,1},{9... | collective-permute-start | bytes 1572872 | tf_op jit(solution)/shard_map/ppermute | solution.py:304
  18.3 3.7 %collective-permute-start.8 = (bf16[144,1024]{1,0:T(8,128)(2,1)S(1)}, bf16[144,1024]{1,0:T(8,128)(2,1)S(1)}, u32[]{:S(2)}, u32[]{:S(2)}) collective-permute-start(bf16[144,1024]{1,0:T(8,128)(2,1)S(1)} %pad_maximum_fusion.1.refs_0_), channel_id=1, source_target_pairs={{0,1},{1,0},{2,3},{3,2},{4,5},{5,4},{6,7},{7,6},{8,9},{9,8},{10,11... | collective-permute-start | bytes 884744 | tf_op jit(solution)/shard_map/ppermute | solution.py:224
  21.1 2.0 %collective-permute-start.10 = (bf16[144,1024]{1,0:T(8,128)(2,1)S(1)}, bf16[144,1024]{1,0:T(8,128)(2,1)S(1)}, u32[]{:S(2)}, u32[]{:S(2)}) collective-permute-start(bf16[144,1024]{1,0:T(8,128)(2,1)S(1)} %collective-permute-done.9.refs_2_), channel_id=1, source_target_pairs={{0,1},{1,0},{2,3},{3,2},{4,5},{5,4},{6,7},{7,6},{8,9},{9,8},{10,11... | collective-permute-start | bytes 884744 | tf_op jit(solution)/shard_map/ppermute | solution.py:224
  42.1 13.1 %collective-permute-start.12 = (bf16[256,1024]{1,0:T(8,128)(2,1)S(1)}, bf16[256,1024]{1,0:T(8,128)(2,1)S(1)}, u32[]{:S(2)}, u32[]{:S(2)}) collective-permute-start(bf16[256,1024]{1,0:T(8,128)(2,1)S(1)} %broadcast_select_fusion), channel_id=1, source_target_pairs={{0,4},{4,0},{8,12},{12,8},{16,20},{20,16},{24,28},{28,24},{1,5},{5... | collective-permute-start | bytes 1572872 | tf_op jit(solution)/shard_map/ppermute | solution.py:254
  42.1 18.3 %collective-permute-start.15 = (bf16[256,1024]{1,0:T(8,128)(2,1)S(1)}, bf16[256,1024]{1,0:T(8,128)(2,1)S(1)}, u32[]{:S(2)}, u32[]{:S(2)}) collective-permute-start(bf16[256,1024]{1,0:T(8,128)(2,1)S(1)} %get-tuple-element.55), channel_id=1, source_target_pairs={{8,8},{16,9},{9,16},{17,17},{10,10},{18,11},{11,18},{19,19},{12,12... | collective-permute-start | bytes 1572872 | tf_op jit(solution)/shard_map/ppermute | solution.py:260
  46.6 18.0 %collective-permute-start.17 = (bf16[256,1024]{1,0:T(8,128)(2,1)S(1)}, bf16[256,1024]{1,0:T(8,128)(2,1)S(1)}, u32[]{:S(2)}, u32[]{:S(2)}) collective-permute-start(bf16[256,1024]{1,0:T(8,128)(2,1)S(1)} %get-tuple-element.55), channel_id=1, source_target_pairs={{0,8},{24,9},{1,16},{25,17},{2,10},{26,11},{3,18},{27,19},{4,12},{... | collective-permute-start | bytes 1572872 | tf_op jit(solution)/shard_map/ppermute | solution.py:261
  55.1 5.4 %copy-start.2 = (bf16[1,1,512,1024]{3,2,1,0:T(8,128)(2,1)S(1)}, bf16[1,1,512,1024]{3,2,1,0:T(8,128)(2,1)}, u32[]{:S(2)}) copy-start(bf16[1,1,512,1024]{3,2,1,0:T(8,128)(2,1)} %param.9) | copy-start | bytes 3145732
  55.5 12.3 %collective-permute-start.16 = (bf16[256,1024]{1,0:T(8,128)(2,1)S(1)}, bf16[256,1024]{1,0:T(8,128)(2,1)S(1)}, u32[]{:S(2)}, u32[]{:S(2)}) collective-permute-start(bf16[256,1024]{1,0:T(8,128)(2,1)S(1)} %add_convert_fusion.2), channel_id=1, source_target_pairs={{8,8},{16,9},{9,16},{17,17},{10,10},{18,11},{11,18},{19,19},{12,12... | collective-permute-start | bytes 1572872 | tf_op jit(solution)/shard_map/ppermute | solution.py:260
  59.1 12.8 %collective-permute-start.18 = (bf16[256,1024]{1,0:T(8,128)(2,1)S(1)}, bf16[256,1024]{1,0:T(8,128)(2,1)S(1)}, u32[]{:S(2)}, u32[]{:S(2)}) collective-permute-start(bf16[256,1024]{1,0:T(8,128)(2,1)S(1)} %add_convert_fusion.2), channel_id=1, source_target_pairs={{0,8},{24,9},{1,16},{25,17},{2,10},{26,11},{3,18},{27,19},{4,12},{... | collective-permute-start | bytes 1572872 | tf_op jit(solution)/shard_map/ppermute | solution.py:261
  60.4 16.9 %collective-permute-start.19 = (bf16[256,1024]{1,0:T(8,128)(2,1)S(1)}, bf16[256,1024]{1,0:T(8,128)(2,1)S(1)}, u32[]{:S(2)}, u32[]{:S(2)}) collective-permute-start(bf16[256,1024]{1,0:T(8,128)(2,1)S(1)} %collective-permute-done.15.refs_2_), channel_id=1, source_target_pairs={{0,1},{1,0},{2,3},{3,2},{4,5},{5,4},{6,7},{7,6},{8,9},{9,8},{10,11... | collective-permute-start | bytes 1572872 | tf_op jit(solution)/shard_map/ppermute | solution.py:273
  64.6 14.0 %collective-permute-start.21 = (bf16[256,1024]{1,0:T(8,128)(2,1)S(1)}, bf16[256,1024]{1,0:T(8,128)(2,1)S(1)}, u32[]{:S(2)}, u32[]{:S(2)}) collective-permute-start(bf16[256,1024]{1,0:T(8,128)(2,1)S(1)} %collective-permute-done.17.refs_4_), channel_id=1, source_target_pairs={{0,1},{1,0},{2,3},{3,2},{4,5},{5,4},{6,7},{7,6},{8,9},{9,8},{10,11... | collective-permute-start | bytes 1572872 | tf_op jit(solution)/shard_map/ppermute | solution.py:274
  67.8 12.2 %collective-permute-start.20 = (bf16[256,1024]{1,0:T(8,128)(2,1)S(1)}, bf16[256,1024]{1,0:T(8,128)(2,1)S(1)}, u32[]{:S(2)}, u32[]{:S(2)}) collective-permute-start(bf16[256,1024]{1,0:T(8,128)(2,1)S(1)} %collective-permute-done.16.refs_3_), channel_id=1, source_target_pairs={{0,1},{1,0},{2,3},{3,2},{4,5},{5,4},{6,7},{7,6},{8,9},{9,8},{10,11... | collective-permute-start | bytes 1572872 | tf_op jit(solution)/shard_map/ppermute | solution.py:273
  71.9 10.2 %collective-permute-start.22 = (bf16[256,1024]{1,0:T(8,128)(2,1)S(1)}, bf16[256,1024]{1,0:T(8,128)(2,1)S(1)}, u32[]{:S(2)}, u32[]{:S(2)}) collective-permute-start(bf16[256,1024]{1,0:T(8,128)(2,1)S(1)} %collective-permute-done.18.refs_5_), channel_id=1, source_target_pairs={{0,1},{1,0},{2,3},{3,2},{4,5},{5,4},{6,7},{7,6},{8,9},{9,8},{10,11... | collective-permute-start | bytes 1572872 | tf_op jit(solution)/shard_map/ppermute | solution.py:274
  73.4 16.0 %collective-permute-start.14 = (bf16[256,1024]{1,0:T(8,128)(2,1)S(1)}, bf16[256,1024]{1,0:T(8,128)(2,1)S(1)}, u32[]{:S(2)}, u32[]{:S(2)}) collective-permute-start(bf16[256,1024]{1,0:T(8,128)(2,1)S(1)} %get-tuple-element.45), channel_id=1, source_target_pairs={{16,8},{8,9},{17,16},{9,17},{18,10},{10,11},{19,18},{11,19},{20,12... | collective-permute-start | bytes 1572872 | tf_op jit(solution)/shard_map/ppermute | solution.py:276
  77.3 17.1 %collective-permute-start.13 = (bf16[256,1024]{1,0:T(8,128)(2,1)S(1)}, bf16[256,1024]{1,0:T(8,128)(2,1)S(1)}, u32[]{:S(2)}, u32[]{:S(2)}) collective-permute-start(bf16[256,1024]{1,0:T(8,128)(2,1)S(1)} %get-tuple-element.45), channel_id=1, source_target_pairs={{0,8},{24,9},{1,16},{25,17},{2,10},{26,11},{3,18},{27,19},{4,12},{... | collective-permute-start | bytes 1572872 | tf_op jit(solution)/shard_map/ppermute | solution.py:276
  78.7 25.3 %collective-permute-start.24 = (bf16[256,1024]{1,0:T(8,128)(2,1)S(1)}, bf16[256,1024]{1,0:T(8,128)(2,1)S(1)}, u32[]{:S(2)}, u32[]{:S(2)}) collective-permute-start(bf16[256,1024]{1,0:T(8,128)(2,1)S(1)} %get-tuple-element.51), channel_id=1, source_target_pairs={{0,8},{24,9},{1,16},{25,17},{2,10},{26,11},{3,18},{27,19},{4,12},{... | collective-permute-start | bytes 1572872 | tf_op jit(solution)/shard_map/ppermute | solution.py:276
  80.0 24.0 %collective-permute-start.25 = (bf16[256,1024]{1,0:T(8,128)(2,1)S(1)}, bf16[256,1024]{1,0:T(8,128)(2,1)S(1)}, u32[]{:S(2)}, u32[]{:S(2)}) collective-permute-start(bf16[256,1024]{1,0:T(8,128)(2,1)S(1)} %get-tuple-element.51), channel_id=1, source_target_pairs={{16,8},{8,9},{17,16},{9,17},{18,10},{10,11},{19,18},{11,19},{20,12... | collective-permute-start | bytes 1572872 | tf_op jit(solution)/shard_map/ppermute | solution.py:276
  94.7 15.9 %collective-permute-start.23 = (bf16[256,1024]{1,0:T(8,128)(2,1)S(1)}, bf16[256,1024]{1,0:T(8,128)(2,1)S(1)}, u32[]{:S(2)}, u32[]{:S(2)}) collective-permute-start(bf16[256,1024]{1,0:T(8,128)(2,1)S(1)} %add_convert_fusion.1), channel_id=1, source_target_pairs={{8,0},{9,24},{16,1},{17,25},{10,2},{11,26},{18,3},{19,27},{12,4},{... | collective-permute-start | bytes 1572872 | tf_op jit(solution)/shard_map/ppermute | solution.py:289
  104.2 10.4 %collective-permute-start.26 = (bf16[256,1024]{1,0:T(8,128)(2,1)S(1)}, bf16[256,1024]{1,0:T(8,128)(2,1)S(1)}, u32[]{:S(2)}, u32[]{:S(2)}) collective-permute-start(bf16[256,1024]{1,0:T(8,128)(2,1)S(1)} %add_convert_fusion), channel_id=1, source_target_pairs={{8,0},{9,24},{16,1},{17,25},{10,2},{11,26},{18,3},{19,27},{12,4},{... | collective-permute-start | bytes 1572872 | tf_op jit(solution)/shard_map/ppermute | solution.py:289
  105.9 12.9 %collective-permute-start.27 = (bf16[256,1024]{1,0:T(8,128)(2,1)S(1)}, bf16[256,1024]{1,0:T(8,128)(2,1)S(1)}, u32[]{:S(2)}, u32[]{:S(2)}) collective-permute-start(bf16[256,1024]{1,0:T(8,128)(2,1)S(1)} %add_convert_fusion.1), channel_id=1, source_target_pairs={{8,16},{9,8},{16,17},{17,9},{10,18},{11,10},{18,19},{19,11},{12,20... | collective-permute-start | bytes 1572872 | tf_op jit(solution)/shard_map/ppermute | solution.py:289
  107.9 16.6 %collective-permute-start.28 = (bf16[256,1024]{1,0:T(8,128)(2,1)S(1)}, bf16[256,1024]{1,0:T(8,128)(2,1)S(1)}, u32[]{:S(2)}, u32[]{:S(2)}) collective-permute-start(bf16[256,1024]{1,0:T(8,128)(2,1)S(1)} %add_convert_fusion), channel_id=1, source_target_pairs={{8,16},{9,8},{16,17},{17,9},{10,18},{11,10},{18,19},{19,11},{12,20... | collective-permute-start | bytes 1572872 | tf_op jit(solution)/shard_map/ppermute | solution.py:289

commit v5 on v4

--- a/solution.py
+++ b/solution.py
@@ -12,9 +12,6 @@
 CHUNKS = 2
 BLOCKS = 2
 DIRECT = 1
-X_LATE = True
-NS_LATE = False
-B_LATE = False
 VMEM_LIMIT = 32 * 1024 * 1024
 
 coef_a = 3.4445
@@ -49,6 +46,11 @@
     return jnp.concatenate([(part * scale).astype(jnp.bfloat16) for part in tracked], axis=0)
 
 
+def row_parts(blocks):
+    ends = [sum(b.shape[0] for b in blocks[: k + 1]) for k in range(len(blocks))]
+    return [slice(end - b.shape[0], end) for b, end in zip(blocks, ends)]
+
+
 def first_step_kernel(chunks, *refs):
     offset, grads, partners = refs[0], refs[1 : 1 + chunks], refs[1 + chunks : 1 + 2 * chunks]
     weight, blocks = refs[1 + 2 * chunks], refs[2 + 2 * chunks :]
@@ -59,9 +61,7 @@
         own = offset[part, :].astype(jnp.float32) + grads[k][...].astype(jnp.float32)
         tracked.append(0.5 * (own + partners[k][...].astype(jnp.float32)))
     (ortho,) = newton_schulz(normalized(tracked))
-    rows = blocks[0].shape[0]
-    for k, block in enumerate(blocks):
-        part = slice(k * rows, (k + 1) * rows)
+    for part, block in zip(row_parts(blocks), blocks):
         value = weight[part, :].astype(jnp.float32) - step_scale * ortho[part, :].astype(jnp.float32)
         block[...] = value.astype(block.dtype)
 
@@ -83,17 +83,14 @@
         starts.append(normalized(tracked))
     first, second = newton_schulz(*starts)
     total = -0.5 * step_scale * (first.astype(jnp.float32) + second.astype(jnp.float32))
-    rows = blocks[0].shape[0]
-    for k, block in enumerate(blocks):
-        block[...] = total[k * rows : (k + 1) * rows, :]
+    for part, block in zip(row_parts(blocks), blocks):
+        block[...] = total[part, :]
 
 
 def last_kernel(blocks, *refs):
     first, second, out, buffer, semaphores = refs[:blocks], refs[blocks : 2 * blocks], *refs[2 * blocks :]
-    rows = first[0].shape[0]
     copies = []
-    for k in range(blocks):
-        part = pl.ds(k * rows, rows)
+    for k, part in enumerate(row_parts(first)):
         buffer[part, :] = first[k][...] + second[k][...]
         copies.append(pltpu.make_async_copy(buffer.at[part], out.at[0, 0, part], semaphores.at[k]))
         copies[-1].start()
@@ -139,33 +136,19 @@
 
 def call(kernel, operands, out_shapes, flops):
     arrays = [a[0] if isinstance(a, tuple) else a for a in operands]
-    fetched = {i: a[1] for i, a in enumerate(operands) if isinstance(a, tuple)}
-    shapes = [a.shape if fetched.get(i) is None else a.shape[1:] for i, a in enumerate(arrays)]
-    count, results, copied = len(arrays), len(out_shapes), list(fetched)
+    picks = [a[1] if isinstance(a, tuple) else None for a in operands]
+    count = len(arrays)
 
     def body(*refs):
-        sources, targets = list(refs[:count]), refs[count : count + results]
-        copies = []
-        for n, i in enumerate(copied):
-            source = sources[i] if fetched[i] is None else sources[i].at[fetched[i]]
-            buffer = refs[count + results + n]
-            copies.append(pltpu.make_async_copy(source, buffer, refs[-1].at[n]))
-            sources[i] = buffer
-        for copy in copies:
-            copy.start()
-        for copy in copies:
-            copy.wait()
-        kernel(*sources, *targets)
-
-    moved = sum(math.prod(s) * a.dtype.itemsize for s, a in zip(shapes, arrays))
-    moved += sum(math.prod(s.shape) * s.dtype.itemsize for s in out_shapes)
+        sources = [r if p is None else r.at[p] for r, p in zip(refs[:count], picks)]
+        kernel(*sources, *refs[count:])
+
+    moved = sum(math.prod(a.shape) * a.dtype.itemsize for a in [*arrays, *out_shapes])
     return pl.pallas_call(
         body,
-        in_specs=[ANY if i in fetched else VMEM for i in range(count)],
-        out_specs=[VMEM] * results,
+        in_specs=[VMEM] * count,
+        out_specs=[VMEM] * len(out_shapes),
         out_shape=out_shapes,
-        scratch_shapes=[pltpu.VMEM(shapes[i], arrays[i].dtype) for i in copied]
-        + [pltpu.SemaphoreType.DMA((max(1, len(copied)),))],
         compiler_params=pltpu.CompilerParams(vmem_limit_bytes=VMEM_LIMIT),
         cost_estimate=pl.CostEstimate(flops=flops, bytes_accessed=moved, transcendentals=0),
     )(*arrays)
@@ -215,30 +198,33 @@
     named = jnp.pad(named, ((0, 0), (0, 15), (0, features - count)))
     gathered = [{0: jnp.concatenate([tokens[k], named[k]], axis=0)} for k in range(steps)]
     top = experts // 2
-    for k in range(steps):
-        level = top
-        if k > 0:
-            gathered[k][0] = after(gathered[k][0], gathered[k - 1][top])
-        while level >= 1:
-            hop = [(e, e ^ level) for e in range(experts)]
-            gathered[k].update({j ^ level: lax.ppermute(t, "expert", hop) for j, t in gathered[k].items()})
-            if k == 0 and level == top:
-                gathered[k][top], (send_own, first_bits, second_bits) = lax.optimization_barrier(
-                    (gathered[k][top], (send_own, first_bits, second_bits))
-                )
-            level //= 2
+
+    def spread(kept, level):
+        hop = [(e, e ^ level) for e in range(experts)]
+        kept.update({j ^ level: lax.ppermute(t, "expert", hop) for j, t in kept.items()})
+
+    spread(gathered[0], top)
+    gathered[0][top], (send_own, first_bits, second_bits) = lax.optimization_barrier(
+        (gathered[0][top], (send_own, first_bits, second_bits))
+    )
+    gathered[1][0] = after(gathered[1][0], gathered[0][top])
+    spread(gathered[1], top)
+    if top > 1:
+        spread(gathered[0], 1)
 
     edges = [fan_rows // 16 * i // CHUNKS * 16 for i in range(CHUNKS)] + [fan_rows]
     parts = [slice(low, high) for low, high in zip(edges, edges[1:])]
     chunk = [jax.ShapeDtypeStruct((p.stop - p.start, features), jnp.bfloat16) for p in parts]
-    whole = [jax.ShapeDtypeStruct((fan_rows, features), jnp.bfloat16)]
     cost = 2 * fan_rows * features * experts * count
-    operands = [gathered[0][j] for j in range(experts)] + [(stashed, 0), (offset, None)]
+    operands = [gathered[0][j] for j in range(experts)] + [(stashed, 0), offset]
     made = call(functools.partial(gradient_kernel, experts, True), operands, chunk * 2, cost)
     first, own = made[:CHUNKS], list(made[CHUNKS:])
     ahead = [from_behind(o, "site", -1) for o in own[:DIRECT]]
     behind = [from_behind(o, "site", 1) for o in own[:DIRECT]]
     fetched = [lax.ppermute(o, "site", helpers) for o in own[DIRECT:]]
+    if top > 1:
+        gathered[1][top] = after(gathered[1][top], made[0])
+        spread(gathered[1], 1)
     operands = [gathered[1][j] for j in range(experts)] + [(stashed, 1)]
     last = call(functools.partial(gradient_kernel, experts, False), operands, chunk, cost)
 
@@ -249,7 +235,7 @@
             partners.append(jnp.where(use_ahead, ahead[i], after(behind[i], last[0])))
         else:
             arrived = after(fetched[i - DIRECT], last[0])
-            if i == DIRECT and i > 0 and X_LATE:
+            if i == DIRECT and i > 0:
                 arrived = after(arrived, partners[-1])
             partners.append(lax.ppermute(jnp.where(send_own, own[i], arrived), "site", beside))
         partner = partners[i] if i == 0 else after(partners[i], second[i - 1])
@@ -261,24 +247,26 @@
         here1.append(lax.ppermute(second[i], both, outer))
 
     cost = NS_ITERS * 2 * (2 * fan_rows * fan_rows * features + fan_rows**3)
-    held = after(partners[-1], (second[-1], here0[0]) if NS_LATE else second[-1])
-    rows = fan_rows // BLOCKS
+    there0 = [lax.ppermute(h, "expert", mates) for h in here0[:-1]]
+    there1 = [lax.ppermute(h, "expert", mates) for h in here1[:-1]]
+    held = after(partners[-1], second[-1])
+    sizes = [fan_rows // BLOCKS] * BLOCKS
     moved = call(
         functools.partial(first_step_kernel, CHUNKS),
-        [(offset, None), *first, *partners[:-1], held, (weight, None)],
-        [jax.ShapeDtypeStruct((rows, features), jnp.bfloat16)] * BLOCKS,
+        [offset, *first, *partners[:-1], held, weight],
+        [jax.ShapeDtypeStruct((rows, features), jnp.bfloat16) for rows in sizes],
         cost,
     )
     here0[-1] = after(here0[-1], moved)
-    there0 = [lax.ppermute(h, "expert", mates) for h in here0]
-    there1 = [lax.ppermute(h, "expert", mates) for h in here1]
-    lent = [after(m, (here0[-1], here1[-1]) if B_LATE else second[-1]) for m in moved]
+    there0.append(lax.ppermute(here0[-1], "expert", mates))
+    there1.append(lax.ppermute(here1[-1], "expert", mates))
+    lent = [after(m, (here0[-1], here1[-1])) for m in moved]
     pairs = [(lax.ppermute(v, both, outer), lax.ppermute(v, both, matched)) for v in lent]
 
     update = call(
         functools.partial(second_step_kernel, CHUNKS),
         [first_bits, second_bits, *here0, *here1, *there0, *there1],
-        [jax.ShapeDtypeStruct((rows, features), jnp.float32)] * BLOCKS,
+        [jax.ShapeDtypeStruct((rows, features), jnp.float32) for rows in sizes],
         2 * cost,
     )
     results = []

time: 126 us -> 126 us (level)
  no operation moved by 1% of the time
where the time goes in v5:
time: 126 us
  waiting for transfers between devices  62 us (49%)
  starting transfers between devices  43.9 us (35%)
  Pallas kernels  15.8 us (13%)
  other arithmetic  2.21 us (2%)
    ppermute x2, waiting for transfers between devices, from_behind(): return lax.ppermute(block, axis, route)  16.6 us
    pallas_call x4, Pallas kernels, call(): pl.pallas_call(body, in_specs=[VMEM] * count, out_specs=[VMEM] * len(out_...  14.8 us
    ppermute x2, waiting for transfers between devices, paired(): lax.ppermute(v, both, outer)  12.6 us
    ppermute x2, waiting for transfers between devices, paired(): lax.ppermute(r, both, to_matched)  9.9 us
    ppermute x2, starting transfers between devices, paired(): here0.append(lax.ppermute(second[i], both, middle))  8.04 us
    ppermute x1, waiting for transfers between devices, paired(): lax.ppermute(jnp.where(send_own, own[i], arrived), 'site', beside)  7.21 us
    ppermute x2, starting transfers between devices, paired(): lax.ppermute(v, both, matched)  6.04 us
    ppermute x6, starting transfers between devices, spread(): lax.ppermute(t, 'expert', hop)  5.74 us
  transfers between devices with their start and end apart: 29, of which 14 were waited for; matrix products, arithmetic and copies ran while one was open for 1% of the time, Pallas kernels for 12%

profile of v5, /device:TPU:9, one launch (start us, length us, event | category | flops | bytes accessed | tf_op | source)
XLA Modules:
  0.0 125.6 jit_solution(13450519494262551687)
XLA Ops:
  0.0 0.7 convert_bitcast_fusion
  0.7 1.2 slice_bitcast_fusion
  1.9 0.0 copy-start.1
  1.9 0.0 copy-start.3
  1.9 1.3 %collective-permute-start.1 = (bf16[144,1024]{1,0:T(8,128)(2,1)S(1)}, bf16[144,1024]{1,0:T(8,128)(2,1)S(1)}, u32[]{:S(2)}, u32[]{:S(2)}) collective-permute-start(bf16[144,1024]{1,0:T(8,128)(2,1)S(1)} %pad_maximum_fusion.refs_0_), channel_id=1, source_target_pairs={{0,2},{1,3},{2,0},{3,1},{4,6},{5,7},{6,4},{7,5},{8,10},{9,11},{10,... | collective-permute-start | bytes 884744 | tf_op jit(solution)/shard_map/ppermute | solution.py:204
  3.2 1.2 collective-permute-start.2
  4.4 1.3 %collective-permute-start.3 = (s32[2]{0:T(128)S(1)}, s32[2]{0:T(128)S(1)}, u32[]{:S(2)}, u32[]{:S(2)}) collective-permute-start(s32[2]{0:T(128)S(1)} %bitcast.36), channel_id=1, source_target_pairs={{0,8},{24,9},{1,16},{25,17},{2,10},{26,11},{3,18},{27,19},{4,12},{... | collective-permute-start | bytes 32 | tf_op jit(solution)/shard_map/ppermute | solution.py:193
  5.7 3.2 %collective-permute-start.4 = (s32[2]{0:T(128)S(1)}, s32[2]{0:T(128)S(1)}, u32[]{:S(2)}, u32[]{:S(2)}) collective-permute-start(s32[2]{0:T(128)S(1)} %bitcast.37), channel_id=1, source_target_pairs={{16,8},{8,9},{17,16},{9,17},{18,10},{10,11},{19,18},{11,19},{20,12... | collective-permute-start | bytes 32 | tf_op jit(solution)/shard_map/ppermute | solution.py:194
  8.9 0.1 collective-permute-start
  9.1 1.3 %collective-permute-done.3 = s32[2]{0:T(128)S(1)} collective-permute-done((s32[2]{0:T(128)S(1)}, s32[2]{0:T(128)S(1)}, u32[]{:S(2)}, u32[]{:S(2)}) %collective-permute-start.3) | collective-permute-done | bytes 40 | tf_op jit(solution)/shard_map/ppermute | solution.py:193
  10.3 0.0 collective-permute-done.4
  10.4 2.0 %collective-permute-start.5 = (bf16[144,1024]{1,0:T(8,128)(2,1)S(1)}, bf16[144,1024]{1,0:T(8,128)(2,1)S(1)}, u32[]{:S(2)}, u32[]{:S(2)}) collective-permute-start(bf16[144,1024]{1,0:T(8,128)(2,1)S(1)} %collective-permute-done.1.refs_2_), channel_id=1, source_target_pairs={{0,1},{1,0},{2,3},{3,2},{4,5},{5,4},{6,7},{7,6},{8,9},{9,8},{10,11... | collective-permute-start | bytes 884744 | tf_op jit(solution)/shard_map/ppermute | solution.py:204
  12.4 0.4 collective-permute-start.9
  12.8 0.0 collective-permute-done.refs_1_
  12.8 0.8 collective-permute-done.5.refs_3_
  13.6 1.7 %shard_map.64 = (bf16[256,1024]{1,0:T(8,128)(2,1)S(1)}, bf16[256,1024]{1,0:T(8,128)(2,1)S(1)}, bf16[256,1024]{1,0:T(8,128)(2,1)S(1)}, bf16[256,1024]{1,0:T(8,128)(2,1)S(1)}) custom-call(bf16[144,1024]{1,0:T(8,128)(2,1)S(1)} %pad_maximum_fusion.refs_0_, bf16[144,1024]{1,0:T(8,128)(2,1)S(1)} %collective-permute-done.refs_1_, ...), custom_call_target="tpu_custom_call" | custom-call | flops 536870912 | bytes 4849664 | tf_op jit(solution)/shard_map/pallas_call | solution.py:147
  15.3 0.4 collective-permute-start.7
  15.7 0.2 collective-permute-start.11
  15.9 2.3 %collective-permute-start.6 = (bf16[256,1024]{1,0:T(8,128)(2,1)S(1)}, bf16[256,1024]{1,0:T(8,128)(2,1)S(1)}, u32[]{:S(2)}, u32[]{:S(2)}) collective-permute-start(bf16[256,1024]{1,0:T(8,128)(2,1)S(1)} %get-tuple-element.34), channel_id=1, source_target_pairs={{4,0},{8,4},{12,8},{16,12},{20,16},{24,20},{28,24},{0,28},{5,1},{9... | collective-permute-start | bytes 1572872 | tf_op jit(solution)/shard_map/ppermute | solution.py:292
  18.2 1.1 collective-permute-start.8
  19.3 1.8 %collective-permute-done.9.refs_2_ = bf16[144,1024]{1,0:T(8,128)(2,1)S(1)} collective-permute-done((bf16[144,1024]{1,0:T(8,128)(2,1)S(1)}, bf16[144,1024]{1,0:T(8,128)(2,1)S(1)}, u32[]{:S(2)}, u32[]{:S(2)}) %collective-permute-start.9) | collective-permute-done | bytes 294944 | tf_op jit(solution)/shard_map/ppermute | solution.py:204
  21.1 0.8 collective-permute-start.10
  21.9 0.0 collective-permute-done.8.refs_1_
  22.0 1.2 collective-permute-done.10.refs_3_
  23.1 1.6 %shard_map.65 = (bf16[256,1024]{1,0:T(8,128)(2,1)S(1)}, bf16[256,1024]{1,0:T(8,128)(2,1)S(1)}) custom-call(bf16[144,1024]{1,0:T(8,128)(2,1)S(1)} %pad_maximum_fusion.1.refs_0_, bf16[144,1024]{1,0:T(8,128)(2,1)S(1)} %collective-permute-done.8.refs_1_, bf16[144,1024]{1,0:T(8,128)(2,1)S(1)} %collective-permute-done.9.refs_2_, ...), custom_call_target="tpu_custom_call" | custom-call | flops 536870912 | bytes 2752512 | tf_op jit(solution)/shard_map/pallas_call | solution.py:147
  24.7 4.7 %collective-permute-done.7 = bf16[256,1024]{1,0:T(8,128)(2,1)S(1)} collective-permute-done((bf16[256,1024]{1,0:T(8,128)(2,1)S(1)}, bf16[256,1024]{1,0:T(8,128)(2,1)S(1)}, u32[]{:S(2)}, u32[]{:S(2)}) %collective-permute-start.7) | collective-permute-done | bytes 524320 | tf_op jit(solution)/shard_map/ppermute | solution.py:292
  29.5 11.9 %collective-permute-done.6 = bf16[256,1024]{1,0:T(8,128)(2,1)S(1)} collective-permute-done((bf16[256,1024]{1,0:T(8,128)(2,1)S(1)}, bf16[256,1024]{1,0:T(8,128)(2,1)S(1)}, u32[]{:S(2)}, u32[]{:S(2)}) %collective-permute-start.6) | collective-permute-done | bytes 524320 | tf_op jit(solution)/shard_map/ppermute | solution.py:292
  41.4 0.5 add_convert_fusion.3
  41.9 0.1 broadcast_select_fusion
  42.0 0.1 collective-permute-start.12
  42.1 4.5 %collective-permute-start.17 = (bf16[256,1024]{1,0:T(8,128)(2,1)S(1)}, bf16[256,1024]{1,0:T(8,128)(2,1)S(1)}, u32[]{:S(2)}, u32[]{:S(2)}) collective-permute-start(bf16[256,1024]{1,0:T(8,128)(2,1)S(1)} %get-tuple-element.57), channel_id=1, source_target_pairs={{8,8},{16,9},{9,16},{17,17},{10,10},{18,11},{11,18},{19,19},{12,12... | collective-permute-start | bytes 1572872 | tf_op jit(solution)/shard_map/ppermute | solution.py:246
  46.5 1.3 %collective-permute-start.18 = (bf16[256,1024]{1,0:T(8,128)(2,1)S(1)}, bf16[256,1024]{1,0:T(8,128)(2,1)S(1)}, u32[]{:S(2)}, u32[]{:S(2)}) collective-permute-start(bf16[256,1024]{1,0:T(8,128)(2,1)S(1)} %get-tuple-element.57), channel_id=1, source_target_pairs={{0,8},{24,9},{1,16},{25,17},{2,10},{26,11},{3,18},{27,19},{4,12},{... | collective-permute-start | bytes 1572872 | tf_op jit(solution)/shard_map/ppermute | solution.py:247
  47.8 7.2 %collective-permute-done.12.refs_4_ = bf16[256,1024]{1,0:T(8,128)(2,1)S(1)} collective-permute-done((bf16[256,1024]{1,0:T(8,128)(2,1)S(1)}, bf16[256,1024]{1,0:T(8,128)(2,1)S(1)}, u32[]{:S(2)}, u32[]{:S(2)}) %collective-permute-start.12) | collective-permute-done | bytes 524320 | tf_op jit(solution)/shard_map/ppermute | solution.py:240
  55.1 0.4 add_convert_fusion.2
  55.4 3.6 %collective-permute-start.13 = (bf16[256,1024]{1,0:T(8,128)(2,1)S(1)}, bf16[256,1024]{1,0:T(8,128)(2,1)S(1)}, u32[]{:S(2)}, u32[]{:S(2)}) collective-permute-start(bf16[256,1024]{1,0:T(8,128)(2,1)S(1)} %add_convert_fusion.2), channel_id=1, source_target_pairs={{8,8},{16,9},{9,16},{17,17},{10,10},{18,11},{11,18},{19,19},{12,12... | collective-permute-start | bytes 1572872 | tf_op jit(solution)/shard_map/ppermute | solution.py:246
  59.0 1.3 %collective-permute-start.14 = (bf16[256,1024]{1,0:T(8,128)(2,1)S(1)}, bf16[256,1024]{1,0:T(8,128)(2,1)S(1)}, u32[]{:S(2)}, u32[]{:S(2)}) collective-permute-start(bf16[256,1024]{1,0:T(8,128)(2,1)S(1)} %add_convert_fusion.2), channel_id=1, source_target_pairs={{0,8},{24,9},{1,16},{25,17},{2,10},{26,11},{3,18},{27,19},{4,12},{... | collective-permute-start | bytes 1572872 | tf_op jit(solution)/shard_map/ppermute | solution.py:247
  60.3 0.1 collective-permute-start.19
  60.4 4.2 %shard_map.66 = (bf16[256,1024]{1,0:T(8,128)(2,1)S(1)}, bf16[256,1024]{1,0:T(8,128)(2,1)S(1)}) custom-call(bf16[512,1024]{1,0:T(8,128)(2,1)S(1)} %bitcast.29, bf16[256,1024]{1,0:T(8,128)(2,1)S(1)} %get-tuple-element.32.refs_1_, bf16[256,1024]{1,0:T(8,128)(2,1)S(1)} %get-tuple-element.33.refs_2_, bf16[256,1024]{1,0:T(8,128)(2,1)S(1)} %get-tuple-element.58.refs_3_, ...), custom_call_target="tpu_custom_call" | custom-call | flops 2684354560 | bytes 5242880 | tf_op jit(solution)/shard_map/pallas_call | solution.py:147
  64.6 0.0 collective-permute-done.18.refs_4_
  64.6 0.5 collective-permute-start.21
  65.2 2.5 %collective-permute-done.13.refs_3_ = bf16[256,1024]{1,0:T(8,128)(2,1)S(1)} collective-permute-done((bf16[256,1024]{1,0:T(8,128)(2,1)S(1)}, bf16[256,1024]{1,0:T(8,128)(2,1)S(1)}, u32[]{:S(2)}, u32[]{:S(2)}) %collective-permute-start.13) | collective-permute-done | bytes 524320 | tf_op jit(solution)/shard_map/ppermute | solution.py:246
  67.7 0.0 collective-permute-start.20
  67.7 4.1 %collective-permute-done.14.refs_5_ = bf16[256,1024]{1,0:T(8,128)(2,1)S(1)} collective-permute-done((bf16[256,1024]{1,0:T(8,128)(2,1)S(1)}, bf16[256,1024]{1,0:T(8,128)(2,1)S(1)}, u32[]{:S(2)}, u32[]{:S(2)}) %collective-permute-start.14) | collective-permute-done | bytes 524320 | tf_op jit(solution)/shard_map/ppermute | solution.py:247
  71.8 1.5 %collective-permute-start.22 = (bf16[256,1024]{1,0:T(8,128)(2,1)S(1)}, bf16[256,1024]{1,0:T(8,128)(2,1)S(1)}, u32[]{:S(2)}, u32[]{:S(2)}) collective-permute-start(bf16[256,1024]{1,0:T(8,128)(2,1)S(1)} %collective-permute-done.14.refs_5_), channel_id=1, source_target_pairs={{0,1},{1,0},{2,3},{3,2},{4,5},{5,4},{6,7},{7,6},{8,9},{9,8},{10,11... | collective-permute-start | bytes 1572872 | tf_op jit(solution)/shard_map/ppermute | solution.py:262
  73.3 3.9 %collective-permute-start.16 = (bf16[256,1024]{1,0:T(8,128)(2,1)S(1)}, bf16[256,1024]{1,0:T(8,128)(2,1)S(1)}, u32[]{:S(2)}, u32[]{:S(2)}) collective-permute-start(bf16[256,1024]{1,0:T(8,128)(2,1)S(1)} %get-tuple-element.49), channel_id=1, source_target_pairs={{16,8},{8,9},{17,16},{9,17},{18,10},{10,11},{19,18},{11,19},{20,12... | collective-permute-start | bytes 1572872 | tf_op jit(solution)/shard_map/ppermute | solution.py:264
  77.3 0.0 collective-permute-done.19.refs_6_
  77.3 1.3 %collective-permute-start.15 = (bf16[256,1024]{1,0:T(8,128)(2,1)S(1)}, bf16[256,1024]{1,0:T(8,128)(2,1)S(1)}, u32[]{:S(2)}, u32[]{:S(2)}) collective-permute-start(bf16[256,1024]{1,0:T(8,128)(2,1)S(1)} %get-tuple-element.49), channel_id=1, source_target_pairs={{0,8},{24,9},{1,16},{25,17},{2,10},{26,11},{3,18},{27,19},{4,12},{... | collective-permute-start | bytes 1572872 | tf_op jit(solution)/shard_map/ppermute | solution.py:264
  78.6 1.3 %collective-permute-start.24 = (bf16[256,1024]{1,0:T(8,128)(2,1)S(1)}, bf16[256,1024]{1,0:T(8,128)(2,1)S(1)}, u32[]{:S(2)}, u32[]{:S(2)}) collective-permute-start(bf16[256,1024]{1,0:T(8,128)(2,1)S(1)} %get-tuple-element.53), channel_id=1, source_target_pairs={{0,8},{24,9},{1,16},{25,17},{2,10},{26,11},{3,18},{27,19},{4,12},{... | collective-permute-start | bytes 1572872 | tf_op jit(solution)/shard_map/ppermute | solution.py:264
  79.9 0.0 collective-permute-done.20.refs_7_
  79.9 2.1 %collective-permute-start.25 = (bf16[256,1024]{1,0:T(8,128)(2,1)S(1)}, bf16[256,1024]{1,0:T(8,128)(2,1)S(1)}, u32[]{:S(2)}, u32[]{:S(2)}) collective-permute-start(bf16[256,1024]{1,0:T(8,128)(2,1)S(1)} %get-tuple-element.53), channel_id=1, source_target_pairs={{16,8},{8,9},{17,16},{9,17},{18,10},{10,11},{19,18},{11,19},{20,12... | collective-permute-start | bytes 1572872 | tf_op jit(solution)/shard_map/ppermute | solution.py:264
  82.0 7.2 %shard_map.67 = (f32[256,1024]{1,0:T(8,128)S(1)}, f32[256,1024]{1,0:T(8,128)S(1)}) custom-call(s32[1,2]{1,0:T(1,128)S(1)} %bitcast.33, s32[1,2]{1,0:T(1,128)S(1)} %bitcast.34, bf16[256,1024]{1,0:T(8,128)(2,1)S(1)} %collective-permute-done.17.refs_2_, bf16[256,1024]{1,0:T(8,128)(2,1)S(1)} %collective-permute-done.13.refs_3_, ...), custom_call_target="tpu_custom_call" | custom-call | flops 5368709120 | bytes 6291472 | tf_op jit(solution)/shard_map/pallas_call | solution.py:147
  89.3 5.1 %collective-permute-done.15 = bf16[256,1024]{1,0:T(8,128)(2,1)S(1)} collective-permute-done((bf16[256,1024]{1,0:T(8,128)(2,1)S(1)}, bf16[256,1024]{1,0:T(8,128)(2,1)S(1)}, u32[]{:S(2)}, u32[]{:S(2)}) %collective-permute-start.15) | collective-permute-done | bytes 524320 | tf_op jit(solution)/shard_map/ppermute | solution.py:264
  94.4 0.2 add_convert_fusion.1
  94.6 1.8 %collective-permute-start.23 = (bf16[256,1024]{1,0:T(8,128)(2,1)S(1)}, bf16[256,1024]{1,0:T(8,128)(2,1)S(1)}, u32[]{:S(2)}, u32[]{:S(2)}) collective-permute-start(bf16[256,1024]{1,0:T(8,128)(2,1)S(1)} %add_convert_fusion.1), channel_id=1, source_target_pairs={{8,0},{9,24},{16,1},{17,25},{10,2},{11,26},{18,3},{19,27},{12,4},{... | collective-permute-start | bytes 1572872 | tf_op jit(solution)/shard_map/ppermute | solution.py:277
  96.4 7.5 %collective-permute-done.24 = bf16[256,1024]{1,0:T(8,128)(2,1)S(1)} collective-permute-done((bf16[256,1024]{1,0:T(8,128)(2,1)S(1)}, bf16[256,1024]{1,0:T(8,128)(2,1)S(1)}, u32[]{:S(2)}, u32[]{:S(2)}) %collective-permute-start.24) | collective-permute-done | bytes 524320 | tf_op jit(solution)/shard_map/ppermute | solution.py:264
  103.9 0.3 add_convert_fusion
  104.1 1.7 %collective-permute-start.26 = (bf16[256,1024]{1,0:T(8,128)(2,1)S(1)}, bf16[256,1024]{1,0:T(8,128)(2,1)S(1)}, u32[]{:S(2)}, u32[]{:S(2)}) collective-permute-start(bf16[256,1024]{1,0:T(8,128)(2,1)S(1)} %add_convert_fusion), channel_id=1, source_target_pairs={{8,0},{9,24},{16,1},{17,25},{10,2},{11,26},{18,3},{19,27},{12,4},{... | collective-permute-start | bytes 1572872 | tf_op jit(solution)/shard_map/ppermute | solution.py:277
  105.9 1.9 %collective-permute-start.27 = (bf16[256,1024]{1,0:T(8,128)(2,1)S(1)}, bf16[256,1024]{1,0:T(8,128)(2,1)S(1)}, u32[]{:S(2)}, u32[]{:S(2)}) collective-permute-start(bf16[256,1024]{1,0:T(8,128)(2,1)S(1)} %add_convert_fusion.1), channel_id=1, source_target_pairs={{8,16},{9,8},{16,17},{17,9},{10,18},{11,10},{18,19},{19,11},{12,20... | collective-permute-start | bytes 1572872 | tf_op jit(solution)/shard_map/ppermute | solution.py:277
  107.8 2.7 %collective-permute-start.28 = (bf16[256,1024]{1,0:T(8,128)(2,1)S(1)}, bf16[256,1024]{1,0:T(8,128)(2,1)S(1)}, u32[]{:S(2)}, u32[]{:S(2)}) collective-permute-start(bf16[256,1024]{1,0:T(8,128)(2,1)S(1)} %add_convert_fusion), channel_id=1, source_target_pairs={{8,16},{9,8},{16,17},{17,9},{10,18},{11,10},{18,19},{19,11},{12,20... | collective-permute-start | bytes 1572872 | tf_op jit(solution)/shard_map/ppermute | solution.py:277
  110.6 0.0 collective-permute-done.23.refs_0_
  110.6 4.0 %collective-permute-done.26.refs_1_ = bf16[256,1024]{1,0:T(8,128)(2,1)S(1)} collective-permute-done((bf16[256,1024]{1,0:T(8,128)(2,1)S(1)}, bf16[256,1024]{1,0:T(8,128)(2,1)S(1)}, u32[]{:S(2)}, u32[]{:S(2)}) %collective-permute-start.26) | collective-permute-done | bytes 524320 | tf_op jit(solution)/shard_map/ppermute | solution.py:277
  114.5 4.3 %collective-permute-done.27.refs_2_ = bf16[256,1024]{1,0:T(8,128)(2,1)S(1)} collective-permute-done((bf16[256,1024]{1,0:T(8,128)(2,1)S(1)}, bf16[256,1024]{1,0:T(8,128)(2,1)S(1)}, u32[]{:S(2)}, u32[]{:S(2)}) %collective-permute-start.27) | collective-permute-done | bytes 524320 | tf_op jit(solution)/shard_map/ppermute | solution.py:277
  118.8 5.6 %collective-permute-done.28.refs_3_ = bf16[256,1024]{1,0:T(8,128)(2,1)S(1)} collective-permute-done((bf16[256,1024]{1,0:T(8,128)(2,1)S(1)}, bf16[256,1024]{1,0:T(8,128)(2,1)S(1)}, u32[]{:S(2)}, u32[]{:S(2)}) %collective-permute-start.28) | collective-permute-done | bytes 524320 | tf_op jit(solution)/shard_map/ppermute | solution.py:277
  124.4 1.0 shard_map.68
  (17 shorter events, 0.1 us)
Async XLA Ops:
  0.7 12.9 %copy-start = (bf16[1,1,512,1024]{3,2,1,0:T(8,128)(2,1)S(1)}, bf16[1,1,512,1024]{3,2,1,0:T(8,128)(2,1)}, u32[]{:S(2)}) copy-start(bf16[1,1,512,1024]{3,2,1,0:T(8,128)(2,1)} %param.10) | copy-start | bytes 3145732
  1.9 11.8 %copy-start.1 = (bf16[2,1,1,256,512]{4,3,2,1,0:T(8,128)(2,1)S(1)}, bf16[2,1,1,256,512]{4,3,2,1,0:T(8,128)(2,1)}, u32[]{:S(2)}) copy-start(bf16[2,1,1,256,512]{4,3,2,1,0:T(8,128)(2,1)} %param.8) | copy-start | bytes 1572868
  1.9 1.3 %copy-start.3 = (s32[1,2]{1,0:T(1,128)S(1)}, s32[1,2]{1,0:T(1,128)}, u32[]{:S(2)}) copy-start(s32[1,2]{1,0:T(1,128)} %param.11) | copy-start | bytes 28
  1.9 8.4 %collective-permute-start.1 = (bf16[144,1024]{1,0:T(8,128)(2,1)S(1)}, bf16[144,1024]{1,0:T(8,128)(2,1)S(1)}, u32[]{:S(2)}, u32[]{:S(2)}) collective-permute-start(bf16[144,1024]{1,0:T(8,128)(2,1)S(1)} %pad_maximum_fusion.refs_0_), channel_id=1, source_target_pairs={{0,2},{1,3},{2,0},{3,1},{4,6},{5,7},{6,4},{7,5},{8,10},{9,11},{10,... | collective-permute-start | bytes 884744 | tf_op jit(solution)/shard_map/ppermute | solution.py:204
  3.2 5.8 %collective-permute-start.2 = (s32[2]{0:T(128)S(1)}, s32[2]{0:T(128)S(1)}, u32[]{:S(2)}, u32[]{:S(2)}) collective-permute-start(s32[2]{0:T(128)S(1)} %bitcast.35), channel_id=1, source_target_pairs={{0,4},{4,0},{8,12},{12,8},{16,20},{20,16},{24,28},{28,24},{1,5},{5... | collective-permute-start | bytes 32 | tf_op jit(solution)/shard_map/ppermute | solution.py:191
  4.4 5.9 %collective-permute-start.3 = (s32[2]{0:T(128)S(1)}, s32[2]{0:T(128)S(1)}, u32[]{:S(2)}, u32[]{:S(2)}) collective-permute-start(s32[2]{0:T(128)S(1)} %bitcast.36), channel_id=1, source_target_pairs={{0,8},{24,9},{1,16},{25,17},{2,10},{26,11},{3,18},{27,19},{4,12},{... | collective-permute-start | bytes 32 | tf_op jit(solution)/shard_map/ppermute | solution.py:193
  5.7 4.6 %collective-permute-start.4 = (s32[2]{0:T(128)S(1)}, s32[2]{0:T(128)S(1)}, u32[]{:S(2)}, u32[]{:S(2)}) collective-permute-start(s32[2]{0:T(128)S(1)} %bitcast.37), channel_id=1, source_target_pairs={{16,8},{8,9},{17,16},{9,17},{18,10},{10,11},{19,18},{11,19},{20,12... | collective-permute-start | bytes 32 | tf_op jit(solution)/shard_map/ppermute | solution.py:194
  8.9 3.9 %collective-permute-start = (bf16[144,1024]{1,0:T(8,128)(2,1)S(1)}, bf16[144,1024]{1,0:T(8,128)(2,1)S(1)}, u32[]{:S(2)}, u32[]{:S(2)}) collective-permute-start(bf16[144,1024]{1,0:T(8,128)(2,1)S(1)} %pad_maximum_fusion.refs_0_), channel_id=1, source_target_pairs={{0,1},{1,0},{2,3},{3,2},{4,5},{5,4},{6,7},{7,6},{8,9},{9,8},{10,11... | collective-permute-start | bytes 884744 | tf_op jit(solution)/shard_map/ppermute | solution.py:204
  10.4 3.2 %collective-permute-start.5 = (bf16[144,1024]{1,0:T(8,128)(2,1)S(1)}, bf16[144,1024]{1,0:T(8,128)(2,1)S(1)}, u32[]{:S(2)}, u32[]{:S(2)}) collective-permute-start(bf16[144,1024]{1,0:T(8,128)(2,1)S(1)} %collective-permute-done.1.refs_2_), channel_id=1, source_target_pairs={{0,1},{1,0},{2,3},{3,2},{4,5},{5,4},{6,7},{7,6},{8,9},{9,8},{10,11... | collective-permute-start | bytes 884744 | tf_op jit(solution)/shard_map/ppermute | solution.py:204
  12.4 8.7 %collective-permute-start.9 = (bf16[144,1024]{1,0:T(8,128)(2,1)S(1)}, bf16[144,1024]{1,0:T(8,128)(2,1)S(1)}, u32[]{:S(2)}, u32[]{:S(2)}) collective-permute-start(bf16[144,1024]{1,0:T(8,128)(2,1)S(1)} %pad_maximum_fusion.1.refs_0_), channel_id=1, source_target_pairs={{0,2},{1,3},{2,0},{3,1},{4,6},{5,7},{6,4},{7,5},{8,10},{9,11},{10,... | collective-permute-start | bytes 884744 | tf_op jit(solution)/shard_map/ppermute | solution.py:204
  15.3 14.1 %collective-permute-start.7 = (bf16[256,1024]{1,0:T(8,128)(2,1)S(1)}, bf16[256,1024]{1,0:T(8,128)(2,1)S(1)}, u32[]{:S(2)}, u32[]{:S(2)}) collective-permute-start(bf16[256,1024]{1,0:T(8,128)(2,1)S(1)} %get-tuple-element.34), channel_id=1, source_target_pairs={{28,0},{0,4},{4,8},{8,12},{12,16},{16,20},{20,24},{24,28},{29,1},{... | collective-permute-start | bytes 1572872 | tf_op jit(solution)/shard_map/ppermute | solution.py:292
  15.7 13.7 %collective-permute-start.11 = (bf16[256,1024]{1,0:T(8,128)(2,1)S(1)}, bf16[256,1024]{1,0:T(8,128)(2,1)S(1)}, u32[]{:S(2)}, u32[]{:S(2)}) collective-permute-start(bf16[256,1024]{1,0:T(8,128)(2,1)S(1)} %get-tuple-element.40), channel_id=1, source_target_pairs={{0,24},{4,12},{8,0},{12,20},{16,8},{20,28},{24,16},{28,4},{1,25},{... | collective-permute-start | bytes 1572872 | tf_op jit(solution)/shard_map/ppermute | solution.py:224
  15.9 25.5 %collective-permute-start.6 = (bf16[256,1024]{1,0:T(8,128)(2,1)S(1)}, bf16[256,1024]{1,0:T(8,128)(2,1)S(1)}, u32[]{:S(2)}, u32[]{:S(2)}) collective-permute-start(bf16[256,1024]{1,0:T(8,128)(2,1)S(1)} %get-tuple-element.34), channel_id=1, source_target_pairs={{4,0},{8,4},{12,8},{16,12},{20,16},{24,20},{28,24},{0,28},{5,1},{9... | collective-permute-start | bytes 1572872 | tf_op jit(solution)/shard_map/ppermute | solution.py:292
  18.2 3.8 %collective-permute-start.8 = (bf16[144,1024]{1,0:T(8,128)(2,1)S(1)}, bf16[144,1024]{1,0:T(8,128)(2,1)S(1)}, u32[]{:S(2)}, u32[]{:S(2)}) collective-permute-start(bf16[144,1024]{1,0:T(8,128)(2,1)S(1)} %pad_maximum_fusion.1.refs_0_), channel_id=1, source_target_pairs={{0,1},{1,0},{2,3},{3,2},{4,5},{5,4},{6,7},{7,6},{8,9},{9,8},{10,11... | collective-permute-start | bytes 884744 | tf_op jit(solution)/shard_map/ppermute | solution.py:204
  21.1 2.0 %collective-permute-start.10 = (bf16[144,1024]{1,0:T(8,128)(2,1)S(1)}, bf16[144,1024]{1,0:T(8,128)(2,1)S(1)}, u32[]{:S(2)}, u32[]{:S(2)}) collective-permute-start(bf16[144,1024]{1,0:T(8,128)(2,1)S(1)} %collective-permute-done.9.refs_2_), channel_id=1, source_target_pairs={{0,1},{1,0},{2,3},{3,2},{4,5},{5,4},{6,7},{7,6},{8,9},{9,8},{10,11... | collective-permute-start | bytes 884744 | tf_op jit(solution)/shard_map/ppermute | solution.py:204
  42.0 13.1 %collective-permute-start.12 = (bf16[256,1024]{1,0:T(8,128)(2,1)S(1)}, bf16[256,1024]{1,0:T(8,128)(2,1)S(1)}, u32[]{:S(2)}, u32[]{:S(2)}) collective-permute-start(bf16[256,1024]{1,0:T(8,128)(2,1)S(1)} %broadcast_select_fusion), channel_id=1, source_target_pairs={{0,4},{4,0},{8,12},{12,8},{16,20},{20,16},{24,28},{28,24},{1,5},{5... | collective-permute-start | bytes 1572872 | tf_op jit(solution)/shard_map/ppermute | solution.py:240
  42.1 18.3 %collective-permute-start.17 = (bf16[256,1024]{1,0:T(8,128)(2,1)S(1)}, bf16[256,1024]{1,0:T(8,128)(2,1)S(1)}, u32[]{:S(2)}, u32[]{:S(2)}) collective-permute-start(bf16[256,1024]{1,0:T(8,128)(2,1)S(1)} %get-tuple-element.57), channel_id=1, source_target_pairs={{8,8},{16,9},{9,16},{17,17},{10,10},{18,11},{11,18},{19,19},{12,12... | collective-permute-start | bytes 1572872 | tf_op jit(solution)/shard_map/ppermute | solution.py:246
  46.5 18.1 %collective-permute-start.18 = (bf16[256,1024]{1,0:T(8,128)(2,1)S(1)}, bf16[256,1024]{1,0:T(8,128)(2,1)S(1)}, u32[]{:S(2)}, u32[]{:S(2)}) collective-permute-start(bf16[256,1024]{1,0:T(8,128)(2,1)S(1)} %get-tuple-element.57), channel_id=1, source_target_pairs={{0,8},{24,9},{1,16},{25,17},{2,10},{26,11},{3,18},{27,19},{4,12},{... | collective-permute-start | bytes 1572872 | tf_op jit(solution)/shard_map/ppermute | solution.py:247
  55.1 5.4 %copy-start.2 = (bf16[1,1,512,1024]{3,2,1,0:T(8,128)(2,1)S(1)}, bf16[1,1,512,1024]{3,2,1,0:T(8,128)(2,1)}, u32[]{:S(2)}) copy-start(bf16[1,1,512,1024]{3,2,1,0:T(8,128)(2,1)} %param.9) | copy-start | bytes 3145732
  55.4 12.3 %collective-permute-start.13 = (bf16[256,1024]{1,0:T(8,128)(2,1)S(1)}, bf16[256,1024]{1,0:T(8,128)(2,1)S(1)}, u32[]{:S(2)}, u32[]{:S(2)}) collective-permute-start(bf16[256,1024]{1,0:T(8,128)(2,1)S(1)} %add_convert_fusion.2), channel_id=1, source_target_pairs={{8,8},{16,9},{9,16},{17,17},{10,10},{18,11},{11,18},{19,19},{12,12... | collective-permute-start | bytes 1572872 | tf_op jit(solution)/shard_map/ppermute | solution.py:246
  59.0 12.8 %collective-permute-start.14 = (bf16[256,1024]{1,0:T(8,128)(2,1)S(1)}, bf16[256,1024]{1,0:T(8,128)(2,1)S(1)}, u32[]{:S(2)}, u32[]{:S(2)}) collective-permute-start(bf16[256,1024]{1,0:T(8,128)(2,1)S(1)} %add_convert_fusion.2), channel_id=1, source_target_pairs={{0,8},{24,9},{1,16},{25,17},{2,10},{26,11},{3,18},{27,19},{4,12},{... | collective-permute-start | bytes 1572872 | tf_op jit(solution)/shard_map/ppermute | solution.py:247
  60.3 16.9 %collective-permute-start.19 = (bf16[256,1024]{1,0:T(8,128)(2,1)S(1)}, bf16[256,1024]{1,0:T(8,128)(2,1)S(1)}, u32[]{:S(2)}, u32[]{:S(2)}) collective-permute-start(bf16[256,1024]{1,0:T(8,128)(2,1)S(1)} %collective-permute-done.17.refs_2_), channel_id=1, source_target_pairs={{0,1},{1,0},{2,3},{3,2},{4,5},{5,4},{6,7},{7,6},{8,9},{9,8},{10,11... | collective-permute-start | bytes 1572872 | tf_op jit(solution)/shard_map/ppermute | solution.py:250
  64.6 13.9 %collective-permute-start.21 = (bf16[256,1024]{1,0:T(8,128)(2,1)S(1)}, bf16[256,1024]{1,0:T(8,128)(2,1)S(1)}, u32[]{:S(2)}, u32[]{:S(2)}) collective-permute-start(bf16[256,1024]{1,0:T(8,128)(2,1)S(1)} %collective-permute-done.18.refs_4_), channel_id=1, source_target_pairs={{0,1},{1,0},{2,3},{3,2},{4,5},{5,4},{6,7},{7,6},{8,9},{9,8},{10,11... | collective-permute-start | bytes 1572872 | tf_op jit(solution)/shard_map/ppermute | solution.py:251
  67.7 12.2 %collective-permute-start.20 = (bf16[256,1024]{1,0:T(8,128)(2,1)S(1)}, bf16[256,1024]{1,0:T(8,128)(2,1)S(1)}, u32[]{:S(2)}, u32[]{:S(2)}) collective-permute-start(bf16[256,1024]{1,0:T(8,128)(2,1)S(1)} %collective-permute-done.13.refs_3_), channel_id=1, source_target_pairs={{0,1},{1,0},{2,3},{3,2},{4,5},{5,4},{6,7},{7,6},{8,9},{9,8},{10,11... | collective-permute-start | bytes 1572872 | tf_op jit(solution)/shard_map/ppermute | solution.py:261
  71.8 10.2 %collective-permute-start.22 = (bf16[256,1024]{1,0:T(8,128)(2,1)S(1)}, bf16[256,1024]{1,0:T(8,128)(2,1)S(1)}, u32[]{:S(2)}, u32[]{:S(2)}) collective-permute-start(bf16[256,1024]{1,0:T(8,128)(2,1)S(1)} %collective-permute-done.14.refs_5_), channel_id=1, source_target_pairs={{0,1},{1,0},{2,3},{3,2},{4,5},{5,4},{6,7},{7,6},{8,9},{9,8},{10,11... | collective-permute-start | bytes 1572872 | tf_op jit(solution)/shard_map/ppermute | solution.py:262
  73.3 15.9 %collective-permute-start.16 = (bf16[256,1024]{1,0:T(8,128)(2,1)S(1)}, bf16[256,1024]{1,0:T(8,128)(2,1)S(1)}, u32[]{:S(2)}, u32[]{:S(2)}) collective-permute-start(bf16[256,1024]{1,0:T(8,128)(2,1)S(1)} %get-tuple-element.49), channel_id=1, source_target_pairs={{16,8},{8,9},{17,16},{9,17},{18,10},{10,11},{19,18},{11,19},{20,12... | collective-permute-start | bytes 1572872 | tf_op jit(solution)/shard_map/ppermute | solution.py:264
  77.3 17.1 %collective-permute-start.15 = (bf16[256,1024]{1,0:T(8,128)(2,1)S(1)}, bf16[256,1024]{1,0:T(8,128)(2,1)S(1)}, u32[]{:S(2)}, u32[]{:S(2)}) collective-permute-start(bf16[256,1024]{1,0:T(8,128)(2,1)S(1)} %get-tuple-element.49), channel_id=1, source_target_pairs={{0,8},{24,9},{1,16},{25,17},{2,10},{26,11},{3,18},{27,19},{4,12},{... | collective-permute-start | bytes 1572872 | tf_op jit(solution)/shard_map/ppermute | solution.py:264
  78.6 25.3 %collective-permute-start.24 = (bf16[256,1024]{1,0:T(8,128)(2,1)S(1)}, bf16[256,1024]{1,0:T(8,128)(2,1)S(1)}, u32[]{:S(2)}, u32[]{:S(2)}) collective-permute-start(bf16[256,1024]{1,0:T(8,128)(2,1)S(1)} %get-tuple-element.53), channel_id=1, source_target_pairs={{0,8},{24,9},{1,16},{25,17},{2,10},{26,11},{3,18},{27,19},{4,12},{... | collective-permute-start | bytes 1572872 | tf_op jit(solution)/shard_map/ppermute | solution.py:264
  79.9 24.0 %collective-permute-start.25 = (bf16[256,1024]{1,0:T(8,128)(2,1)S(1)}, bf16[256,1024]{1,0:T(8,128)(2,1)S(1)}, u32[]{:S(2)}, u32[]{:S(2)}) collective-permute-start(bf16[256,1024]{1,0:T(8,128)(2,1)S(1)} %get-tuple-element.53), channel_id=1, source_target_pairs={{16,8},{8,9},{17,16},{9,17},{18,10},{10,11},{19,18},{11,19},{20,12... | collective-permute-start | bytes 1572872 | tf_op jit(solution)/shard_map/ppermute | solution.py:264
  94.6 15.9 %collective-permute-start.23 = (bf16[256,1024]{1,0:T(8,128)(2,1)S(1)}, bf16[256,1024]{1,0:T(8,128)(2,1)S(1)}, u32[]{:S(2)}, u32[]{:S(2)}) collective-permute-start(bf16[256,1024]{1,0:T(8,128)(2,1)S(1)} %add_convert_fusion.1), channel_id=1, source_target_pairs={{8,0},{9,24},{16,1},{17,25},{10,2},{11,26},{18,3},{19,27},{12,4},{... | collective-permute-start | bytes 1572872 | tf_op jit(solution)/shard_map/ppermute | solution.py:277
  104.1 10.4 %collective-permute-start.26 = (bf16[256,1024]{1,0:T(8,128)(2,1)S(1)}, bf16[256,1024]{1,0:T(8,128)(2,1)S(1)}, u32[]{:S(2)}, u32[]{:S(2)}) collective-permute-start(bf16[256,1024]{1,0:T(8,128)(2,1)S(1)} %add_convert_fusion), channel_id=1, source_target_pairs={{8,0},{9,24},{16,1},{17,25},{10,2},{11,26},{18,3},{19,27},{12,4},{... | collective-permute-start | bytes 1572872 | tf_op jit(solution)/shard_map/ppermute | solution.py:277
  105.9 12.9 %collective-permute-start.27 = (bf16[256,1024]{1,0:T(8,128)(2,1)S(1)}, bf16[256,1024]{1,0:T(8,128)(2,1)S(1)}, u32[]{:S(2)}, u32[]{:S(2)}) collective-permute-start(bf16[256,1024]{1,0:T(8,128)(2,1)S(1)} %add_convert_fusion.1), channel_id=1, source_target_pairs={{8,16},{9,8},{16,17},{17,9},{10,18},{11,10},{18,19},{19,11},{12,20... | collective-permute-start | bytes 1572872 | tf_op jit(solution)/shard_map/ppermute | solution.py:277
  107.8 16.6 %collective-permute-start.28 = (bf16[256,1024]{1,0:T(8,128)(2,1)S(1)}, bf16[256,1024]{1,0:T(8,128)(2,1)S(1)}, u32[]{:S(2)}, u32[]{:S(2)}) collective-permute-start(bf16[256,1024]{1,0:T(8,128)(2,1)S(1)} %add_convert_fusion), channel_id=1, source_target_pairs={{8,16},{9,8},{16,17},{17,9},{10,18},{11,10},{18,19},{19,11},{12,20... | collective-permute-start | bytes 1572872 | tf_op jit(solution)/shard_map/ppermute | solution.py:277

commit v6 on v5

--- a/solution.py
+++ b/solution.py
@@ -10,6 +10,7 @@
 
 NS_ITERS = 2
 CHUNKS = 2
+FIRST = 18
 BLOCKS = 2
 DIRECT = 1
 VMEM_LIMIT = 32 * 1024 * 1024
@@ -212,7 +213,7 @@
     if top > 1:
         spread(gathered[0], 1)
 
-    edges = [fan_rows // 16 * i // CHUNKS * 16 for i in range(CHUNKS)] + [fan_rows]
+    edges = [0, fan_rows // 32 * FIRST, fan_rows]
     parts = [slice(low, high) for low, high in zip(edges, edges[1:])]
     chunk = [jax.ShapeDtypeStruct((p.stop - p.start, features), jnp.bfloat16) for p in parts]
     cost = 2 * fan_rows * features * experts * count

time: 126 us -> 126 us (level)
  the two profiles are of different devices: /device:TPU:9 before, /device:TPU:11 now
where the time goes in v6:
time: 126 us; the launch traced here: 125 us
  waiting for transfers between devices  61.4 us (49%)
  starting transfers between devices  44.2 us (35%)
  Pallas kernels  15.6 us (12%)
  other arithmetic  2.24 us (2%)
    ppermute x1, waiting for transfers between devices, paired(): fetched = [lax.ppermute(o, 'site', helpers) for o in own[DIRECT:]]  16 us
    pallas_call x4, Pallas kernels, call(): pl.pallas_call(body, in_specs=[VMEM] * count, out_specs=[VMEM] * len(out_...  14.5 us
    ppermute x2, waiting for transfers between devices, paired(): lax.ppermute(v, both, outer)  12.8 us
    ppermute x2, starting transfers between devices, paired(): here0.append(lax.ppermute(second[i], both, middle))  9.4 us
    ppermute x2, waiting for transfers between devices, paired(): lax.ppermute(r, both, to_matched)  9.36 us
    ppermute x2, waiting for transfers between devices, paired(): here1.append(lax.ppermute(second[i], both, outer))  6.99 us
    ppermute x2, starting transfers between devices, paired(): lax.ppermute(v, both, matched)  6.4 us
    ppermute x6, starting transfers between devices, spread(): lax.ppermute(t, 'expert', hop)  6.14 us
  transfers between devices with their start and end apart: 29, of which 15 were waited for; matrix products, arithmetic and copies ran while one was open for 1% of the time, Pallas kernels for 12%

profile of v6, /device:TPU:11, one launch (start us, length us, event | category | flops | bytes accessed | tf_op | source)
XLA Modules:
  0.0 125.2 jit_solution(2819625011404348556)
XLA Ops:
  0.0 0.7 convert_bitcast_fusion
  0.7 0.0 copy-start.1
  0.7 1.2 slice_bitcast_fusion
  1.9 1.3 %collective-permute-start.1 = (bf16[144,1024]{1,0:T(8,128)(2,1)S(1)}, bf16[144,1024]{1,0:T(8,128)(2,1)S(1)}, u32[]{:S(2)}, u32[]{:S(2)}) collective-permute-start(bf16[144,1024]{1,0:T(8,128)(2,1)S(1)} %pad_maximum_fusion.refs_0_), channel_id=1, source_target_pairs={{0,2},{1,3},{2,0},{3,1},{4,6},{5,7},{6,4},{7,5},{8,10},{9,11},{10,... | collective-permute-start | bytes 884744 | tf_op jit(solution)/shard_map/ppermute | solution.py:205
  3.2 0.3 collective-permute-start.2
  3.5 1.3 %collective-permute-start.3 = (s32[2]{0:T(128)S(1)}, s32[2]{0:T(128)S(1)}, u32[]{:S(2)}, u32[]{:S(2)}) collective-permute-start(s32[2]{0:T(128)S(1)} %bitcast.36), channel_id=1, source_target_pairs={{0,8},{24,9},{1,16},{25,17},{2,10},{26,11},{3,18},{27,19},{4,12},{... | collective-permute-start | bytes 32 | tf_op jit(solution)/shard_map/ppermute | solution.py:194
  4.8 3.2 %collective-permute-start.4 = (s32[2]{0:T(128)S(1)}, s32[2]{0:T(128)S(1)}, u32[]{:S(2)}, u32[]{:S(2)}) collective-permute-start(s32[2]{0:T(128)S(1)} %bitcast.37), channel_id=1, source_target_pairs={{16,8},{8,9},{17,16},{9,17},{18,10},{10,11},{19,18},{11,19},{20,12... | collective-permute-start | bytes 32 | tf_op jit(solution)/shard_map/ppermute | solution.py:195
  8.0 0.1 collective-permute-start
  8.1 0.0 collective-permute-done.2
  8.1 1.3 %collective-permute-done.3 = s32[2]{0:T(128)S(1)} collective-permute-done((s32[2]{0:T(128)S(1)}, s32[2]{0:T(128)S(1)}, u32[]{:S(2)}, u32[]{:S(2)}) %collective-permute-start.3) | collective-permute-done | bytes 40 | tf_op jit(solution)/shard_map/ppermute | solution.py:194
  9.4 0.5 collective-permute-done.1.refs_2_
  9.9 1.6 %collective-permute-start.5 = (bf16[144,1024]{1,0:T(8,128)(2,1)S(1)}, bf16[144,1024]{1,0:T(8,128)(2,1)S(1)}, u32[]{:S(2)}, u32[]{:S(2)}) collective-permute-start(bf16[144,1024]{1,0:T(8,128)(2,1)S(1)} %collective-permute-done.1.refs_2_), channel_id=1, source_target_pairs={{0,1},{1,0},{2,3},{3,2},{4,5},{5,4},{6,7},{7,6},{8,9},{9,8},{10,11... | collective-permute-start | bytes 884744 | tf_op jit(solution)/shard_map/ppermute | solution.py:205
  11.5 1.3 %collective-permute-start.9 = (bf16[144,1024]{1,0:T(8,128)(2,1)S(1)}, bf16[144,1024]{1,0:T(8,128)(2,1)S(1)}, u32[]{:S(2)}, u32[]{:S(2)}) collective-permute-start(bf16[144,1024]{1,0:T(8,128)(2,1)S(1)} %pad_maximum_fusion.1.refs_0_), channel_id=1, source_target_pairs={{0,2},{1,3},{2,0},{3,1},{4,6},{5,7},{6,4},{7,5},{8,10},{9,11},{10,... | collective-permute-start | bytes 884744 | tf_op jit(solution)/shard_map/ppermute | solution.py:205
  12.8 0.0 collective-permute-done.refs_1_
  12.8 0.0 collective-permute-done.5.refs_3_
  12.8 1.7 %shard_map.64 = (bf16[288,1024]{1,0:T(8,128)(2,1)S(1)}, bf16[224,1024]{1,0:T(8,128)(2,1)S(1)}, bf16[288,1024]{1,0:T(8,128)(2,1)S(1)}, bf16[224,1024]{1,0:T(8,128)(2,1)S(1)}) custom-call(bf16[144,1024]{1,0:T(8,128)(2,1)S(1)} %pad_maximum_fusion.refs_0_, bf16[144,1024]{1,0:T(8,128)(2,1)S(1)} %collective-permute-done.refs_1_, ...), custom_call_target="tpu_custom_call" | custom-call | flops 536870912 | bytes 4849664 | tf_op jit(solution)/shard_map/pallas_call | solution.py:148
  14.5 1.3 %collective-permute-start.7 = (bf16[288,1024]{1,0:T(8,128)(2,1)S(1)}, bf16[288,1024]{1,0:T(8,128)(2,1)S(1)}, u32[]{:S(2)}, u32[]{:S(2)}) collective-permute-start(bf16[288,1024]{1,0:T(8,128)(2,1)S(1)} %get-tuple-element.34), channel_id=1, source_target_pairs={{28,0},{0,4},{4,8},{8,12},{12,16},{16,20},{20,24},{24,28},{29,1},{... | collective-permute-start | bytes 1769480 | tf_op jit(solution)/shard_map/ppermute | solution.py:293
  15.8 0.2 collective-permute-start.6
  16.0 1.3 %collective-permute-start.11 = (bf16[224,1024]{1,0:T(8,128)(2,1)S(1)}, bf16[224,1024]{1,0:T(8,128)(2,1)S(1)}, u32[]{:S(2)}, u32[]{:S(2)}) collective-permute-start(bf16[224,1024]{1,0:T(8,128)(2,1)S(1)} %get-tuple-element.40), channel_id=1, source_target_pairs={{0,24},{4,12},{8,0},{12,20},{16,8},{20,28},{24,16},{28,4},{1,25},{... | collective-permute-start | bytes 1376264 | tf_op jit(solution)/shard_map/ppermute | solution.py:225
  17.3 1.1 collective-permute-start.8
  18.5 1.7 %collective-permute-done.9.refs_2_ = bf16[144,1024]{1,0:T(8,128)(2,1)S(1)} collective-permute-done((bf16[144,1024]{1,0:T(8,128)(2,1)S(1)}, bf16[144,1024]{1,0:T(8,128)(2,1)S(1)}, u32[]{:S(2)}, u32[]{:S(2)}) %collective-permute-start.9) | collective-permute-done | bytes 294944 | tf_op jit(solution)/shard_map/ppermute | solution.py:205
  20.2 0.8 collective-permute-start.10
  21.0 0.0 collective-permute-done.8.refs_1_
  21.0 1.2 collective-permute-done.10.refs_3_
  22.2 1.6 %shard_map.65 = (bf16[288,1024]{1,0:T(8,128)(2,1)S(1)}, bf16[224,1024]{1,0:T(8,128)(2,1)S(1)}) custom-call(bf16[144,1024]{1,0:T(8,128)(2,1)S(1)} %pad_maximum_fusion.1.refs_0_, bf16[144,1024]{1,0:T(8,128)(2,1)S(1)} %collective-permute-done.8.refs_1_, bf16[144,1024]{1,0:T(8,128)(2,1)S(1)} %collective-permute-done.9.refs_2_, ...), custom_call_target="tpu_custom_call" | custom-call | flops 536870912 | bytes 2752512 | tf_op jit(solution)/shard_map/pallas_call | solution.py:148
  23.8 16.0 %collective-permute-done.11 = bf16[224,1024]{1,0:T(8,128)(2,1)S(1)} collective-permute-done((bf16[224,1024]{1,0:T(8,128)(2,1)S(1)}, bf16[224,1024]{1,0:T(8,128)(2,1)S(1)}, u32[]{:S(2)}, u32[]{:S(2)}) %collective-permute-start.11) | collective-permute-done | bytes 458784 | tf_op jit(solution)/shard_map/ppermute | solution.py:225
  39.8 2.0 %collective-permute-done.7 = bf16[288,1024]{1,0:T(8,128)(2,1)S(1)} collective-permute-done((bf16[288,1024]{1,0:T(8,128)(2,1)S(1)}, bf16[288,1024]{1,0:T(8,128)(2,1)S(1)}, u32[]{:S(2)}, u32[]{:S(2)}) %collective-permute-start.7) | collective-permute-done | bytes 589856 | tf_op jit(solution)/shard_map/ppermute | solution.py:293
  41.8 0.0 collective-permute-done.6
  41.8 0.6 add_convert_fusion
  42.5 0.1 broadcast_select_fusion.1
  42.5 1.6 %collective-permute-start.12 = (bf16[224,1024]{1,0:T(8,128)(2,1)S(1)}, bf16[224,1024]{1,0:T(8,128)(2,1)S(1)}, u32[]{:S(2)}, u32[]{:S(2)}) collective-permute-start(bf16[224,1024]{1,0:T(8,128)(2,1)S(1)} %broadcast_select_fusion.1), channel_id=1, source_target_pairs={{0,4},{4,0},{8,12},{12,8},{16,20},{20,16},{24,28},{28,24},{1,5},{5... | collective-permute-start | bytes 1376264 | tf_op jit(solution)/shard_map/ppermute | solution.py:241
  44.1 4.1 %collective-permute-start.17 = (bf16[288,1024]{1,0:T(8,128)(2,1)S(1)}, bf16[288,1024]{1,0:T(8,128)(2,1)S(1)}, u32[]{:S(2)}, u32[]{:S(2)}) collective-permute-start(bf16[288,1024]{1,0:T(8,128)(2,1)S(1)} %get-tuple-element.57), channel_id=1, source_target_pairs={{8,8},{16,9},{9,16},{17,17},{10,10},{18,11},{11,18},{19,19},{12,12... | collective-permute-start | bytes 1769480 | tf_op jit(solution)/shard_map/ppermute | solution.py:247
  48.2 1.3 %collective-permute-start.18 = (bf16[288,1024]{1,0:T(8,128)(2,1)S(1)}, bf16[288,1024]{1,0:T(8,128)(2,1)S(1)}, u32[]{:S(2)}, u32[]{:S(2)}) collective-permute-start(bf16[288,1024]{1,0:T(8,128)(2,1)S(1)} %get-tuple-element.57), channel_id=1, source_target_pairs={{0,8},{24,9},{1,16},{25,17},{2,10},{26,11},{3,18},{27,19},{4,12},{... | collective-permute-start | bytes 1769480 | tf_op jit(solution)/shard_map/ppermute | solution.py:248
  49.5 4.1 %collective-permute-done.12.refs_4_ = bf16[224,1024]{1,0:T(8,128)(2,1)S(1)} collective-permute-done((bf16[224,1024]{1,0:T(8,128)(2,1)S(1)}, bf16[224,1024]{1,0:T(8,128)(2,1)S(1)}, u32[]{:S(2)}, u32[]{:S(2)}) %collective-permute-start.12) | collective-permute-done | bytes 458784 | tf_op jit(solution)/shard_map/ppermute | solution.py:241
  53.6 0.3 add_convert_fusion.3
  54.0 5.3 %collective-permute-start.13 = (bf16[224,1024]{1,0:T(8,128)(2,1)S(1)}, bf16[224,1024]{1,0:T(8,128)(2,1)S(1)}, u32[]{:S(2)}, u32[]{:S(2)}) collective-permute-start(bf16[224,1024]{1,0:T(8,128)(2,1)S(1)} %add_convert_fusion.3), channel_id=1, source_target_pairs={{8,8},{16,9},{9,16},{17,17},{10,10},{18,11},{11,18},{19,19},{12,12... | collective-permute-start | bytes 1376264 | tf_op jit(solution)/shard_map/ppermute | solution.py:247
  59.3 1.3 %collective-permute-start.14 = (bf16[224,1024]{1,0:T(8,128)(2,1)S(1)}, bf16[224,1024]{1,0:T(8,128)(2,1)S(1)}, u32[]{:S(2)}, u32[]{:S(2)}) collective-permute-start(bf16[224,1024]{1,0:T(8,128)(2,1)S(1)} %add_convert_fusion.3), channel_id=1, source_target_pairs={{0,8},{24,9},{1,16},{25,17},{2,10},{26,11},{3,18},{27,19},{4,12},{... | collective-permute-start | bytes 1376264 | tf_op jit(solution)/shard_map/ppermute | solution.py:248
  60.6 0.0 collective-permute-done.17.refs_2_
  60.6 0.1 collective-permute-start.19
  60.7 4.8 %collective-permute-done.18.refs_4_ = bf16[288,1024]{1,0:T(8,128)(2,1)S(1)} collective-permute-done((bf16[288,1024]{1,0:T(8,128)(2,1)S(1)}, bf16[288,1024]{1,0:T(8,128)(2,1)S(1)}, u32[]{:S(2)}, u32[]{:S(2)}) %collective-permute-start.18) | collective-permute-done | bytes 589856 | tf_op jit(solution)/shard_map/ppermute | solution.py:248
  65.5 0.0 collective-permute-start.21
  65.5 4.2 %shard_map.66 = (bf16[256,1024]{1,0:T(8,128)(2,1)S(1)}, bf16[256,1024]{1,0:T(8,128)(2,1)S(1)}) custom-call(bf16[512,1024]{1,0:T(8,128)(2,1)S(1)} %bitcast.29, bf16[288,1024]{1,0:T(8,128)(2,1)S(1)} %get-tuple-element.32.refs_1_, bf16[224,1024]{1,0:T(8,128)(2,1)S(1)} %get-tuple-element.33.refs_2_, bf16[288,1024]{1,0:T(8,128)(2,1)S(1)} %get-tuple-element.58.refs_3_, ...), custom_call_target="tpu_custom_call" | custom-call | flops 2684354560 | bytes 5242880 | tf_op jit(solution)/shard_map/pallas_call | solution.py:148
  69.7 1.0 collective-permute-done.13.refs_3_
  70.7 0.0 collective-permute-start.20
  70.7 2.2 %collective-permute-done.14.refs_5_ = bf16[224,1024]{1,0:T(8,128)(2,1)S(1)} collective-permute-done((bf16[224,1024]{1,0:T(8,128)(2,1)S(1)}, bf16[224,1024]{1,0:T(8,128)(2,1)S(1)}, u32[]{:S(2)}, u32[]{:S(2)}) %collective-permute-start.14) | collective-permute-done | bytes 458784 | tf_op jit(solution)/shard_map/ppermute | solution.py:248
  72.9 0.0 collective-permute-start.22
  72.9 4.3 %collective-permute-start.16 = (bf16[256,1024]{1,0:T(8,128)(2,1)S(1)}, bf16[256,1024]{1,0:T(8,128)(2,1)S(1)}, u32[]{:S(2)}, u32[]{:S(2)}) collective-permute-start(bf16[256,1024]{1,0:T(8,128)(2,1)S(1)} %get-tuple-element.49), channel_id=1, source_target_pairs={{16,8},{8,9},{17,16},{9,17},{18,10},{10,11},{19,18},{11,19},{20,12... | collective-permute-start | bytes 1572872 | tf_op jit(solution)/shard_map/ppermute | solution.py:265
  77.2 0.0 collective-permute-done.19.refs_6_
  77.2 1.3 %collective-permute-start.15 = (bf16[256,1024]{1,0:T(8,128)(2,1)S(1)}, bf16[256,1024]{1,0:T(8,128)(2,1)S(1)}, u32[]{:S(2)}, u32[]{:S(2)}) collective-permute-start(bf16[256,1024]{1,0:T(8,128)(2,1)S(1)} %get-tuple-element.49), channel_id=1, source_target_pairs={{0,8},{24,9},{1,16},{25,17},{2,10},{26,11},{3,18},{27,19},{4,12},{... | collective-permute-start | bytes 1572872 | tf_op jit(solution)/shard_map/ppermute | solution.py:265
  78.5 1.3 %collective-permute-start.24 = (bf16[256,1024]{1,0:T(8,128)(2,1)S(1)}, bf16[256,1024]{1,0:T(8,128)(2,1)S(1)}, u32[]{:S(2)}, u32[]{:S(2)}) collective-permute-start(bf16[256,1024]{1,0:T(8,128)(2,1)S(1)} %get-tuple-element.53), channel_id=1, source_target_pairs={{0,8},{24,9},{1,16},{25,17},{2,10},{26,11},{3,18},{27,19},{4,12},{... | collective-permute-start | bytes 1572872 | tf_op jit(solution)/shard_map/ppermute | solution.py:265
  79.8 2.1 %collective-permute-start.25 = (bf16[256,1024]{1,0:T(8,128)(2,1)S(1)}, bf16[256,1024]{1,0:T(8,128)(2,1)S(1)}, u32[]{:S(2)}, u32[]{:S(2)}) collective-permute-start(bf16[256,1024]{1,0:T(8,128)(2,1)S(1)} %get-tuple-element.53), channel_id=1, source_target_pairs={{16,8},{8,9},{17,16},{9,17},{18,10},{10,11},{19,18},{11,19},{20,12... | collective-permute-start | bytes 1572872 | tf_op jit(solution)/shard_map/ppermute | solution.py:265
  81.9 7.0 %shard_map.67 = (f32[256,1024]{1,0:T(8,128)S(1)}, f32[256,1024]{1,0:T(8,128)S(1)}) custom-call(s32[1,2]{1,0:T(1,128)S(1)} %bitcast.33, s32[1,2]{1,0:T(1,128)S(1)} %bitcast.34, bf16[288,1024]{1,0:T(8,128)(2,1)S(1)} %collective-permute-done.17.refs_2_, bf16[224,1024]{1,0:T(8,128)(2,1)S(1)} %collective-permute-done.13.refs_3_, ...), custom_call_target="tpu_custom_call" | custom-call | flops 5368709120 | bytes 6291472 | tf_op jit(solution)/shard_map/pallas_call | solution.py:148
  89.0 5.3 %collective-permute-done.15 = bf16[256,1024]{1,0:T(8,128)(2,1)S(1)} collective-permute-done((bf16[256,1024]{1,0:T(8,128)(2,1)S(1)}, bf16[256,1024]{1,0:T(8,128)(2,1)S(1)}, u32[]{:S(2)}, u32[]{:S(2)}) %collective-permute-start.15) | collective-permute-done | bytes 524320 | tf_op jit(solution)/shard_map/ppermute | solution.py:265
  94.3 0.2 add_convert_fusion.2
  94.5 1.8 %collective-permute-start.23 = (bf16[256,1024]{1,0:T(8,128)(2,1)S(1)}, bf16[256,1024]{1,0:T(8,128)(2,1)S(1)}, u32[]{:S(2)}, u32[]{:S(2)}) collective-permute-start(bf16[256,1024]{1,0:T(8,128)(2,1)S(1)} %add_convert_fusion.2), channel_id=1, source_target_pairs={{8,0},{9,24},{16,1},{17,25},{10,2},{11,26},{18,3},{19,27},{12,4},{... | collective-permute-start | bytes 1572872 | tf_op jit(solution)/shard_map/ppermute | solution.py:278
  96.3 7.5 %collective-permute-done.24 = bf16[256,1024]{1,0:T(8,128)(2,1)S(1)} collective-permute-done((bf16[256,1024]{1,0:T(8,128)(2,1)S(1)}, bf16[256,1024]{1,0:T(8,128)(2,1)S(1)}, u32[]{:S(2)}, u32[]{:S(2)}) %collective-permute-start.24) | collective-permute-done | bytes 524320 | tf_op jit(solution)/shard_map/ppermute | solution.py:265
  103.8 0.3 add_convert_fusion.1
  104.0 1.7 %collective-permute-start.26 = (bf16[256,1024]{1,0:T(8,128)(2,1)S(1)}, bf16[256,1024]{1,0:T(8,128)(2,1)S(1)}, u32[]{:S(2)}, u32[]{:S(2)}) collective-permute-start(bf16[256,1024]{1,0:T(8,128)(2,1)S(1)} %add_convert_fusion.1), channel_id=1, source_target_pairs={{8,0},{9,24},{16,1},{17,25},{10,2},{11,26},{18,3},{19,27},{12,4},{... | collective-permute-start | bytes 1572872 | tf_op jit(solution)/shard_map/ppermute | solution.py:278
  105.8 1.9 %collective-permute-start.27 = (bf16[256,1024]{1,0:T(8,128)(2,1)S(1)}, bf16[256,1024]{1,0:T(8,128)(2,1)S(1)}, u32[]{:S(2)}, u32[]{:S(2)}) collective-permute-start(bf16[256,1024]{1,0:T(8,128)(2,1)S(1)} %add_convert_fusion.2), channel_id=1, source_target_pairs={{8,16},{9,8},{16,17},{17,9},{10,18},{11,10},{18,19},{19,11},{12,20... | collective-permute-start | bytes 1572872 | tf_op jit(solution)/shard_map/ppermute | solution.py:278
  107.7 2.5 %collective-permute-start.28 = (bf16[256,1024]{1,0:T(8,128)(2,1)S(1)}, bf16[256,1024]{1,0:T(8,128)(2,1)S(1)}, u32[]{:S(2)}, u32[]{:S(2)}) collective-permute-start(bf16[256,1024]{1,0:T(8,128)(2,1)S(1)} %add_convert_fusion.1), channel_id=1, source_target_pairs={{8,16},{9,8},{16,17},{17,9},{10,18},{11,10},{18,19},{19,11},{12,20... | collective-permute-start | bytes 1572872 | tf_op jit(solution)/shard_map/ppermute | solution.py:278
  110.2 4.4 %collective-permute-done.26.refs_1_ = bf16[256,1024]{1,0:T(8,128)(2,1)S(1)} collective-permute-done((bf16[256,1024]{1,0:T(8,128)(2,1)S(1)}, bf16[256,1024]{1,0:T(8,128)(2,1)S(1)}, u32[]{:S(2)}, u32[]{:S(2)}) %collective-permute-start.26) | collective-permute-done | bytes 524320 | tf_op jit(solution)/shard_map/ppermute | solution.py:278
  114.7 3.7 %collective-permute-done.27.refs_2_ = bf16[256,1024]{1,0:T(8,128)(2,1)S(1)} collective-permute-done((bf16[256,1024]{1,0:T(8,128)(2,1)S(1)}, bf16[256,1024]{1,0:T(8,128)(2,1)S(1)}, u32[]{:S(2)}, u32[]{:S(2)}) %collective-permute-start.27) | collective-permute-done | bytes 524320 | tf_op jit(solution)/shard_map/ppermute | solution.py:278
  118.4 5.6 %collective-permute-done.28.refs_3_ = bf16[256,1024]{1,0:T(8,128)(2,1)S(1)} collective-permute-done((bf16[256,1024]{1,0:T(8,128)(2,1)S(1)}, bf16[256,1024]{1,0:T(8,128)(2,1)S(1)}, u32[]{:S(2)}, u32[]{:S(2)}) %collective-permute-start.28) | collective-permute-done | bytes 524320 | tf_op jit(solution)/shard_map/ppermute | solution.py:278
  124.0 1.0 shard_map.68
  (17 shorter events, 0.1 us)
Async XLA Ops:
  0.0 3.2 %copy-start.3 = (s32[1,2]{1,0:T(1,128)S(1)}, s32[1,2]{1,0:T(1,128)}, u32[]{:S(2)}) copy-start(s32[1,2]{1,0:T(1,128)} %param.11) | copy-start | bytes 28
  0.7 12.1 %copy-start = (bf16[1,1,512,1024]{3,2,1,0:T(8,128)(2,1)S(1)}, bf16[1,1,512,1024]{3,2,1,0:T(8,128)(2,1)}, u32[]{:S(2)}) copy-start(bf16[1,1,512,1024]{3,2,1,0:T(8,128)(2,1)} %param.10) | copy-start | bytes 3145732
  0.7 12.1 %copy-start.1 = (bf16[2,1,1,256,512]{4,3,2,1,0:T(8,128)(2,1)S(1)}, bf16[2,1,1,256,512]{4,3,2,1,0:T(8,128)(2,1)}, u32[]{:S(2)}) copy-start(bf16[2,1,1,256,512]{4,3,2,1,0:T(8,128)(2,1)} %param.8) | copy-start | bytes 1572868
  1.9 7.9 %collective-permute-start.1 = (bf16[144,1024]{1,0:T(8,128)(2,1)S(1)}, bf16[144,1024]{1,0:T(8,128)(2,1)S(1)}, u32[]{:S(2)}, u32[]{:S(2)}) collective-permute-start(bf16[144,1024]{1,0:T(8,128)(2,1)S(1)} %pad_maximum_fusion.refs_0_), channel_id=1, source_target_pairs={{0,2},{1,3},{2,0},{3,1},{4,6},{5,7},{6,4},{7,5},{8,10},{9,11},{10,... | collective-permute-start | bytes 884744 | tf_op jit(solution)/shard_map/ppermute | solution.py:205
  3.2 4.8 %collective-permute-start.2 = (s32[2]{0:T(128)S(1)}, s32[2]{0:T(128)S(1)}, u32[]{:S(2)}, u32[]{:S(2)}) collective-permute-start(s32[2]{0:T(128)S(1)} %bitcast.35), channel_id=1, source_target_pairs={{0,4},{4,0},{8,12},{12,8},{16,20},{20,16},{24,28},{28,24},{1,5},{5... | collective-permute-start | bytes 32 | tf_op jit(solution)/shard_map/ppermute | solution.py:192
  3.5 5.9 %collective-permute-start.3 = (s32[2]{0:T(128)S(1)}, s32[2]{0:T(128)S(1)}, u32[]{:S(2)}, u32[]{:S(2)}) collective-permute-start(s32[2]{0:T(128)S(1)} %bitcast.36), channel_id=1, source_target_pairs={{0,8},{24,9},{1,16},{25,17},{2,10},{26,11},{3,18},{27,19},{4,12},{... | collective-permute-start | bytes 32 | tf_op jit(solution)/shard_map/ppermute | solution.py:194
  4.8 4.6 %collective-permute-start.4 = (s32[2]{0:T(128)S(1)}, s32[2]{0:T(128)S(1)}, u32[]{:S(2)}, u32[]{:S(2)}) collective-permute-start(s32[2]{0:T(128)S(1)} %bitcast.37), channel_id=1, source_target_pairs={{16,8},{8,9},{17,16},{9,17},{18,10},{10,11},{19,18},{11,19},{20,12... | collective-permute-start | bytes 32 | tf_op jit(solution)/shard_map/ppermute | solution.py:195
  8.0 4.8 %collective-permute-start = (bf16[144,1024]{1,0:T(8,128)(2,1)S(1)}, bf16[144,1024]{1,0:T(8,128)(2,1)S(1)}, u32[]{:S(2)}, u32[]{:S(2)}) collective-permute-start(bf16[144,1024]{1,0:T(8,128)(2,1)S(1)} %pad_maximum_fusion.refs_0_), channel_id=1, source_target_pairs={{0,1},{1,0},{2,3},{3,2},{4,5},{5,4},{6,7},{7,6},{8,9},{9,8},{10,11... | collective-permute-start | bytes 884744 | tf_op jit(solution)/shard_map/ppermute | solution.py:205
  9.9 2.9 %collective-permute-start.5 = (bf16[144,1024]{1,0:T(8,128)(2,1)S(1)}, bf16[144,1024]{1,0:T(8,128)(2,1)S(1)}, u32[]{:S(2)}, u32[]{:S(2)}) collective-permute-start(bf16[144,1024]{1,0:T(8,128)(2,1)S(1)} %collective-permute-done.1.refs_2_), channel_id=1, source_target_pairs={{0,1},{1,0},{2,3},{3,2},{4,5},{5,4},{6,7},{7,6},{8,9},{9,8},{10,11... | collective-permute-start | bytes 884744 | tf_op jit(solution)/shard_map/ppermute | solution.py:205
  11.5 8.7 %collective-permute-start.9 = (bf16[144,1024]{1,0:T(8,128)(2,1)S(1)}, bf16[144,1024]{1,0:T(8,128)(2,1)S(1)}, u32[]{:S(2)}, u32[]{:S(2)}) collective-permute-start(bf16[144,1024]{1,0:T(8,128)(2,1)S(1)} %pad_maximum_fusion.1.refs_0_), channel_id=1, source_target_pairs={{0,2},{1,3},{2,0},{3,1},{4,6},{5,7},{6,4},{7,5},{8,10},{9,11},{10,... | collective-permute-start | bytes 884744 | tf_op jit(solution)/shard_map/ppermute | solution.py:205
  14.5 27.3 %collective-permute-start.7 = (bf16[288,1024]{1,0:T(8,128)(2,1)S(1)}, bf16[288,1024]{1,0:T(8,128)(2,1)S(1)}, u32[]{:S(2)}, u32[]{:S(2)}) collective-permute-start(bf16[288,1024]{1,0:T(8,128)(2,1)S(1)} %get-tuple-element.34), channel_id=1, source_target_pairs={{28,0},{0,4},{4,8},{8,12},{12,16},{16,20},{20,24},{24,28},{29,1},{... | collective-permute-start | bytes 1769480 | tf_op jit(solution)/shard_map/ppermute | solution.py:293
  15.8 26.0 %collective-permute-start.6 = (bf16[288,1024]{1,0:T(8,128)(2,1)S(1)}, bf16[288,1024]{1,0:T(8,128)(2,1)S(1)}, u32[]{:S(2)}, u32[]{:S(2)}) collective-permute-start(bf16[288,1024]{1,0:T(8,128)(2,1)S(1)} %get-tuple-element.34), channel_id=1, source_target_pairs={{4,0},{8,4},{12,8},{16,12},{20,16},{24,20},{28,24},{0,28},{5,1},{9... | collective-permute-start | bytes 1769480 | tf_op jit(solution)/shard_map/ppermute | solution.py:293
  16.0 23.8 %collective-permute-start.11 = (bf16[224,1024]{1,0:T(8,128)(2,1)S(1)}, bf16[224,1024]{1,0:T(8,128)(2,1)S(1)}, u32[]{:S(2)}, u32[]{:S(2)}) collective-permute-start(bf16[224,1024]{1,0:T(8,128)(2,1)S(1)} %get-tuple-element.40), channel_id=1, source_target_pairs={{0,24},{4,12},{8,0},{12,20},{16,8},{20,28},{24,16},{28,4},{1,25},{... | collective-permute-start | bytes 1376264 | tf_op jit(solution)/shard_map/ppermute | solution.py:225
  17.3 3.7 %collective-permute-start.8 = (bf16[144,1024]{1,0:T(8,128)(2,1)S(1)}, bf16[144,1024]{1,0:T(8,128)(2,1)S(1)}, u32[]{:S(2)}, u32[]{:S(2)}) collective-permute-start(bf16[144,1024]{1,0:T(8,128)(2,1)S(1)} %pad_maximum_fusion.1.refs_0_), channel_id=1, source_target_pairs={{0,1},{1,0},{2,3},{3,2},{4,5},{5,4},{6,7},{7,6},{8,9},{9,8},{10,11... | collective-permute-start | bytes 884744 | tf_op jit(solution)/shard_map/ppermute | solution.py:205
  20.2 2.0 %collective-permute-start.10 = (bf16[144,1024]{1,0:T(8,128)(2,1)S(1)}, bf16[144,1024]{1,0:T(8,128)(2,1)S(1)}, u32[]{:S(2)}, u32[]{:S(2)}) collective-permute-start(bf16[144,1024]{1,0:T(8,128)(2,1)S(1)} %collective-permute-done.9.refs_2_), channel_id=1, source_target_pairs={{0,1},{1,0},{2,3},{3,2},{4,5},{5,4},{6,7},{7,6},{8,9},{9,8},{10,11... | collective-permute-start | bytes 884744 | tf_op jit(solution)/shard_map/ppermute | solution.py:205
  42.5 11.1 %collective-permute-start.12 = (bf16[224,1024]{1,0:T(8,128)(2,1)S(1)}, bf16[224,1024]{1,0:T(8,128)(2,1)S(1)}, u32[]{:S(2)}, u32[]{:S(2)}) collective-permute-start(bf16[224,1024]{1,0:T(8,128)(2,1)S(1)} %broadcast_select_fusion.1), channel_id=1, source_target_pairs={{0,4},{4,0},{8,12},{12,8},{16,20},{20,16},{24,28},{28,24},{1,5},{5... | collective-permute-start | bytes 1376264 | tf_op jit(solution)/shard_map/ppermute | solution.py:241
  44.1 16.4 %collective-permute-start.17 = (bf16[288,1024]{1,0:T(8,128)(2,1)S(1)}, bf16[288,1024]{1,0:T(8,128)(2,1)S(1)}, u32[]{:S(2)}, u32[]{:S(2)}) collective-permute-start(bf16[288,1024]{1,0:T(8,128)(2,1)S(1)} %get-tuple-element.57), channel_id=1, source_target_pairs={{8,8},{16,9},{9,16},{17,17},{10,10},{18,11},{11,18},{19,19},{12,12... | collective-permute-start | bytes 1769480 | tf_op jit(solution)/shard_map/ppermute | solution.py:247
  48.2 17.3 %collective-permute-start.18 = (bf16[288,1024]{1,0:T(8,128)(2,1)S(1)}, bf16[288,1024]{1,0:T(8,128)(2,1)S(1)}, u32[]{:S(2)}, u32[]{:S(2)}) collective-permute-start(bf16[288,1024]{1,0:T(8,128)(2,1)S(1)} %get-tuple-element.57), channel_id=1, source_target_pairs={{0,8},{24,9},{1,16},{25,17},{2,10},{26,11},{3,18},{27,19},{4,12},{... | collective-permute-start | bytes 1769480 | tf_op jit(solution)/shard_map/ppermute | solution.py:248
  53.6 11.9 %copy-start.2 = (bf16[1,1,512,1024]{3,2,1,0:T(8,128)(2,1)S(1)}, bf16[1,1,512,1024]{3,2,1,0:T(8,128)(2,1)}, u32[]{:S(2)}) copy-start(bf16[1,1,512,1024]{3,2,1,0:T(8,128)(2,1)} %param.9) | copy-start | bytes 3145732
  54.0 16.7 %collective-permute-start.13 = (bf16[224,1024]{1,0:T(8,128)(2,1)S(1)}, bf16[224,1024]{1,0:T(8,128)(2,1)S(1)}, u32[]{:S(2)}, u32[]{:S(2)}) collective-permute-start(bf16[224,1024]{1,0:T(8,128)(2,1)S(1)} %add_convert_fusion.3), channel_id=1, source_target_pairs={{8,8},{16,9},{9,16},{17,17},{10,10},{18,11},{11,18},{19,19},{12,12... | collective-permute-start | bytes 1376264 | tf_op jit(solution)/shard_map/ppermute | solution.py:247
  59.3 13.6 %collective-permute-start.14 = (bf16[224,1024]{1,0:T(8,128)(2,1)S(1)}, bf16[224,1024]{1,0:T(8,128)(2,1)S(1)}, u32[]{:S(2)}, u32[]{:S(2)}) collective-permute-start(bf16[224,1024]{1,0:T(8,128)(2,1)S(1)} %add_convert_fusion.3), channel_id=1, source_target_pairs={{0,8},{24,9},{1,16},{25,17},{2,10},{26,11},{3,18},{27,19},{4,12},{... | collective-permute-start | bytes 1376264 | tf_op jit(solution)/shard_map/ppermute | solution.py:248
  60.6 16.6 %collective-permute-start.19 = (bf16[288,1024]{1,0:T(8,128)(2,1)S(1)}, bf16[288,1024]{1,0:T(8,128)(2,1)S(1)}, u32[]{:S(2)}, u32[]{:S(2)}) collective-permute-start(bf16[288,1024]{1,0:T(8,128)(2,1)S(1)} %collective-permute-done.17.refs_2_), channel_id=1, source_target_pairs={{0,1},{1,0},{2,3},{3,2},{4,5},{5,4},{6,7},{7,6},{8,9},{9,8},{10,11... | collective-permute-start | bytes 1769480 | tf_op jit(solution)/shard_map/ppermute | solution.py:251
  65.5 13.0 %collective-permute-start.21 = (bf16[288,1024]{1,0:T(8,128)(2,1)S(1)}, bf16[288,1024]{1,0:T(8,128)(2,1)S(1)}, u32[]{:S(2)}, u32[]{:S(2)}) collective-permute-start(bf16[288,1024]{1,0:T(8,128)(2,1)S(1)} %collective-permute-done.18.refs_4_), channel_id=1, source_target_pairs={{0,1},{1,0},{2,3},{3,2},{4,5},{5,4},{6,7},{7,6},{8,9},{9,8},{10,11... | collective-permute-start | bytes 1769480 | tf_op jit(solution)/shard_map/ppermute | solution.py:252
  70.7 9.1 %collective-permute-start.20 = (bf16[224,1024]{1,0:T(8,128)(2,1)S(1)}, bf16[224,1024]{1,0:T(8,128)(2,1)S(1)}, u32[]{:S(2)}, u32[]{:S(2)}) collective-permute-start(bf16[224,1024]{1,0:T(8,128)(2,1)S(1)} %collective-permute-done.13.refs_3_), channel_id=1, source_target_pairs={{0,1},{1,0},{2,3},{3,2},{4,5},{5,4},{6,7},{7,6},{8,9},{9,8},{10,11... | collective-permute-start | bytes 1376264 | tf_op jit(solution)/shard_map/ppermute | solution.py:262
  72.9 9.1 %collective-permute-start.22 = (bf16[224,1024]{1,0:T(8,128)(2,1)S(1)}, bf16[224,1024]{1,0:T(8,128)(2,1)S(1)}, u32[]{:S(2)}, u32[]{:S(2)}) collective-permute-start(bf16[224,1024]{1,0:T(8,128)(2,1)S(1)} %collective-permute-done.14.refs_5_), channel_id=1, source_target_pairs={{0,1},{1,0},{2,3},{3,2},{4,5},{5,4},{6,7},{7,6},{8,9},{9,8},{10,11... | collective-permute-start | bytes 1376264 | tf_op jit(solution)/shard_map/ppermute | solution.py:263
  72.9 16.1 %collective-permute-start.16 = (bf16[256,1024]{1,0:T(8,128)(2,1)S(1)}, bf16[256,1024]{1,0:T(8,128)(2,1)S(1)}, u32[]{:S(2)}, u32[]{:S(2)}) collective-permute-start(bf16[256,1024]{1,0:T(8,128)(2,1)S(1)} %get-tuple-element.49), channel_id=1, source_target_pairs={{16,8},{8,9},{17,16},{9,17},{18,10},{10,11},{19,18},{11,19},{20,12... | collective-permute-start | bytes 1572872 | tf_op jit(solution)/shard_map/ppermute | solution.py:265
  77.2 17.1 %collective-permute-start.15 = (bf16[256,1024]{1,0:T(8,128)(2,1)S(1)}, bf16[256,1024]{1,0:T(8,128)(2,1)S(1)}, u32[]{:S(2)}, u32[]{:S(2)}) collective-permute-start(bf16[256,1024]{1,0:T(8,128)(2,1)S(1)} %get-tuple-element.49), channel_id=1, source_target_pairs={{0,8},{24,9},{1,16},{25,17},{2,10},{26,11},{3,18},{27,19},{4,12},{... | collective-permute-start | bytes 1572872 | tf_op jit(solution)/shard_map/ppermute | solution.py:265
  78.5 25.3 %collective-permute-start.24 = (bf16[256,1024]{1,0:T(8,128)(2,1)S(1)}, bf16[256,1024]{1,0:T(8,128)(2,1)S(1)}, u32[]{:S(2)}, u32[]{:S(2)}) collective-permute-start(bf16[256,1024]{1,0:T(8,128)(2,1)S(1)} %get-tuple-element.53), channel_id=1, source_target_pairs={{0,8},{24,9},{1,16},{25,17},{2,10},{26,11},{3,18},{27,19},{4,12},{... | collective-permute-start | bytes 1572872 | tf_op jit(solution)/shard_map/ppermute | solution.py:265
  79.8 24.0 %collective-permute-start.25 = (bf16[256,1024]{1,0:T(8,128)(2,1)S(1)}, bf16[256,1024]{1,0:T(8,128)(2,1)S(1)}, u32[]{:S(2)}, u32[]{:S(2)}) collective-permute-start(bf16[256,1024]{1,0:T(8,128)(2,1)S(1)} %get-tuple-element.53), channel_id=1, source_target_pairs={{16,8},{8,9},{17,16},{9,17},{18,10},{10,11},{19,18},{11,19},{20,12... | collective-permute-start | bytes 1572872 | tf_op jit(solution)/shard_map/ppermute | solution.py:265
  94.5 15.7 %collective-permute-start.23 = (bf16[256,1024]{1,0:T(8,128)(2,1)S(1)}, bf16[256,1024]{1,0:T(8,128)(2,1)S(1)}, u32[]{:S(2)}, u32[]{:S(2)}) collective-permute-start(bf16[256,1024]{1,0:T(8,128)(2,1)S(1)} %add_convert_fusion.2), channel_id=1, source_target_pairs={{8,0},{9,24},{16,1},{17,25},{10,2},{11,26},{18,3},{19,27},{12,4},{... | collective-permute-start | bytes 1572872 | tf_op jit(solution)/shard_map/ppermute | solution.py:278
  104.0 10.6 %collective-permute-start.26 = (bf16[256,1024]{1,0:T(8,128)(2,1)S(1)}, bf16[256,1024]{1,0:T(8,128)(2,1)S(1)}, u32[]{:S(2)}, u32[]{:S(2)}) collective-permute-start(bf16[256,1024]{1,0:T(8,128)(2,1)S(1)} %add_convert_fusion.1), channel_id=1, source_target_pairs={{8,0},{9,24},{16,1},{17,25},{10,2},{11,26},{18,3},{19,27},{12,4},{... | collective-permute-start | bytes 1572872 | tf_op jit(solution)/shard_map/ppermute | solution.py:278
  105.8 12.6 %collective-permute-start.27 = (bf16[256,1024]{1,0:T(8,128)(2,1)S(1)}, bf16[256,1024]{1,0:T(8,128)(2,1)S(1)}, u32[]{:S(2)}, u32[]{:S(2)}) collective-permute-start(bf16[256,1024]{1,0:T(8,128)(2,1)S(1)} %add_convert_fusion.2), channel_id=1, source_target_pairs={{8,16},{9,8},{16,17},{17,9},{10,18},{11,10},{18,19},{19,11},{12,20... | collective-permute-start | bytes 1572872 | tf_op jit(solution)/shard_map/ppermute | solution.py:278
  107.7 16.3 %collective-permute-start.28 = (bf16[256,1024]{1,0:T(8,128)(2,1)S(1)}, bf16[256,1024]{1,0:T(8,128)(2,1)S(1)}, u32[]{:S(2)}, u32[]{:S(2)}) collective-permute-start(bf16[256,1024]{1,0:T(8,128)(2,1)S(1)} %add_convert_fusion.1), channel_id=1, source_target_pairs={{8,16},{9,8},{16,17},{17,9},{10,18},{11,10},{18,19},{19,11},{12,20... | collective-permute-start | bytes 1572872 | tf_op jit(solution)/shard_map/ppermute | solution.py:278
